TPU v7x, 128 devices: a whole 4x4x4 slice. The times are simulated.
128 devices in a mesh: inst: 16 (over y_hi, x, core), tp: 8 (over y_lo, z).
Axes of the slice: x: 4, y: 4 (y_hi: 2, y_lo: 2; y = y_hi * 2 + y_lo), z: 4, core: 2. Of those that a mesh axis runs over, the one named last changes fastest.
Arguments:
- hidden: bfloat16 [4, 512, 8192], P(None, 'inst'), may hold values from -6 to 6
- query_weight: bfloat16 [8192, 4096], P(None, 'tp'), may hold values from -0.0625 to 0.0625
- output_weight: bfloat16 [4096, 8192], P('tp'), may hold values from -0.09375 to 0.09375
- kv_pool: bfloat16 [1536, 2, 64, 1024], P('inst', None, None, 'tp'), may hold values from -620 to 620
- new_kv: bfloat16 [4, 512, 2, 1024], P(None, 'inst', None, 'tp'), may hold values from -6 to 6
- lengths: int32 [512], P('inst'), may hold values from 1 to 192, as said below
- page_table: int32 [512, 3], P('inst'), may hold values from 0 to 95, as said below
- mig_req: int32 [256], P('inst'), may hold values from 0 to 31, as said below
- mig_dest: int32 [256, 1], P('inst'), may hold values from 0 to 15; in each aligned block of 16 rows (0 to 15, 16 to 31, ...) at most 2 rows name the same one
- resume: int32 [256], P('inst'), may hold values from 0 to 3
Outputs:
- home_out: bfloat16 [4, 512, 8192], P(None, 'inst', 'tp')
- arrival_out: bfloat16 [4, 512, 8192], P(None, 'inst', 'tp')
- arrival_cache: bfloat16 [512, 3, 2, 64, 1024], P('inst', None, None, None, 'tp')
Inputs may be any that keep to these rules, and one draw needn't show every extreme that they name: Every draw has a request with exactly 192 cached tokens; typical lengths differ between instances by up to a factor of four. `page_table`: each instance's rows together name every page number of its pool exactly once. `mig_req`: the leaving requests of one instance are distinct. `mig_dest`: among the rows of one instance, no instance is named more than 2 times.
All inputs are finite; a program needn't handle non-finite values.
Results may differ from a plain program's by a relative error of at most 0.012.
Values may be sent and summed in bfloat16 or wider, within the bound.
No kernel may reach another device: no remote copies, remote signals or barrier semaphores. Data moves between devices by JAX's collectives and lax.ppermute only.
A program may use at most 128 MiB of HBM per device.

v0:
```python
import jax
import jax.numpy as jnp
from jax import lax
from jax.sharding import PartitionSpec as P

HD = 128
GROUP = 4
CAP = 2


ROPE_BASE = 500000.0


def rotate(query, position):
    half = query.shape[-1] // 2
    inverse = ROPE_BASE ** (-jnp.arange(half, dtype=jnp.float32) * 2.0 / query.shape[-1])
    angles = position.astype(jnp.float32)[..., None] * inverse
    angles = jnp.concatenate([angles, angles], axis=-1)
    turned = jnp.concatenate([-query[..., half:], query[..., :half]], axis=-1)
    return query * jnp.cos(angles) + turned * jnp.sin(angles)


def attend(query, pages, length, fresh):
    count = pages.shape[0]
    depth = query.shape[-1]
    steps_n = query.shape[0]
    keys = pages[:, :, 0].reshape(count, -1, depth)
    values = pages[:, :, 1].reshape(count, -1, depth)
    scale = depth ** (-0.5)
    older = jnp.einsum("sbgd,bld->bsgl", query, keys, preferred_element_type=jnp.float32) * scale
    newer = (
        jnp.einsum("sbgd,ubd->bsgu", query, fresh[:, :, 0], preferred_element_type=jnp.float32)
        * scale
    )
    live = jnp.arange(keys.shape[1], dtype=jnp.int32)[None, :] < length[:, None]
    older = jnp.where(live[:, None, None, :], older, -1e30)
    step_ids = jnp.arange(steps_n, dtype=jnp.int32)
    causal = step_ids[None, :] <= step_ids[:, None]
    newer = jnp.where(causal[None, :, None, :], newer, -1e30)
    top = jnp.maximum(jnp.max(older, axis=-1), jnp.max(newer, axis=-1))[..., None]
    older_w = jnp.exp(older - top)
    newer_w = jnp.exp(newer - top)
    total = (jnp.sum(older_w, axis=-1) + jnp.sum(newer_w, axis=-1))[..., None]
    older_p = (older_w / total).astype(jnp.bfloat16)
    newer_p = (newer_w / total).astype(jnp.bfloat16)
    result = jnp.einsum("bsgl,bld->sbgd", older_p, values, preferred_element_type=jnp.float32)
    result = result + jnp.einsum(
        "bsgu,ubd->sbgd", newer_p, fresh[:, :, 1], preferred_element_type=jnp.float32
    )
    return result.astype(jnp.bfloat16).reshape(steps_n, count, -1)


def local(
    hidden,
    query_weight,
    output_weight,
    kv_pool,
    new_kv,
    lengths,
    page_table,
    mig_req,
    mig_dest,
    resume,
):
    steps_n, local_rows, width = hidden.shape
    instances = lax.axis_size("inst")
    query = jnp.dot(hidden.reshape(-1, width), query_weight, preferred_element_type=jnp.float32)
    query = query.reshape(steps_n, local_rows, GROUP, HD)
    position = lengths[None, :] + jnp.arange(steps_n, dtype=jnp.int32)[:, None]
    rotated = rotate(query, position[:, :, None]).astype(jnp.bfloat16)
    pages = kv_pool[page_table]
    attended = attend(rotated, pages, lengths, new_kv)
    leaving = mig_req.shape[0]
    order = jnp.arange(leaving, dtype=jnp.int32)
    hit = mig_req[:, None] == jnp.arange(local_rows, dtype=jnp.int32)[None, :]
    moved = jnp.min(jnp.where(hit, resume[:, None], steps_n), axis=0)
    step_ids = jnp.arange(steps_n, dtype=jnp.int32)[:, None]
    home_rows = jnp.where(
        (step_ids < moved[None, :])[:, :, None], attended, jnp.zeros_like(attended)
    )
    dest = mig_dest[:, 0]
    same = dest[None, :] == dest[:, None]
    earlier = order[None, :] < order[:, None]
    rank = jnp.sum((same & earlier).astype(jnp.int32), axis=1)
    slot = dest * CAP + rank
    slot_ids = jnp.arange(instances * CAP, dtype=jnp.int32)
    chosen = (slot_ids[:, None] == slot[None, :]).astype(jnp.int32)
    slot_request = jnp.sum(chosen * mig_req[None, :], axis=1)
    filled = jnp.sum(chosen, axis=1)
    slot_resume = jnp.where(filled > 0, jnp.sum(chosen * resume[None, :], axis=1), steps_n)
    slot_pages = jnp.where(
        (filled > 0)[:, None, None, None, None], pages[slot_request], jnp.zeros_like(pages[:1])
    )
    slot_query = jnp.transpose(rotated[:, slot_request], (1, 0, 2, 3)).reshape(
        instances * CAP, steps_n, GROUP * HD
    )
    slot_fresh = jnp.transpose(new_kv[:, slot_request], (1, 0, 2, 3))
    got_pages, got_query, got_fresh = (
        lax.all_to_all(slot_pages, "inst", split_axis=0, concat_axis=0, tiled=True),
        lax.all_to_all(slot_query, "inst", split_axis=0, concat_axis=0, tiled=True),
        lax.all_to_all(slot_fresh, "inst", split_axis=0, concat_axis=0, tiled=True),
    )
    slot_meta = jnp.stack([lengths[slot_request], slot_resume], axis=1)
    got_meta = lax.all_to_all(slot_meta, "inst", split_axis=0, concat_axis=0, tiled=True)
    arrive_query = jnp.transpose(
        got_query.reshape(instances * CAP, steps_n, GROUP, HD), (1, 0, 2, 3)
    )
    arrive_fresh = jnp.transpose(got_fresh, (1, 0, 2, 3))
    arrived = attend(arrive_query, got_pages, got_meta[:, 0], arrive_fresh)
    arrival_rows = jnp.where(
        (step_ids >= got_meta[None, :, 1])[:, :, None], arrived, jnp.zeros_like(arrived)
    )
    combined = jnp.concatenate([home_rows, arrival_rows], axis=1)
    partial_sum = jnp.dot(
        combined.reshape(-1, combined.shape[-1]), output_weight, preferred_element_type=jnp.float32
    )
    partial_sum = partial_sum.reshape(steps_n, -1, width)
    summed = lax.psum(partial_sum, "tp")
    share = width // lax.axis_size("tp")
    mine = lax.dynamic_slice_in_dim(summed, lax.axis_index("tp") * share, share, 2)
    mine = mine.astype(jnp.bfloat16)
    return (mine[:, :local_rows], mine[:, local_rows:], got_pages)


def solution(mesh):
    in_specs = (
        P(None, "inst", None),
        P(None, "tp"),
        P("tp", None),
        P("inst", None, None, "tp"),
        P(None, "inst", None, "tp"),
        P("inst"),
        P("inst", None),
        P("inst"),
        P("inst", None),
        P("inst"),
    )
    out_specs = (P(None, "inst", "tp"), P(None, "inst", "tp"), P("inst", None, None, None, "tp"))
    return jax.shard_map(local, mesh=mesh, in_specs=in_specs, out_specs=out_specs, check_vma=False)
```

profile of v0, /device:TPU:1, one launch (start us, length us, event | category | flops | bytes accessed | tf_op | source)
XLA Modules:
  0.0 314.2 jit_solution(14717688473950331987)
XLA Ops:
  0.6 1.0 convert_reduce_fusion.1
  3.7 1.4 gather_fusion.1
  5.9 8.4 %all-to-all-start = ((s32[16,2,2]{1,2,0:T(2,128)}), s32[16,2,2]{1,2,0:T(2,128)S(1)}, u32[]{:S(2)}, u32[]{:S(2)}) async-start(s32[16,2,2]{1,2,0:T(2,128)} %copy.134), calls=%async_computation | async-start | bytes 32768 | tf_op jit(solution)/shard_map/all_to_all | solution.py:104
  15.5 11.4 %copy.157 = bf16[512,8192]{1,0:T(8,128)(2,1)} copy(bf16[512,8192]{0,1:T(8,128)(2,1)} %bitcast.102) | data formatting | bytes 16777216 | tf_op jit(solution)/shard_map/dot_general | solution.py:67
  26.9 6.9 %fusion.2 = f32[4,32,4,128]{3,1,2,0:T(8,128)S(1)} fusion(bf16[4,128,8192,1]{2,1,0,3:T(8,128)(2,1)} %bitcast.103, bf16[4,32,8192]{2,1,0:T(8,128)(2,1)} %param.10), kind=kOutput, calls=%fused_computation.8 | convolution fusion | flops 1073741824 | bytes 10747904 | tf_op jit(solution)/shard_map/dot_general | solution.py:67
  33.9 0.9 slice_negate_fusion
  34.8 0.9 fusion.29
  36.0 2.7 gather_fusion
  38.7 3.2 %gather_fusion.2 = bf16[32,3,2,64,128]{4,3,2,1,0:T(8,128)(2,1)S(1)} fusion(bf16[32,3,2,64,128]{4,3,2,1,0:T(8,128)(2,1)} %bitcast.100, s32[1024]{0:T(1024)} %copy-done.7), kind=kCustom, calls=%fused_computation.2 | custom fusion | bytes 6291584 | tf_op jit(solution)/shard_map/gather | solution.py:92
  41.9 2.6 broadcast_select_fusion
  44.7 0.8 gather_fusion.4
  46.2 7.2 %all-to-all-start.3 = ((bf16[32,4,2,128]{3,1,2,0:T(4,128)(2,1)}), bf16[32,4,2,128]{3,1,2,0:T(4,128)(2,1)S(1)}, u32[]{:S(2)}, u32[]{:S(2)}) async-start(bf16[32,4,2,128]{3,1,2,0:T(4,128)(2,1)} %copy.139), calls=%async_computation.3 | async-start | bytes 131072 | tf_op jit(solution)/shard_map/all_to_all | solution.py:101
  53.6 0.8 gather_fusion.3
  55.2 5.6 %all-to-all-done.3 = bf16[32,4,2,128]{3,1,2,0:T(4,128)(2,1)S(1)} async-done(((bf16[32,4,2,128]{3,1,2,0:T(4,128)(2,1)}), bf16[32,4,2,128]{3,1,2,0:T(4,128)(2,1)S(1)}, u32[]{:S(2)}, u32[]{:S(2)}) %all-to-all-start.3) | async-done | bytes 65568 | tf_op jit(solution)/shard_map/all_to_all | solution.py:101
  60.8 3.7 %all-to-all-start.2 = ((bf16[32,4,512]{2,1,0:T(4,128)(2,1)}), bf16[32,4,512]{2,1,0:T(4,128)(2,1)S(1)}, u32[]{:S(2)}, u32[]{:S(2)}) async-start(bf16[32,4,512]{2,1,0:T(4,128)(2,1)} %reshape.312), calls=%async_computation.2 | async-start | bytes 262144 | tf_op jit(solution)/shard_map/all_to_all | solution.py:100
  64.5 1.3 fusion.25
  65.9 6.2 %all-to-all-done.2 = bf16[32,4,512]{2,1,0:T(4,128)(2,1)S(1)} async-done(((bf16[32,4,512]{2,1,0:T(4,128)(2,1)}), bf16[32,4,512]{2,1,0:T(4,128)(2,1)S(1)}, u32[]{:S(2)}, u32[]{:S(2)}) %all-to-all-start.2) | async-done | bytes 131104 | tf_op jit(solution)/shard_map/all_to_all | solution.py:100
  72.1 4.7 %all-to-all-start.1 = ((bf16[32,3,2,64,128]{4,3,2,1,0:T(8,128)(2,1)}), bf16[32,3,2,64,128]{4,3,2,1,0:T(8,128)(2,1)}, u32[]{:S(2)}, u32[]{:S(2)}) async-start(bf16[32,3,2,64,128]{4,3,2,1,0:T(8,128)(2,1)} %broadcast_select_fusion), calls=%async_computation.1 | async-start | bytes 6291456 | tf_op jit(solution)/shard_map/all_to_all | solution.py:99
  77.2 3.8 %fusion.37 = (bf16[32,3,1,64,128]{4,3,2,1,0:T(8,128)(2,1)}, bf16[32,3,1,64,128]{4,3,2,1,0:T(8,128)(2,1)S(1)}) fusion(bf16[32,3,2,64,128]{4,3,2,1,0:T(8,128)(2,1)} %bitcast.101), kind=kLoop, calls=%fused_computation.95 | loop fusion | bytes 6291456 | tf_op jit(solution)/shard_map/slice | solution.py:28
  80.9 1.0 fusion.42
  83.0 1.2 fusion.22
  84.9 2.7 convolution_bitcast_fusion.1
  87.6 30.7 %all-to-all-done.1 = bf16[32,3,2,64,128]{4,3,2,1,0:T(8,128)(2,1)} async-done(((bf16[32,3,2,64,128]{4,3,2,1,0:T(8,128)(2,1)}), bf16[32,3,2,64,128]{4,3,2,1,0:T(8,128)(2,1)}, u32[]{:S(2)}, u32[]{:S(2)}) %all-to-all-start.1) | async-done | bytes 3145760 | tf_op jit(solution)/shard_map/all_to_all | solution.py:99
  118.3 3.8 %fusion.38 = (bf16[32,3,1,64,128]{4,3,2,1,0:T(8,128)(2,1)S(1)}, bf16[32,3,1,64,128]{4,3,2,1,0:T(8,128)(2,1)}) fusion(bf16[32,3,2,64,128]{4,3,2,1,0:T(8,128)(2,1)} %all-to-all-done.1), kind=kLoop, calls=%fused_computation.96 | loop fusion | bytes 6291456 | tf_op jit(solution)/shard_map/slice | solution.py:27
  122.1 1.0 fusion.41
  123.6 1.1 fusion.7
  125.8 2.0 fusion.12
  128.2 9.0 %fusion = f32[4,64,8192]{2,1,0:T(8,128)} fusion(bf16[512,8192]{1,0:T(8,128)(2,1)} %param.12, bf16[4,32,512]{2,1,0:T(8,128)(2,1)S(1)} %get-tuple-element.28, bf16[4,32,512]{2,1,0:T(8,128)(2,1)S(1)} %get-tuple-element.29), kind=kOutput, calls=%fused_computation.5 | convolution fusion | flops 2148007936 | bytes 17039360 | tf_op jit(solution)/shard_map/dot_general | solution.py:114
  137.2 170.1 %all-reduce.1 = bf16[4,64,8192]{2,1,0:T(8,128)(2,1)} all-reduce(f32[4,64,8192]{2,1,0:T(8,128)} %fusion), channel_id=1, replica_groups=mesh['inst'=16,'tp'=8] {'tp'}, use_global_device_ids=true, to_apply=%region_13.14 | all-reduce | flops 2097152 | bytes 12582912 | tf_op jit(solution)/shard_map/psum | solution.py:118
  307.3 1.1 dynamic-slice_convert_fusion
  308.3 0.8 fusion.39
  309.2 5.0 %copy.178 = bf16[32,3,2,64,128]{4,3,2,1,0:T(8,128)(2,1)} copy(bf16[32,3,2,64,128]{4,3,2,1,0:T(8,128)(2,1)} %all-to-all-done.1) | data formatting | bytes 6291456
  (82 shorter events, 10.0 us)
Async XLA Ops:
  0.6 35.4 %copy-start = (bf16[96,2,64,128]{3,2,1,0:T(8,128)(2,1)S(1)}, bf16[96,2,64,128]{3,2,1,0:T(8,128)(2,1)}, u32[]{:S(2)}) copy-start(bf16[96,2,64,128]{3,2,1,0:T(8,128)(2,1)} %param.13) | copy-start | bytes 9437188
  3.1 0.6 copy-start.7
  5.9 40.3 %all-to-all-start = ((s32[16,2,2]{1,2,0:T(2,128)}), s32[16,2,2]{1,2,0:T(2,128)S(1)}, u32[]{:S(2)}, u32[]{:S(2)}) async-start(s32[16,2,2]{1,2,0:T(2,128)} %copy.134), calls=%async_computation | async-start | bytes 32768 | tf_op jit(solution)/shard_map/all_to_all | solution.py:104
  26.9 8.8 %copy-start.8 = (s32[32,3]{0,1:T(4,128)S(1)}, s32[32,3]{0,1:T(4,128)}, u32[]{:S(2)}) copy-start(s32[32,3]{0,1:T(4,128)} %param.16) | copy-start | bytes 1156
  41.9 2.7 copy-start.3
  41.9 2.6 copy-start.4
  41.9 2.6 copy-start.6
  41.9 2.8 copy-start.5
  46.2 14.6 %all-to-all-start.3 = ((bf16[32,4,2,128]{3,1,2,0:T(4,128)(2,1)}), bf16[32,4,2,128]{3,1,2,0:T(4,128)(2,1)S(1)}, u32[]{:S(2)}, u32[]{:S(2)}) async-start(bf16[32,4,2,128]{3,1,2,0:T(4,128)(2,1)} %copy.139), calls=%async_computation.3 | async-start | bytes 131072 | tf_op jit(solution)/shard_map/all_to_all | solution.py:101
  60.8 11.4 %all-to-all-start.2 = ((bf16[32,4,512]{2,1,0:T(4,128)(2,1)}), bf16[32,4,512]{2,1,0:T(4,128)(2,1)S(1)}, u32[]{:S(2)}, u32[]{:S(2)}) async-start(bf16[32,4,512]{2,1,0:T(4,128)(2,1)} %reshape.312), calls=%async_computation.2 | async-start | bytes 262144 | tf_op jit(solution)/shard_map/all_to_all | solution.py:100
  65.9 11.2 %copy-start.2 = (s32[32]{0:T(128)S(1)}, s32[32]{0:T(128)}, u32[]{:S(2)}) copy-start(s32[32]{0:T(128)} %param.15) | copy-start | bytes 388
  72.1 46.2 %all-to-all-start.1 = ((bf16[32,3,2,64,128]{4,3,2,1,0:T(8,128)(2,1)}), bf16[32,3,2,64,128]{4,3,2,1,0:T(8,128)(2,1)}, u32[]{:S(2)}, u32[]{:S(2)}) async-start(bf16[32,3,2,64,128]{4,3,2,1,0:T(8,128)(2,1)} %broadcast_select_fusion), calls=%async_computation.1 | async-start | bytes 6291456 | tf_op jit(solution)/shard_map/all_to_all | solution.py:99
  77.1 5.0 %copy-start.9 = (s32[16]{0:T(128)S(1)}, s32[16]{0:T(128)}, u32[]{:S(2)}) copy-start(s32[16]{0:T(128)} %param.19) | copy-start | bytes 196
  77.1 5.0 %copy-start.10 = (s32[16]{0:T(128)S(1)}, s32[16]{0:T(128)}, u32[]{:S(2)}) copy-start(s32[16]{0:T(128)} %param.17) | copy-start | bytes 196
  309.2 5.0 %copy-start.1 = (bf16[96,2,64,128]{3,2,1,0:T(8,128)(2,1)S(1)}, bf16[96,2,64,128]{3,2,1,0:T(8,128)(2,1)}, u32[]{:S(2)}) copy-start(bf16[96,2,64,128]{3,2,1,0:T(8,128)(2,1)} %param.13) | copy-start | bytes 9437188
where the time goes:
time: 317 us; the launch traced here: 314 us
  blocking collectives  170 us (54%)
  waiting for transfers between devices  42.5 us (13%)
  local copies, waits for them, and re-layouts  39.9 us (13%)
  matrix products  26.5 us (8%)
  starting transfers between devices  24.1 us (8%)
  other arithmetic  10.1 us (3%)
    psum x1, blocking collectives, local(): summed = lax.psum(partial_sum, 'tp')  170 us
    all_to_all x1, waiting for transfers between devices, local(): lax.all_to_all(slot_pages, 'inst', split_axis=0, concat_axis=0, tiled=True)  30.7 us
    dot_general x1, local copies, waits for them, and re-layouts, local(): jnp.dot(hidden.reshape(-1, width), query_weight, preferred_element_type=j...  11.4 us
    dot_general x1, matrix products, local(): jnp.dot(combined.reshape(-1, combined.shape[-1]), output_weight, preferre...  8.95 us
    all_to_all x1, starting transfers between devices, local(): lax.all_to_all(slot_meta, 'inst', split_axis=0, concat_axis=0, tiled=True)  8.45 us
    all_to_all x1, starting transfers between devices, local(): lax.all_to_all(slot_fresh, 'inst', split_axis=0, concat_axis=0, tiled=True)  7.23 us
    dot_general x1, matrix products, local(): jnp.dot(hidden.reshape(-1, width), query_weight, preferred_element_type=j...  6.95 us
  transfers between devices with their start and end apart: 4, of which 3 were waited for; matrix products, arithmetic and copies ran while one was open for 14% of the time, Pallas kernels for 0%

commit v1 on v0

v1 whole, which is shorter than its diff:
```python
import jax
import jax.numpy as jnp
import numpy as np
from jax import lax
from jax.experimental import pallas as pl
from jax.experimental.pallas import tpu as pltpu
from jax.sharding import PartitionSpec as P

HD = 128
GROUP = 4
CAP = 2
STEPS = 4
REQS = 32
MIG = 16
INST = 16
PAGE = 64
MAXP = 3
RING = 4
SPAN = MAXP * PAGE
ROWS = STEPS * REQS
WIDE = 256
ROPE_BASE = 500000.0
F32 = jnp.float32
BF16 = jnp.bfloat16
SMEM = pl.BlockSpec(memory_space=pltpu.SMEM)
VMEM = pl.BlockSpec(memory_space=pltpu.VMEM)
ANY = pl.BlockSpec(memory_space=pl.ANY)


def pack_kernel(table, mreq, mdest, resume, pool, send, pick, slot_req, count, zeros, wide, sem):
    zeros[...] = jnp.zeros_like(zeros)

    def clear(s, carry):
        slot_req[s] = -1
        return carry

    def fresh(d, carry):
        count[d] = 0
        return carry

    lax.fori_loop(0, INST * CAP, clear, 0)
    lax.fori_loop(0, INST, fresh, 0)

    def place(k, carry):
        d = mdest[k]
        c = count[d]
        count[d] = c + 1
        slot_req[d * CAP + c] = mreq[k]
        return carry

    lax.fori_loop(0, MIG, place, 0)

    def ship(s, carry):
        req = slot_req[s]

        @pl.when(req >= 0)
        def _():
            for p in range(MAXP):
                pltpu.make_async_copy(pool.at[table[req * MAXP + p]], send.at[s, p], sem).start()

        @pl.when(req < 0)
        def _():
            pltpu.make_async_copy(zeros, send.at[s], sem).start()

        return carry

    lax.fori_loop(0, INST * CAP, ship, 0)

    rows = lax.broadcasted_iota(jnp.int32, (2 * ROWS, ROWS), 0)
    cols = lax.broadcasted_iota(jnp.int32, (2 * ROWS, ROWS), 1)
    wide[...] = jnp.where(rows == cols, 1.0, 0.0).astype(F32)
    lane = lax.broadcasted_iota(jnp.int32, (1, ROWS), 1)

    def clear_count(d, carry):
        count[d] = 0
        return carry

    lax.fori_loop(0, INST, clear_count, 0)

    def choose(k, carry):
        d = mdest[k]
        c = count[d]
        count[d] = c + 1
        req = mreq[k]
        first = resume[k]
        for t in range(STEPS):
            at = t * REQS + req
            here = jnp.where(lane == at, 1.0, 0.0).astype(F32)
            stay = jnp.where(t < first, 1.0, 0.0).astype(F32)
            wide[pl.ds(at, 1), :] = here * stay
            wide[pl.ds(ROWS + d * (STEPS * CAP) + t * CAP + c, 1), :] = here * (1.0 - stay)
        return carry

    lax.fori_loop(0, MIG, choose, 0)
    pick[...] = wide[...].astype(BF16)
    pltpu.make_async_copy(send, send, sem).wait()


def attend_kernel(
    where, lengths, table, len_row, freq, hidden, wq, wo, pool, new_kv,
    near0, near1, near2, near3,
    x, q_w, o_w, kv, fresh, turned, scores, probs, mixed, outs, acc, x_sem, q_sem, o_sem, kv_sem, out_sem,
):
    chunks = x_sem.shape[0]
    depth = x.shape[1] // chunks
    share = outs.shape[-1]
    y, z = where[0], where[1]

    def load(k):
        cut = pl.ds(k * depth, depth)
        return (
            pltpu.make_async_copy(hidden.at[:, cut], x.at[:, cut], x_sem.at[k]),
            pltpu.make_async_copy(wq.at[cut], q_w.at[cut], q_sem.at[k]),
        )

    for k in range(chunks):
        for copy in load(k):
            copy.start()
    kv_copy = pltpu.make_async_copy(pool, kv, kv_sem)
    kv_copy.start()
    order = [(k, j) for k in (2, 1, 3, 0) for j in (1, 0)]

    def weight(i):
        k, j = order[i]
        n = lax.rem(y + j, 2) * RING + lax.rem(z + k, RING)
        cut = pl.ds(pl.multiple_of(n * share, share), share)
        return pltpu.make_async_copy(wo.at[:, cut], o_w.at[i], o_sem.at[i])

    for i in range(len(order)):
        weight(i).start()

    row = lax.broadcasted_iota(jnp.int32, (REQS * 16, ROWS * 2), 0)
    col = lax.broadcasted_iota(jnp.int32, (REQS * 16, ROWS * 2), 1)
    home = (row % 16) * (2 * REQS) + (row // 16) * 2
    source = new_kv[...]
    for j in range(2):
        choice = jnp.where((col == home + j) & (row % 16 < STEPS), 1.0, 0.0).astype(BF16)
        fresh[j] = jnp.dot(choice, source, preferred_element_type=F32).astype(BF16)

    at = lax.broadcasted_iota(jnp.int32, (ROWS, REQS), 0)
    req = lax.broadcasted_iota(jnp.int32, (ROWS, REQS), 1)
    base = jnp.sum(
        jnp.where(at % REQS == req, len_row[...].astype(F32), 0.0), axis=1, keepdims=True
    )
    step = (lax.broadcasted_iota(jnp.int32, (ROWS, 1), 0) // REQS).astype(F32)
    angles = (base + step) * freq[...]
    cos = jnp.cos(angles)
    sin = jnp.sin(angles)
    lane = lax.broadcasted_iota(jnp.int32, (ROWS, HD), 1)
    sin = jnp.where(lane < HD // 2, -sin, sin)

    for k in range(chunks):
        for copy in load(k):
            copy.wait()
        cut = pl.ds(k * depth, depth)
        part = jnp.dot(x[:, cut], q_w[cut], preferred_element_type=F32)
        if k == 0:
            acc[...] = part
        else:
            acc[...] += part

    for g in range(GROUP):
        head = acc[:, g * HD:(g + 1) * HD]
        turned[g * ROWS:(g + 1) * ROWS] = head * cos + pltpu.roll(head, HD // 2, 1) * sin

    kv_copy.wait()
    scale = HD ** -0.5
    spot = lax.broadcasted_iota(jnp.int32, (16, WIDE), 1)
    when = lax.broadcasted_iota(jnp.int32, (16, WIDE), 0) % STEPS
    causal = (spot >= SPAN) & (spot - SPAN <= when)
    rest = jnp.zeros((WIDE - SPAN - 16, HD), BF16)

    def pages(r, j):
        cached = [kv[table[r * MAXP + p], j] for p in range(MAXP)]
        return jnp.concatenate(cached + [fresh[j, r * 16:(r + 1) * 16], rest], axis=0)

    for r in range(REQS):
        query = turned[pl.ds(r, 16, stride=REQS), :].astype(BF16)
        found = lax.dot_general(
            query, pages(r, 0), (((1,), (1,)), ((), ())), preferred_element_type=F32
        ) * scale
        live = (spot < lengths[r]) | causal
        scores[r * 16:(r + 1) * 16] = jnp.where(live, found, -1e30)

    held = scores[...]
    top = jnp.max(held, axis=1, keepdims=True)
    raised = jnp.exp(held - top)
    total = jnp.sum(raised, axis=1, keepdims=True)
    probs[...] = (raised * (1.0 / total)).astype(BF16)

    for r in range(REQS):
        mixed[pl.ds(r, 16, stride=REQS), :] = jnp.dot(
            probs[r * 16:(r + 1) * 16], pages(r, 1), preferred_element_type=F32
        )

    rows = jnp.concatenate(
        [mixed[g * ROWS:(g + 1) * ROWS].astype(BF16) for g in range(GROUP)], axis=1
    )
    near = (near0, near1, near2, near3)
    stores = []
    for i, (k, j) in enumerate(order):
        weight(i).wait()
        outs[i] = jnp.dot(rows, o_w[i], preferred_element_type=F32).astype(BF16)
        store = pltpu.make_async_copy(outs.at[i], near[k].at[j], out_sem.at[i])
        store.start()
        stores.append(store)
    for store in stores:
        store.wait()


def sum_kernel(own, a, b, c, out):
    out[...] = (
        own[1].astype(F32) + a[1].astype(F32) + b[1].astype(F32) + c[1].astype(F32)
    ).astype(BF16)


def close_kernel(own, a, b, c, other, pick, home, slots):
    total = (
        own[0].astype(F32) + a[0].astype(F32) + b[0].astype(F32) + c[0].astype(F32)
        + other[...].astype(F32)
    ).astype(BF16)
    both = jnp.dot(pick[...], total, preferred_element_type=F32).astype(BF16)
    home[...] = both[:ROWS]
    slots[...] = both[ROWS:]


def local(
    hidden, query_weight, output_weight, kv_pool, new_kv,
    lengths, page_table, mig_req, mig_dest, resume,
):
    width = hidden.shape[-1]
    share = width // lax.axis_size("tp")
    table = page_table.reshape(-1)
    send, pick = pl.pallas_call(
        pack_kernel,
        out_shape=(
            jax.ShapeDtypeStruct((INST * CAP,) + (MAXP,) + kv_pool.shape[1:], BF16),
            jax.ShapeDtypeStruct((2 * ROWS, ROWS), BF16),
        ),
        in_specs=[SMEM] * 4 + [ANY],
        out_specs=(ANY, VMEM),
        scratch_shapes=[
            pltpu.SMEM((INST * CAP,), jnp.int32),
            pltpu.SMEM((INST,), jnp.int32),
            pltpu.VMEM((MAXP,) + kv_pool.shape[1:], BF16),
            pltpu.VMEM((2 * ROWS, ROWS), F32),
            pltpu.SemaphoreType.DMA,
        ],
        cost_estimate=pl.CostEstimate(flops=0, bytes_accessed=6 << 20, transcendentals=0),
        name="pack_pages",
    )(table, mig_req, mig_dest.reshape(-1), resume, kv_pool)
    arrival_cache = lax.all_to_all(send, "inst", split_axis=0, concat_axis=0, tiled=True)

    tp = lax.axis_index("tp")
    where = jnp.stack([tp // RING, tp % RING]).astype(jnp.int32)
    half = HD // 2
    inverse = np.float32(ROPE_BASE) ** (-np.arange(half, dtype=np.float32) * np.float32(2.0) / np.float32(HD))
    freq = jnp.asarray(np.concatenate([inverse, inverse])[None, :].astype(np.float32))
    chunks = 8
    near_shape = jax.ShapeDtypeStruct((2, ROWS, share), BF16)
    near = pl.pallas_call(
        attend_kernel,
        out_shape=(near_shape,) * RING,
        in_specs=[SMEM, SMEM, SMEM, VMEM, VMEM, ANY, ANY, ANY, ANY, VMEM],
        out_specs=(ANY,) * RING,
        scratch_shapes=[
            pltpu.VMEM((ROWS, width), BF16),
            pltpu.VMEM(query_weight.shape, BF16),
            pltpu.VMEM((2 * RING, GROUP * HD, share), BF16),
            pltpu.VMEM(kv_pool.shape, BF16),
            pltpu.VMEM((2, REQS * 16, HD), BF16),
            pltpu.VMEM((GROUP * ROWS, HD), F32),
            pltpu.VMEM((REQS * 16, WIDE), F32),
            pltpu.VMEM((REQS * 16, WIDE), BF16),
            pltpu.VMEM((GROUP * ROWS, HD), F32),
            pltpu.VMEM((2 * RING, ROWS, share), BF16),
            pltpu.VMEM((ROWS, GROUP * HD), F32),
            pltpu.SemaphoreType.DMA((chunks,)),
            pltpu.SemaphoreType.DMA((chunks,)),
            pltpu.SemaphoreType.DMA((2 * RING,)),
            pltpu.SemaphoreType.DMA,
            pltpu.SemaphoreType.DMA((2 * RING,)),
        ],
        compiler_params=pltpu.CompilerParams(vmem_limit_bytes=40 << 20),
        cost_estimate=pl.CostEstimate(flops=2_400_000_000, bytes_accessed=24 << 20, transcendentals=200_000),
        name="attend",
    )(
        where, lengths, table, lengths.reshape(1, REQS), freq,
        hidden.reshape(ROWS, width), query_weight, output_weight, kv_pool,
        new_kv.reshape(2 * ROWS, HD),
    )

    def shift(k):
        return [(s, (s // RING) * RING + (s + k) % RING) for s in range(2 * RING)]

    got = [lax.ppermute(near[k], "tp", shift(k)) for k in (2, 1, 3)]
    part = pl.pallas_call(
        sum_kernel,
        out_shape=jax.ShapeDtypeStruct((ROWS, share), BF16),
        in_specs=[VMEM] * 4,
        out_specs=VMEM,
        cost_estimate=pl.CostEstimate(flops=0, bytes_accessed=2 << 20, transcendentals=0),
        name="sum_ring",
    )(near[0], *got)
    other = lax.ppermute(part, "tp", [(s, (s + RING) % (2 * RING)) for s in range(2 * RING)])
    home, slots = pl.pallas_call(
        close_kernel,
        out_shape=(jax.ShapeDtypeStruct((ROWS, share), BF16),) * 2,
        in_specs=[VMEM] * 6,
        out_specs=(VMEM,) * 2,
        cost_estimate=pl.CostEstimate(flops=0, bytes_accessed=2 << 20, transcendentals=0),
        name="close",
    )(near[0], *got, other, pick)
    rows = lax.all_to_all(
        slots.reshape(INST, STEPS * CAP, share), "inst", split_axis=0, concat_axis=0, tiled=True
    )
    arrival = jnp.transpose(rows.reshape(INST, STEPS, CAP, share), (1, 0, 2, 3))
    return (
        home.reshape(STEPS, REQS, share),
        arrival.reshape(STEPS, INST * CAP, share),
        arrival_cache,
    )


def solution(mesh):
    in_specs = (
        P(None, "inst", None),
        P(None, "tp"),
        P("tp", None),
        P("inst", None, None, "tp"),
        P(None, "inst", None, "tp"),
        P("inst"),
        P("inst", None),
        P("inst"),
        P("inst", None),
        P("inst"),
    )
    out_specs = (P(None, "inst", "tp"), P(None, "inst", "tp"), P("inst", None, None, None, "tp"))
    return jax.shard_map(local, mesh=mesh, in_specs=in_specs, out_specs=out_specs, check_vma=False)
```

time: 317 us -> 169 us (0.53)
  blocking collectives: 170 us -> 16.7 us
  Pallas kernels: 0 us -> 64.4 us
  matrix products: 26.5 us -> 0 us
  local copies, waits for them, and re-layouts: 39.9 us -> 13.4 us
  waiting for transfers between devices: 42.5 us -> 59.9 us
  starting transfers between devices: 24.1 us -> 12.7 us
  other arithmetic: 10.1 us -> 0.08 us
    psum x1 -> x0, blocking collectives: 170 us -> none  [local(): summed = lax.psum(partial_sum, 'tp')]
    pallas_call x0 -> x4, Pallas kernels: none -> 64.4 us  [the longest x1 50.5 us: local(): pl.pallas_call(pack_kernel, out_shape=(jax.ShapeDtypeStruct((INST * CAP,)...]
    dot_general x10 -> x0, matrix products: 26.5 us -> none  [the longest x1 8.95 us: local(): jnp.dot(combined.reshape(-1, combined.shape[-1]), output_weight, preferre...]
    ppermute x0 -> x4, waiting for transfers between devices: none -> 20.9 us  [the longest x3 20.9 us: local(): got = [lax.ppermute(near[k], 'tp', shift(k)) for k in (2, 1, 3)]]
    all_to_all x4 -> x1, starting transfers between devices: 24.1 us -> 4.33 us  [local(): lax.all_to_all(send, 'inst', split_axis=0, concat_axis=0, tiled=True)]
    all_to_all x0 -> x1, blocking collectives: none -> 16.7 us  [local(): lax.all_to_all(slots.reshape(INST, STEPS * CAP, share), 'inst', split_axi...]
    dot_general x3 -> x0, local copies, waits for them, and re-layouts: 11.8 us -> none  [the longest x1 11.4 us: local(): jnp.dot(hidden.reshape(-1, width), query_weight, preferred_element_type=j...]
    gather x6 -> x0, local copies, waits for them, and re-layouts: 9.57 us -> none  [the longest x1 3.16 us: local(): pages[slot_request]]
  transfers between devices with their start and end apart: 4 -> 5, of which waited for: 3 -> 3; matrix products, arithmetic and copies ran while one was open for 14% -> 2% of each run, Pallas kernels for 0% -> 30%
where the time goes in v1:
time: 169 us; the launch traced here: 168 us
  Pallas kernels  64.4 us (38%)
  waiting for transfers between devices  59.9 us (35%)
  blocking collectives  16.7 us (10%)
  local copies, waits for them, and re-layouts  13.4 us (8%)
  starting transfers between devices  12.7 us (8%)
    pallas_call x1, Pallas kernels, local(): pl.pallas_call(pack_kernel, out_shape=(jax.ShapeDtypeStruct((INST * CAP,)...  50.5 us
    all_to_all x1, waiting for transfers between devices, local(): lax.all_to_all(send, 'inst', split_axis=0, concat_axis=0, tiled=True)  39 us
    ppermute x3, waiting for transfers between devices, local(): got = [lax.ppermute(near[k], 'tp', shift(k)) for k in (2, 1, 3)]  20.9 us
    all_to_all x1, blocking collectives, local(): lax.all_to_all(slots.reshape(INST, STEPS * CAP, share), 'inst', split_axi...  16.7 us
    unnamed x24, local copies, waits for them, and re-layouts  10.5 us
    pallas_call x1, Pallas kernels, local(): pl.pallas_call(attend_kernel, out_shape=(near_shape,) * RING, in_specs=[S...  8.84 us
    ppermute x3, starting transfers between devices, local(): got = [lax.ppermute(near[k], 'tp', shift(k)) for k in (2, 1, 3)]  7.1 us
    all_to_all x1, starting transfers between devices, local(): lax.all_to_all(send, 'inst', split_axis=0, concat_axis=0, tiled=True)  4.33 us
  transfers between devices with their start and end apart: 5, of which 3 were waited for; matrix products, arithmetic and copies ran while one was open for 2% of the time, Pallas kernels for 30%

profile of v1, /device:TPU:1, one launch (start us, length us, event | category | flops | bytes accessed | tf_op | source)
XLA Modules:
  0.0 168.0 jit_solution(155314674997183923)
XLA Ops:
  0.6 0.8 copy.16
  1.4 0.1 reshape.33.table
  1.5 0.1 pad_add_fusion.where
  1.6 1.9 %copy-done = bf16[96,2,64,128]{3,2,1,0:T(8,128)(2,1)S(1)} copy-done((bf16[96,2,64,128]{3,2,1,0:T(8,128)(2,1)S(1)}, bf16[96,2,64,128]{3,2,1,0:T(8,128)(2,1)}, u32[]{:S(2)}) %copy-start) | copy-done | bytes 3145752
  3.5 1.6 copy-done.1
  5.1 0.8 copy-done.3
  5.9 0.7 copy-done.5
  6.6 0.7 copy-done.6
  7.3 8.8 %attend.1 = (bf16[2,128,1024]{2,1,0:T(8,128)(2,1)S(1)}, bf16[2,128,1024]{2,1,0:T(8,128)(2,1)S(1)}, bf16[2,128,1024]{2,1,0:T(8,128)(2,1)S(1)}, bf16[2,128,1024]{2,1,0:T(8,128)(2,1)S(1)}) custom-call(s32[2]{0:T(128)S(1)} %pad_add_fusion.where, s32[32]{0:T(128)S(1)} %copy-done.5, s32[96]{0:T(128)S(1)} %reshape.33.table, s32[1,32]{1,0:T(1,128)S(1)} %bitcast.13, ...), custom_call_target="tpu_custom_call" | custom-call | flops 2400000000 | bytes 25165824 | tf_op jit(solution)/shard_map/attend/pallas_call | solution.py:261
  16.1 0.8 copy-done.2
  16.9 4.4 %collective-permute-start = (bf16[2,128,1024]{2,1,0:T(8,128)(2,1)S(1)}, bf16[2,128,1024]{2,1,0:T(8,128)(2,1)S(1)}, u32[]{:S(2)}, u32[]{:S(2)}) collective-permute-start(bf16[2,128,1024]{2,1,0:T(8,128)(2,1)S(1)} %get-tuple-element.12), channel_id=1, source_target_pairs={{0,2},{1,3},{2,0},{3,1},{4,6},{5,7},{6,4},{7,5},{8,10},{9,11},{10,... | collective-permute-start | bytes 1572872 | tf_op jit(solution)/shard_map/ppermute | solution.py:296
  21.3 0.7 collective-permute-start.1
  22.1 1.9 %collective-permute-start.2 = (bf16[2,128,1024]{2,1,0:T(8,128)(2,1)S(1)}, bf16[2,128,1024]{2,1,0:T(8,128)(2,1)S(1)}, u32[]{:S(2)}, u32[]{:S(2)}) collective-permute-start(bf16[2,128,1024]{2,1,0:T(8,128)(2,1)S(1)} %get-tuple-element.14), channel_id=1, source_target_pairs={{0,3},{1,0},{2,1},{3,2},{4,7},{5,4},{6,5},{7,6},{8,11},{9,8},{10,9... | collective-permute-start | bytes 1572872 | tf_op jit(solution)/shard_map/ppermute | solution.py:296
  24.0 9.0 %collective-permute-done.a = bf16[2,128,1024]{2,1,0:T(8,128)(2,1)S(1)} collective-permute-done((bf16[2,128,1024]{2,1,0:T(8,128)(2,1)S(1)}, bf16[2,128,1024]{2,1,0:T(8,128)(2,1)S(1)}, u32[]{:S(2)}, u32[]{:S(2)}) %collective-permute-start) | collective-permute-done | bytes 524320 | tf_op jit(solution)/shard_map/ppermute | solution.py:296
  33.0 11.9 %collective-permute-done.1.b = bf16[2,128,1024]{2,1,0:T(8,128)(2,1)S(1)} collective-permute-done((bf16[2,128,1024]{2,1,0:T(8,128)(2,1)S(1)}, bf16[2,128,1024]{2,1,0:T(8,128)(2,1)S(1)}, u32[]{:S(2)}, u32[]{:S(2)}) %collective-permute-start.1) | collective-permute-done | bytes 524320 | tf_op jit(solution)/shard_map/ppermute | solution.py:296
  44.9 0.0 collective-permute-done.2.c
  45.0 0.8 copy-done.8
  45.8 0.2 copy-done.9
  45.9 2.3 %sum_ring.1 = bf16[128,1024]{1,0:T(8,128)(2,1)} custom-call(bf16[2,128,1024]{2,1,0:T(8,128)(2,1)} %copy-done.2, bf16[2,128,1024]{2,1,0:T(8,128)(2,1)} %copy-done.7, bf16[2,128,1024]{2,1,0:T(8,128)(2,1)} %copy-done.8, bf16[2,128,1024]{2,1,0:T(8,128)(2,1)} %copy-done.9), custom_call_target="tpu_custom_call" | custom-call | bytes 2097152 | tf_op jit(solution)/shard_map/sum_ring/pallas_call | solution.py:297
  48.3 1.3 collective-permute-start.3
  49.6 50.5 %pack_pages.1 = (bf16[32,3,2,64,128]{4,3,2,1,0:T(8,128)(2,1)}, bf16[256,128]{1,0:T(8,128)(2,1)}) custom-call(s32[96]{0:T(128)} %copy-done.4, s32[16]{0:T(128)} %mreq.1, s32[16]{0:T(128)} %bitcast.16, s32[16]{0:T(128)} %resume.1, bf16[96,2,64,128]{3,2,1,0:T(8,128)(2,1)} %pool.3), custom_call_target="tpu_custom_call" | custom-call | bytes 6291456 | tf_op jit(solution)/shard_map/pack_pages/pallas_call | solution.py:234
  100.1 0.0 collective-permute-done.3.other
  100.1 0.0 copy-start.10
  100.1 0.7 copy-done.10
  100.8 2.7 %close.1 = (bf16[128,1024]{1,0:T(8,128)(2,1)}, bf16[128,1024]{1,0:T(8,128)(2,1)}) custom-call(bf16[2,128,1024]{2,1,0:T(8,128)(2,1)} %copy-done.2, bf16[2,128,1024]{2,1,0:T(8,128)(2,1)} %copy-done.7, bf16[2,128,1024]{2,1,0:T(8,128)(2,1)} %copy-done.8, bf16[2,128,1024]{2,1,0:T(8,128)(2,1)} %copy-done.9, bf16[128,1024]{1,0:T(8,128)(2,1)} %copy-done.10, ...), custom_call_target="tpu_custom_call" | custom-call | bytes 2097152 | tf_op jit(solution)/shard_map/close/pallas_call | solution.py:306
  103.5 16.7 %all_to_all.10 = bf16[16,8,1024]{2,1,0:T(8,128)(2,1)S(1)} all-to-all(bf16[16,8,1024]{2,1,0:T(8,128)(2,1)} %bitcast.15), channel_id=1, replica_groups=mesh['inst'=16,'tp'=8] {'inst'}, dimensions={0} | all-to-all | bytes 524288 | tf_op jit(solution)/shard_map/all_to_all | solution.py:314
  120.2 4.3 %all-to-all-start.1 = ((bf16[32,3,2,64,128]{4,3,2,1,0:T(8,128)(2,1)}), bf16[32,3,2,64,128]{4,3,2,1,0:T(8,128)(2,1)S(1)}, u32[]{:S(2)}, u32[]{:S(2)}) async-start(bf16[32,3,2,64,128]{4,3,2,1,0:T(8,128)(2,1)} %get-tuple-element.18), calls=%async_computation.1 | async-start | bytes 6291456 | tf_op jit(solution)/shard_map/all_to_all | solution.py:252
  124.6 0.8 reshape.40
  125.4 1.1 copy.19
  126.5 0.8 reshape.41
  127.3 39.0 %all-to-all-done.1 = bf16[32,3,2,64,128]{4,3,2,1,0:T(8,128)(2,1)S(1)} async-done(((bf16[32,3,2,64,128]{4,3,2,1,0:T(8,128)(2,1)}), bf16[32,3,2,64,128]{4,3,2,1,0:T(8,128)(2,1)S(1)}, u32[]{:S(2)}, u32[]{:S(2)}) %all-to-all-start.1) | async-done | bytes 3145760 | tf_op jit(solution)/shard_map/all_to_all | solution.py:252
  166.3 1.7 copy.21
  (12 shorter events, 0.0 us)
Async XLA Ops:
  1.5 14.6 %copy-start.4 = (s32[96]{0:T(128)}, s32[96]{0:T(128)S(1)}, u32[]{:S(2)}) copy-start(s32[96]{0:T(128)S(1)} %reshape.33.table) | copy-start | bytes 1156
  1.6 1.9 %copy-start = (bf16[96,2,64,128]{3,2,1,0:T(8,128)(2,1)S(1)}, bf16[96,2,64,128]{3,2,1,0:T(8,128)(2,1)}, u32[]{:S(2)}) copy-start(bf16[96,2,64,128]{3,2,1,0:T(8,128)(2,1)} %pool.3) | copy-start | bytes 9437188
  3.5 1.6 copy-start.1
  5.1 0.8 copy-start.3
  5.9 0.7 copy-start.5
  6.6 0.7 copy-start.6
  16.1 0.8 copy-start.2
  16.9 16.1 %collective-permute-start = (bf16[2,128,1024]{2,1,0:T(8,128)(2,1)S(1)}, bf16[2,128,1024]{2,1,0:T(8,128)(2,1)S(1)}, u32[]{:S(2)}, u32[]{:S(2)}) collective-permute-start(bf16[2,128,1024]{2,1,0:T(8,128)(2,1)S(1)} %get-tuple-element.12), channel_id=1, source_target_pairs={{0,2},{1,3},{2,0},{3,1},{4,6},{5,7},{6,4},{7,5},{8,10},{9,11},{10,... | collective-permute-start | bytes 1572872 | tf_op jit(solution)/shard_map/ppermute | solution.py:296
  21.3 23.6 %collective-permute-start.1 = (bf16[2,128,1024]{2,1,0:T(8,128)(2,1)S(1)}, bf16[2,128,1024]{2,1,0:T(8,128)(2,1)S(1)}, u32[]{:S(2)}, u32[]{:S(2)}) collective-permute-start(bf16[2,128,1024]{2,1,0:T(8,128)(2,1)S(1)} %get-tuple-element.13), channel_id=1, source_target_pairs={{0,1},{1,2},{2,3},{3,0},{4,5},{5,6},{6,7},{7,4},{8,9},{9,10},{10,1... | collective-permute-start | bytes 1572872 | tf_op jit(solution)/shard_map/ppermute | solution.py:296
  22.1 22.9 %collective-permute-start.2 = (bf16[2,128,1024]{2,1,0:T(8,128)(2,1)S(1)}, bf16[2,128,1024]{2,1,0:T(8,128)(2,1)S(1)}, u32[]{:S(2)}, u32[]{:S(2)}) collective-permute-start(bf16[2,128,1024]{2,1,0:T(8,128)(2,1)S(1)} %get-tuple-element.14), channel_id=1, source_target_pairs={{0,3},{1,0},{2,1},{3,2},{4,7},{5,4},{6,5},{7,6},{8,11},{9,8},{10,9... | collective-permute-start | bytes 1572872 | tf_op jit(solution)/shard_map/ppermute | solution.py:296
  33.0 11.9 %copy-start.7 = (bf16[2,128,1024]{2,1,0:T(8,128)(2,1)}, bf16[2,128,1024]{2,1,0:T(8,128)(2,1)S(1)}, u32[]{:S(2)}) copy-start(bf16[2,128,1024]{2,1,0:T(8,128)(2,1)S(1)} %collective-permute-done.a) | copy-start | bytes 1572868
  44.9 0.8 copy-start.8
  45.0 1.0 copy-start.9
  48.3 51.8 %collective-permute-start.3 = (bf16[128,1024]{1,0:T(8,128)(2,1)}, bf16[128,1024]{1,0:T(8,128)(2,1)S(1)}, u32[]{:S(2)}, u32[]{:S(2)}) collective-permute-start(bf16[128,1024]{1,0:T(8,128)(2,1)} %sum_ring.1), channel_id=1, source_target_pairs={{0,4},{1,5},{2,6},{3,7},{4,0},{5,1},{6,2},{7,3},{8,12},{9,13},{10,... | collective-permute-start | bytes 786440 | tf_op jit(solution)/shard_map/ppermute | solution.py:305
  100.1 0.7 copy-start.10
  120.2 46.1 %all-to-all-start.1 = ((bf16[32,3,2,64,128]{4,3,2,1,0:T(8,128)(2,1)}), bf16[32,3,2,64,128]{4,3,2,1,0:T(8,128)(2,1)S(1)}, u32[]{:S(2)}, u32[]{:S(2)}) async-start(bf16[32,3,2,64,128]{4,3,2,1,0:T(8,128)(2,1)} %get-tuple-element.18), calls=%async_computation.1 | async-start | bytes 6291456 | tf_op jit(solution)/shard_map/all_to_all | solution.py:252

commit v2 on v1

--- a/solution.py
+++ b/solution.py
@@ -20,6 +20,7 @@
 ROWS = STEPS * REQS
 WIDE = 256
 ROPE_BASE = 500000.0
+VMEM_LIMIT = 58 << 20
 F32 = jnp.float32
 BF16 = jnp.bfloat16
 SMEM = pl.BlockSpec(memory_space=pltpu.SMEM)
@@ -27,7 +28,9 @@
 ANY = pl.BlockSpec(memory_space=pl.ANY)
 
 
-def pack_kernel(table, mreq, mdest, resume, pool, send, pick, slot_req, count, zeros, wide, sem):
+def pack_kernel(table, mreq, mdest, resume, pool, send, pick, slot_req, count, kv, zeros, wide, kv_sem, sem):
+    load = pltpu.make_async_copy(pool, kv, kv_sem)
+    load.start()
     zeros[...] = jnp.zeros_like(zeros)
 
     def clear(s, carry):
@@ -49,6 +52,7 @@
         return carry
 
     lax.fori_loop(0, MIG, place, 0)
+    load.wait()
 
     def ship(s, carry):
         req = slot_req[s]
@@ -56,7 +60,7 @@
         @pl.when(req >= 0)
         def _():
             for p in range(MAXP):
-                pltpu.make_async_copy(pool.at[table[req * MAXP + p]], send.at[s, p], sem).start()
+                pltpu.make_async_copy(kv.at[table[req * MAXP + p]], send.at[s, p], sem).start()
 
         @pl.when(req < 0)
         def _():
@@ -242,10 +246,13 @@
         scratch_shapes=[
             pltpu.SMEM((INST * CAP,), jnp.int32),
             pltpu.SMEM((INST,), jnp.int32),
+            pltpu.VMEM(kv_pool.shape, BF16),
             pltpu.VMEM((MAXP,) + kv_pool.shape[1:], BF16),
             pltpu.VMEM((2 * ROWS, ROWS), F32),
             pltpu.SemaphoreType.DMA,
+            pltpu.SemaphoreType.DMA,
         ],
+        compiler_params=pltpu.CompilerParams(vmem_limit_bytes=VMEM_LIMIT),
         cost_estimate=pl.CostEstimate(flops=0, bytes_accessed=6 << 20, transcendentals=0),
         name="pack_pages",
     )(table, mig_req, mig_dest.reshape(-1), resume, kv_pool)
@@ -281,7 +288,7 @@
             pltpu.SemaphoreType.DMA,
             pltpu.SemaphoreType.DMA((2 * RING,)),
         ],
-        compiler_params=pltpu.CompilerParams(vmem_limit_bytes=40 << 20),
+        compiler_params=pltpu.CompilerParams(vmem_limit_bytes=VMEM_LIMIT),
         cost_estimate=pl.CostEstimate(flops=2_400_000_000, bytes_accessed=24 << 20, transcendentals=200_000),
         name="attend",
     )(
@@ -311,6 +318,7 @@
         cost_estimate=pl.CostEstimate(flops=0, bytes_accessed=2 << 20, transcendentals=0),
         name="close",
     )(near[0], *got, other, pick)
+    arrival_cache, slots = lax.optimization_barrier((arrival_cache, slots))
     rows = lax.all_to_all(
         slots.reshape(INST, STEPS * CAP, share), "inst", split_axis=0, concat_axis=0, tiled=True
     )

time: 169 us -> 91.8 us (0.54)
  Pallas kernels: 64.4 us -> 22.9 us
  waiting for transfers between devices: 59.9 us -> 36.9 us
  blocking collectives: 16.7 us -> 0 us
  starting transfers between devices: 12.7 us -> 23.7 us
  local copies, waits for them, and re-layouts: 13.4 us -> 6.55 us
    pallas_call x1, Pallas kernels: 50.5 us -> 4.84 us  [local(): pl.pallas_call(pack_kernel, out_shape=(jax.ShapeDtypeStruct((INST * CAP,)...]
    all_to_all x1, waiting for transfers between devices: 39 us -> 0.01 us  [local(): lax.all_to_all(send, 'inst', split_axis=0, concat_axis=0, tiled=True)]
    all_to_all x1 -> x0, blocking collectives: 16.7 us -> none  [local(): lax.all_to_all(slots.reshape(INST, STEPS * CAP, share), 'inst', split_axi...]
    all_to_all x0 -> x1, waiting for transfers between devices: none -> 8.68 us  [local(): lax.all_to_all(slots.reshape(INST, STEPS * CAP, share), 'inst', split_axi...]
    all_to_all x0 -> x1, starting transfers between devices: none -> 8.51 us  [local(): lax.all_to_all(slots.reshape(INST, STEPS * CAP, share), 'inst', split_axi...]
    unnamed x24 -> x4, local copies, waits for them, and re-layouts: 10.5 us -> 3.13 us
    ppermute x1, waiting for transfers between devices: 0.01 us -> 6.68 us  [local(): lax.ppermute(part, 'tp', [(s, (s + RING) % (2 * RING)) for s in range(2 *...]
    pallas_call x1, Pallas kernels: 8.84 us -> 13 us  [local(): pl.pallas_call(attend_kernel, out_shape=(near_shape,) * RING, in_specs=[S...]
  transfers between devices with their start and end apart: 5 -> 6, of which waited for: 3 -> 5; matrix products, arithmetic and copies ran while one was open for 2% -> 1% of each run, Pallas kernels for 30% -> 20%
where the time goes in v2:
time: 91.8 us; the launch traced here: 91.3 us
  waiting for transfers between devices  36.9 us (40%)
  starting transfers between devices  23.7 us (26%)
  Pallas kernels  22.9 us (25%)
  local copies, waits for them, and re-layouts  6.55 us (7%)
    ppermute x3, waiting for transfers between devices, local(): got = [lax.ppermute(near[k], 'tp', shift(k)) for k in (2, 1, 3)]  21.6 us
    pallas_call x1, Pallas kernels, local(): pl.pallas_call(attend_kernel, out_shape=(near_shape,) * RING, in_specs=[S...  13 us
    all_to_all x1, waiting for transfers between devices, local(): lax.all_to_all(slots.reshape(INST, STEPS * CAP, share), 'inst', split_axi...  8.68 us
    all_to_all x1, starting transfers between devices, local(): lax.all_to_all(slots.reshape(INST, STEPS * CAP, share), 'inst', split_axi...  8.51 us
    all_to_all x1, starting transfers between devices, local(): lax.all_to_all(send, 'inst', split_axis=0, concat_axis=0, tiled=True)  8.46 us
    ppermute x1, waiting for transfers between devices, local(): lax.ppermute(part, 'tp', [(s, (s + RING) % (2 * RING)) for s in range(2 *...  6.68 us
    ppermute x3, starting transfers between devices, local(): got = [lax.ppermute(near[k], 'tp', shift(k)) for k in (2, 1, 3)]  6.35 us
    pallas_call x1, Pallas kernels, local(): pl.pallas_call(pack_kernel, out_shape=(jax.ShapeDtypeStruct((INST * CAP,)...  4.84 us
  transfers between devices with their start and end apart: 6, of which 5 were waited for; matrix products, arithmetic and copies ran while one was open for 1% of the time, Pallas kernels for 20%

profile of v2, /device:TPU:1, one launch (start us, length us, event | category | flops | bytes accessed | tf_op | source)
XLA Modules:
  0.0 91.3 jit_solution(5895428739603411684)
XLA Ops:
  0.6 0.8 copy.16
  1.4 0.7 reshape.33.table
  2.1 4.8 %pack_pages.1 = (bf16[32,3,2,64,128]{4,3,2,1,0:T(8,128)(2,1)}, bf16[256,128]{1,0:T(8,128)(2,1)}) custom-call(s32[96]{0:T(128)} %reshape.33.table, s32[16]{0:T(128)} %mreq.1, s32[16]{0:T(128)} %bitcast.16, s32[16]{0:T(128)} %resume.1, bf16[96,2,64,128]{3,2,1,0:T(8,128)(2,1)} %pool.3), custom_call_target="tpu_custom_call" | custom-call | bytes 6291456 | tf_op jit(solution)/shard_map/pack_pages/pallas_call | solution.py:238
  6.9 8.5 %all-to-all-start = ((bf16[32,3,2,64,128]{4,3,2,1,0:T(8,128)(2,1)}), bf16[32,3,2,64,128]{4,3,2,1,0:T(8,128)(2,1)S(1)}, u32[]{:S(2)}, u32[]{:S(2)}) async-start(bf16[32,3,2,64,128]{4,3,2,1,0:T(8,128)(2,1)} %get-tuple-element.19), calls=%async_computation | async-start | bytes 6291456 | tf_op jit(solution)/shard_map/all_to_all | solution.py:259
  15.4 0.6 pad_add_fusion.where
  15.9 13.0 %attend.1 = (bf16[2,128,1024]{2,1,0:T(8,128)(2,1)}, bf16[2,128,1024]{2,1,0:T(8,128)(2,1)}, bf16[2,128,1024]{2,1,0:T(8,128)(2,1)}, bf16[2,128,1024]{2,1,0:T(8,128)(2,1)}) custom-call(s32[2]{0:T(128)} %pad_add_fusion.where, s32[32]{0:T(128)} %lengths.1, s32[96]{0:T(128)} %reshape.33.table, s32[1,32]{1,0:T(1,128)} %bitcast.15, f32[1,128]{1,0:T(1,128)} %constant.32.clone.freq, ...), custom_call_target="tpu_custom_call" | custom-call | flops 2400000000 | bytes 25165824 | tf_op jit(solution)/shard_map/attend/pallas_call | solution.py:268
  28.9 3.7 %collective-permute-start = (bf16[2,128,1024]{2,1,0:T(8,128)(2,1)}, bf16[2,128,1024]{2,1,0:T(8,128)(2,1)}, u32[]{:S(2)}, u32[]{:S(2)}) collective-permute-start(bf16[2,128,1024]{2,1,0:T(8,128)(2,1)} %get-tuple-element.14), channel_id=1, source_target_pairs={{0,2},{1,3},{2,0},{3,1},{4,6},{5,7},{6,4},{7,5},{8,10},{9,11},{10,... | collective-permute-start | bytes 1572872 | tf_op jit(solution)/shard_map/ppermute | solution.py:303
  32.6 0.7 collective-permute-start.1
  33.3 1.9 %collective-permute-start.2 = (bf16[2,128,1024]{2,1,0:T(8,128)(2,1)}, bf16[2,128,1024]{2,1,0:T(8,128)(2,1)}, u32[]{:S(2)}, u32[]{:S(2)}) collective-permute-start(bf16[2,128,1024]{2,1,0:T(8,128)(2,1)} %get-tuple-element.16), channel_id=1, source_target_pairs={{0,3},{1,0},{2,1},{3,2},{4,7},{5,4},{6,5},{7,6},{8,11},{9,8},{10,9... | collective-permute-start | bytes 1572872 | tf_op jit(solution)/shard_map/ppermute | solution.py:303
  35.3 9.9 %collective-permute-done.a = bf16[2,128,1024]{2,1,0:T(8,128)(2,1)} collective-permute-done((bf16[2,128,1024]{2,1,0:T(8,128)(2,1)}, bf16[2,128,1024]{2,1,0:T(8,128)(2,1)}, u32[]{:S(2)}, u32[]{:S(2)}) %collective-permute-start) | collective-permute-done | bytes 524320 | tf_op jit(solution)/shard_map/ppermute | solution.py:303
  45.1 11.4 %collective-permute-done.1.b = bf16[2,128,1024]{2,1,0:T(8,128)(2,1)} collective-permute-done((bf16[2,128,1024]{2,1,0:T(8,128)(2,1)}, bf16[2,128,1024]{2,1,0:T(8,128)(2,1)}, u32[]{:S(2)}, u32[]{:S(2)}) %collective-permute-start.1) | collective-permute-done | bytes 524320 | tf_op jit(solution)/shard_map/ppermute | solution.py:303
  56.5 0.3 collective-permute-done.2.c
  56.8 2.3 %sum_ring.1 = bf16[128,1024]{1,0:T(8,128)(2,1)} custom-call(bf16[2,128,1024]{2,1,0:T(8,128)(2,1)} %get-tuple-element.13.own, bf16[2,128,1024]{2,1,0:T(8,128)(2,1)} %collective-permute-done.a, bf16[2,128,1024]{2,1,0:T(8,128)(2,1)} %collective-permute-done.1.b, bf16[2,128,1024]{2,1,0:T(8,128)(2,1)} %collective-permute-done.2.c), custom_call_target="tpu_custom_call" | custom-call | bytes 2097152 | tf_op jit(solution)/shard_map/sum_ring/pallas_call | solution.py:304
  59.2 0.4 collective-permute-start.3
  59.6 6.7 %collective-permute-done.3.other = bf16[128,1024]{1,0:T(8,128)(2,1)S(1)} collective-permute-done((bf16[128,1024]{1,0:T(8,128)(2,1)}, bf16[128,1024]{1,0:T(8,128)(2,1)S(1)}, u32[]{:S(2)}, u32[]{:S(2)}) %collective-permute-start.3) | collective-permute-done | bytes 262176 | tf_op jit(solution)/shard_map/ppermute | solution.py:312
  66.3 0.0 copy-start
  66.3 0.7 copy-done
  67.0 2.7 %close.1 = (bf16[128,1024]{1,0:T(8,128)(2,1)}, bf16[128,1024]{1,0:T(8,128)(2,1)}) custom-call(bf16[2,128,1024]{2,1,0:T(8,128)(2,1)} %get-tuple-element.13.own, bf16[2,128,1024]{2,1,0:T(8,128)(2,1)} %collective-permute-done.a, bf16[2,128,1024]{2,1,0:T(8,128)(2,1)} %collective-permute-done.1.b, bf16[2,128,1024]{2,1,0:T(8,128)(2,1)} %collective-permute-done.2.c, ...), custom_call_target="tpu_custom_call" | custom-call | bytes 2097152 | tf_op jit(solution)/shard_map/close/pallas_call | solution.py:313
  69.7 0.0 all-to-all-done
  69.7 8.5 %all-to-all-start.1 = ((bf16[16,8,1024]{2,1,0:T(8,128)(2,1)}), bf16[16,8,1024]{2,1,0:T(8,128)(2,1)S(1)}, u32[]{:S(2)}, u32[]{:S(2)}) async-start(bf16[16,8,1024]{2,1,0:T(8,128)(2,1)} %bitcast.13), calls=%async_computation.1 | async-start | bytes 524288 | tf_op jit(solution)/shard_map/all_to_all | solution.py:322
  78.2 8.7 %all-to-all-done.1 = bf16[16,8,1024]{2,1,0:T(8,128)(2,1)S(1)} async-done(((bf16[16,8,1024]{2,1,0:T(8,128)(2,1)}), bf16[16,8,1024]{2,1,0:T(8,128)(2,1)S(1)}, u32[]{:S(2)}, u32[]{:S(2)}) %all-to-all-start.1) | async-done | bytes 262176 | tf_op jit(solution)/shard_map/all_to_all | solution.py:322
  86.9 0.8 reshape.40
  87.7 1.1 %copy.19 = bf16[16,4,2,1024]{3,2,0,1:T(2,128)(2,1)S(1)} copy(bf16[16,4,2,1024]{3,2,1,0:T(2,128)(2,1)} %reshape.40) | data formatting | bytes 524288 | tf_op jit(solution)/shard_map/reshape | solution.py:325
  88.8 0.8 reshape.41
  89.6 1.7 %copy.21 = bf16[32,3,2,64,128]{4,3,2,1,0:T(8,128)(2,1)} copy(bf16[32,3,2,64,128]{4,3,2,1,0:T(8,128)(2,1)S(1)} %all-to-all-done) | data formatting | bytes 6291456
Async XLA Ops:
  6.9 62.8 %all-to-all-start = ((bf16[32,3,2,64,128]{4,3,2,1,0:T(8,128)(2,1)}), bf16[32,3,2,64,128]{4,3,2,1,0:T(8,128)(2,1)S(1)}, u32[]{:S(2)}, u32[]{:S(2)}) async-start(bf16[32,3,2,64,128]{4,3,2,1,0:T(8,128)(2,1)} %get-tuple-element.19), calls=%async_computation | async-start | bytes 6291456 | tf_op jit(solution)/shard_map/all_to_all | solution.py:259
  28.9 16.2 %collective-permute-start = (bf16[2,128,1024]{2,1,0:T(8,128)(2,1)}, bf16[2,128,1024]{2,1,0:T(8,128)(2,1)}, u32[]{:S(2)}, u32[]{:S(2)}) collective-permute-start(bf16[2,128,1024]{2,1,0:T(8,128)(2,1)} %get-tuple-element.14), channel_id=1, source_target_pairs={{0,2},{1,3},{2,0},{3,1},{4,6},{5,7},{6,4},{7,5},{8,10},{9,11},{10,... | collective-permute-start | bytes 1572872 | tf_op jit(solution)/shard_map/ppermute | solution.py:303
  32.6 23.9 %collective-permute-start.1 = (bf16[2,128,1024]{2,1,0:T(8,128)(2,1)}, bf16[2,128,1024]{2,1,0:T(8,128)(2,1)}, u32[]{:S(2)}, u32[]{:S(2)}) collective-permute-start(bf16[2,128,1024]{2,1,0:T(8,128)(2,1)} %get-tuple-element.15), channel_id=1, source_target_pairs={{0,1},{1,2},{2,3},{3,0},{4,5},{5,6},{6,7},{7,4},{8,9},{9,10},{10,1... | collective-permute-start | bytes 1572872 | tf_op jit(solution)/shard_map/ppermute | solution.py:303
  33.3 23.5 %collective-permute-start.2 = (bf16[2,128,1024]{2,1,0:T(8,128)(2,1)}, bf16[2,128,1024]{2,1,0:T(8,128)(2,1)}, u32[]{:S(2)}, u32[]{:S(2)}) collective-permute-start(bf16[2,128,1024]{2,1,0:T(8,128)(2,1)} %get-tuple-element.16), channel_id=1, source_target_pairs={{0,3},{1,0},{2,1},{3,2},{4,7},{5,4},{6,5},{7,6},{8,11},{9,8},{10,9... | collective-permute-start | bytes 1572872 | tf_op jit(solution)/shard_map/ppermute | solution.py:303
  59.2 7.1 %collective-permute-start.3 = (bf16[128,1024]{1,0:T(8,128)(2,1)}, bf16[128,1024]{1,0:T(8,128)(2,1)S(1)}, u32[]{:S(2)}, u32[]{:S(2)}) collective-permute-start(bf16[128,1024]{1,0:T(8,128)(2,1)} %sum_ring.1), channel_id=1, source_target_pairs={{0,4},{1,5},{2,6},{3,7},{4,0},{5,1},{6,2},{7,3},{8,12},{9,13},{10,... | collective-permute-start | bytes 786440 | tf_op jit(solution)/shard_map/ppermute | solution.py:312
  66.3 0.7 copy-start
  69.7 17.2 %all-to-all-start.1 = ((bf16[16,8,1024]{2,1,0:T(8,128)(2,1)}), bf16[16,8,1024]{2,1,0:T(8,128)(2,1)S(1)}, u32[]{:S(2)}, u32[]{:S(2)}) async-start(bf16[16,8,1024]{2,1,0:T(8,128)(2,1)} %bitcast.13), calls=%async_computation.1 | async-start | bytes 524288 | tf_op jit(solution)/shard_map/all_to_all | solution.py:322

commit v3 on v2

--- a/solution.py
+++ b/solution.py
@@ -20,7 +20,8 @@
 ROWS = STEPS * REQS
 WIDE = 256
 ROPE_BASE = 500000.0
-VMEM_LIMIT = 58 << 20
+FULL_VMEM = 58 << 20
+SMALL_VMEM = 6 << 20
 F32 = jnp.float32
 BF16 = jnp.bfloat16
 SMEM = pl.BlockSpec(memory_space=pltpu.SMEM)
@@ -60,7 +61,7 @@
         @pl.when(req >= 0)
         def _():
             for p in range(MAXP):
-                pltpu.make_async_copy(kv.at[table[req * MAXP + p]], send.at[s, p], sem).start()
+                pltpu.make_async_copy(kv.at[table[p, req]], send.at[s, p], sem).start()
 
         @pl.when(req < 0)
         def _():
@@ -101,14 +102,15 @@
 
 
 def attend_kernel(
-    where, lengths, table, len_row, freq, hidden, wq, wo, pool, new_kv,
+    lengths, table, len_row, freq, hidden, wq, wo, pool, new_kv,
     near0, near1, near2, near3,
     x, q_w, o_w, kv, fresh, turned, scores, probs, mixed, outs, acc, x_sem, q_sem, o_sem, kv_sem, out_sem,
 ):
     chunks = x_sem.shape[0]
     depth = x.shape[1] // chunks
     share = outs.shape[-1]
-    y, z = where[0], where[1]
+    tp = lax.axis_index("tp")
+    y, z = tp // RING, tp % RING
 
     def load(k):
         cut = pl.ds(k * depth, depth)
@@ -121,7 +123,6 @@
         for copy in load(k):
             copy.start()
     kv_copy = pltpu.make_async_copy(pool, kv, kv_sem)
-    kv_copy.start()
     order = [(k, j) for k in (2, 1, 3, 0) for j in (1, 0)]
 
     def weight(i):
@@ -129,9 +130,6 @@
         n = lax.rem(y + j, 2) * RING + lax.rem(z + k, RING)
         cut = pl.ds(pl.multiple_of(n * share, share), share)
         return pltpu.make_async_copy(wo.at[:, cut], o_w.at[i], o_sem.at[i])
-
-    for i in range(len(order)):
-        weight(i).start()
 
     row = lax.broadcasted_iota(jnp.int32, (REQS * 16, ROWS * 2), 0)
     col = lax.broadcasted_iota(jnp.int32, (REQS * 16, ROWS * 2), 1)
@@ -156,6 +154,11 @@
     for k in range(chunks):
         for copy in load(k):
             copy.wait()
+        if k == 2:
+            kv_copy.start()
+        if k >= 4:
+            for i in (2 * k - 8, 2 * k - 7):
+                weight(i).start()
         cut = pl.ds(k * depth, depth)
         part = jnp.dot(x[:, cut], q_w[cut], preferred_element_type=F32)
         if k == 0:
@@ -175,7 +178,7 @@
     rest = jnp.zeros((WIDE - SPAN - 16, HD), BF16)
 
     def pages(r, j):
-        cached = [kv[table[r * MAXP + p], j] for p in range(MAXP)]
+        cached = [kv[table[p, r], j] for p in range(MAXP)]
         return jnp.concatenate(cached + [fresh[j, r * 16:(r + 1) * 16], rest], axis=0)
 
     for r in range(REQS):
@@ -228,13 +231,25 @@
     slots[...] = both[ROWS:]
 
 
+def arrive_kernel(rows, out):
+    to = lax.broadcasted_iota(jnp.int32, (ROWS, ROWS), 0)
+    come = lax.broadcasted_iota(jnp.int32, (ROWS, ROWS), 1)
+    t, s, c = to // (INST * CAP), (to // CAP) % INST, to % CAP
+    turn = jnp.where(come == s * (STEPS * CAP) + t * CAP + c, 1.0, 0.0).astype(BF16)
+    out[...] = jnp.dot(turn, rows[...], preferred_element_type=F32).astype(BF16)
+
+
+def copy_kernel(got, out):
+    out[...] = got[...]
+
+
 def local(
     hidden, query_weight, output_weight, kv_pool, new_kv,
     lengths, page_table, mig_req, mig_dest, resume,
 ):
     width = hidden.shape[-1]
     share = width // lax.axis_size("tp")
-    table = page_table.reshape(-1)
+    table = page_table.T
     send, pick = pl.pallas_call(
         pack_kernel,
         out_shape=(
@@ -252,14 +267,12 @@
             pltpu.SemaphoreType.DMA,
             pltpu.SemaphoreType.DMA,
         ],
-        compiler_params=pltpu.CompilerParams(vmem_limit_bytes=VMEM_LIMIT),
+        compiler_params=pltpu.CompilerParams(vmem_limit_bytes=FULL_VMEM),
         cost_estimate=pl.CostEstimate(flops=0, bytes_accessed=6 << 20, transcendentals=0),
         name="pack_pages",
     )(table, mig_req, mig_dest.reshape(-1), resume, kv_pool)
     arrival_cache = lax.all_to_all(send, "inst", split_axis=0, concat_axis=0, tiled=True)
 
-    tp = lax.axis_index("tp")
-    where = jnp.stack([tp // RING, tp % RING]).astype(jnp.int32)
     half = HD // 2
     inverse = np.float32(ROPE_BASE) ** (-np.arange(half, dtype=np.float32) * np.float32(2.0) / np.float32(HD))
     freq = jnp.asarray(np.concatenate([inverse, inverse])[None, :].astype(np.float32))
@@ -268,7 +281,7 @@
     near = pl.pallas_call(
         attend_kernel,
         out_shape=(near_shape,) * RING,
-        in_specs=[SMEM, SMEM, SMEM, VMEM, VMEM, ANY, ANY, ANY, ANY, VMEM],
+        in_specs=[SMEM, SMEM, VMEM, VMEM, ANY, ANY, ANY, ANY, VMEM],
         out_specs=(ANY,) * RING,
         scratch_shapes=[
             pltpu.VMEM((ROWS, width), BF16),
@@ -288,11 +301,11 @@
             pltpu.SemaphoreType.DMA,
             pltpu.SemaphoreType.DMA((2 * RING,)),
         ],
-        compiler_params=pltpu.CompilerParams(vmem_limit_bytes=VMEM_LIMIT),
+        compiler_params=pltpu.CompilerParams(vmem_limit_bytes=FULL_VMEM),
         cost_estimate=pl.CostEstimate(flops=2_400_000_000, bytes_accessed=24 << 20, transcendentals=200_000),
         name="attend",
     )(
-        where, lengths, table, lengths.reshape(1, REQS), freq,
+        lengths, table, lengths.reshape(1, REQS), freq,
         hidden.reshape(ROWS, width), query_weight, output_weight, kv_pool,
         new_kv.reshape(2 * ROWS, HD),
     )
@@ -306,6 +319,7 @@
         out_shape=jax.ShapeDtypeStruct((ROWS, share), BF16),
         in_specs=[VMEM] * 4,
         out_specs=VMEM,
+        compiler_params=pltpu.CompilerParams(vmem_limit_bytes=SMALL_VMEM),
         cost_estimate=pl.CostEstimate(flops=0, bytes_accessed=2 << 20, transcendentals=0),
         name="sum_ring",
     )(near[0], *got)
@@ -315,6 +329,7 @@
         out_shape=(jax.ShapeDtypeStruct((ROWS, share), BF16),) * 2,
         in_specs=[VMEM] * 6,
         out_specs=(VMEM,) * 2,
+        compiler_params=pltpu.CompilerParams(vmem_limit_bytes=SMALL_VMEM),
         cost_estimate=pl.CostEstimate(flops=0, bytes_accessed=2 << 20, transcendentals=0),
         name="close",
     )(near[0], *got, other, pick)
@@ -322,7 +337,25 @@
     rows = lax.all_to_all(
         slots.reshape(INST, STEPS * CAP, share), "inst", split_axis=0, concat_axis=0, tiled=True
     )
-    arrival = jnp.transpose(rows.reshape(INST, STEPS, CAP, share), (1, 0, 2, 3))
+    arrival = pl.pallas_call(
+        arrive_kernel,
+        out_shape=jax.ShapeDtypeStruct((ROWS, share), BF16),
+        in_specs=[VMEM],
+        out_specs=VMEM,
+        compiler_params=pltpu.CompilerParams(vmem_limit_bytes=SMALL_VMEM),
+        name="arrive",
+    )(rows.reshape(ROWS, share))
+    block = pl.BlockSpec((4,) + arrival_cache.shape[1:], lambda i: (i, 0, 0, 0, 0))
+    arrival_cache = pl.pallas_call(
+        copy_kernel,
+        out_shape=jax.ShapeDtypeStruct(arrival_cache.shape, BF16),
+        grid=(INST * CAP // 4,),
+        in_specs=[block],
+        out_specs=block,
+        compiler_params=pltpu.CompilerParams(vmem_limit_bytes=SMALL_VMEM),
+        cost_estimate=pl.CostEstimate(flops=0, bytes_accessed=6 << 20, transcendentals=0),
+        name="keep_pages",
+    )(arrival_cache)
     return (
         home.reshape(STEPS, REQS, share),
         arrival.reshape(STEPS, INST * CAP, share),

time: 91.8 us -> 81.3 us (0.89)
  local copies, waits for them, and re-layouts: 6.55 us -> 1.75 us
  waiting for transfers between devices: 36.9 us -> 33.6 us
  Pallas kernels: 22.9 us -> 21.3 us
    pallas_call x0 -> x2, Pallas kernels: none -> 4.15 us  [the longest x1 3.23 us: local(): pl.pallas_call(copy_kernel, out_shape=jax.ShapeDtypeStruct(arrival_cache....]
    reshape x4 -> x0, local copies, waits for them, and re-layouts: 3.42 us -> none  [the longest x2 1.93 us: local(): arrival = jnp.transpose(rows.reshape(INST, STEPS, CAP, share), (1, 0, 2, 3))]
    all_to_all x1, waiting for transfers between devices: 8.68 us -> 5.45 us  [local(): lax.all_to_all(slots.reshape(INST, STEPS * CAP, share), 'inst', split_axi...]
    pallas_call x1, Pallas kernels: 2.35 us -> 0.13 us  [local(): pl.pallas_call(sum_kernel, out_shape=jax.ShapeDtypeStruct((ROWS, share),...]
    pallas_call x1, Pallas kernels: 13 us -> 11.1 us  [local(): pl.pallas_call(attend_kernel, out_shape=(near_shape,) * RING, in_specs=[S...]
    pallas_call x1, Pallas kernels: 2.71 us -> 1.05 us  [local(): pl.pallas_call(close_kernel, out_shape=(jax.ShapeDtypeStruct((ROWS, share...]
    unnamed x4 -> x6, local copies, waits for them, and re-layouts: 3.13 us -> 1.75 us
  transfers between devices with their start and end apart: 6 -> 6, of which waited for: 5 -> 5; matrix products, arithmetic and copies ran while one was open for 1% -> 0% of each run, Pallas kernels for 20% -> 19%
where the time goes in v3:
time: 81.3 us; the launch traced here: 80.9 us
  waiting for transfers between devices  33.6 us (41%)
  starting transfers between devices  23.6 us (29%)
  Pallas kernels  21.3 us (26%)
  local copies, waits for them, and re-layouts  1.75 us (2%)
    ppermute x3, waiting for transfers between devices, local(): got = [lax.ppermute(near[k], 'tp', shift(k)) for k in (2, 1, 3)]  21.6 us
    pallas_call x1, Pallas kernels, local(): pl.pallas_call(attend_kernel, out_shape=(near_shape,) * RING, in_specs=[S...  11.1 us
    all_to_all x1, starting transfers between devices, local(): lax.all_to_all(send, 'inst', split_axis=0, concat_axis=0, tiled=True)  8.46 us
    all_to_all x1, starting transfers between devices, local(): lax.all_to_all(slots.reshape(INST, STEPS * CAP, share), 'inst', split_axi...  8.3 us
    ppermute x1, waiting for transfers between devices, local(): lax.ppermute(part, 'tp', [(s, (s + RING) % (2 * RING)) for s in range(2 *...  6.55 us
    ppermute x3, starting transfers between devices, local(): got = [lax.ppermute(near[k], 'tp', shift(k)) for k in (2, 1, 3)]  6.37 us
    all_to_all x1, waiting for transfers between devices, local(): lax.all_to_all(slots.reshape(INST, STEPS * CAP, share), 'inst', split_axi...  5.45 us
    pallas_call x1, Pallas kernels, local(): pl.pallas_call(pack_kernel, out_shape=(jax.ShapeDtypeStruct((INST * CAP,)...  4.88 us
  transfers between devices with their start and end apart: 6, of which 5 were waited for; matrix products, arithmetic and copies ran while one was open for 0% of the time, Pallas kernels for 19%

profile of v3, /device:TPU:1, one launch (start us, length us, event | category | flops | bytes accessed | tf_op | source)
XLA Modules:
  0.0 80.9 jit_solution(8484069242367651519)
XLA Ops:
  0.6 4.9 %pack_pages.1 = (bf16[32,3,2,64,128]{4,3,2,1,0:T(8,128)(2,1)}, bf16[256,128]{1,0:T(8,128)(2,1)}) custom-call(s32[3,32]{1,0:T(4,128)} %bitcast.14, s32[16]{0:T(128)} %mreq.1, s32[16]{0:T(128)} %bitcast.17, s32[16]{0:T(128)} %resume.1, bf16[96,2,64,128]{3,2,1,0:T(8,128)(2,1)} %pool.3), custom_call_target="tpu_custom_call" | custom-call | bytes 6291456 | tf_op jit(solution)/shard_map/pack_pages/pallas_call | solution.py:253
  5.5 8.5 %all-to-all-start = ((bf16[32,3,2,64,128]{4,3,2,1,0:T(8,128)(2,1)}), bf16[32,3,2,64,128]{4,3,2,1,0:T(8,128)(2,1)S(1)}, u32[]{:S(2)}, u32[]{:S(2)}) async-start(bf16[32,3,2,64,128]{4,3,2,1,0:T(8,128)(2,1)} %get-tuple-element.19), calls=%async_computation | async-start | bytes 6291456 | tf_op jit(solution)/shard_map/all_to_all | solution.py:274
  14.0 0.0 copy-start.2
  14.0 11.1 %attend.1 = (bf16[2,128,1024]{2,1,0:T(8,128)(2,1)}, bf16[2,128,1024]{2,1,0:T(8,128)(2,1)}, bf16[2,128,1024]{2,1,0:T(8,128)(2,1)}, bf16[2,128,1024]{2,1,0:T(8,128)(2,1)}) custom-call(s32[32]{0:T(128)} %lengths.1, s32[3,32]{1,0:T(4,128)} %bitcast.15, s32[1,32]{1,0:T(1,128)} %bitcast.16, f32[1,128]{1,0:T(1,128)} %constant.2.clone.freq, ...), custom_call_target="tpu_custom_call" | custom-call | flops 2400000000 | bytes 25165824 | tf_op jit(solution)/shard_map/attend/pallas_call | solution.py:281
  25.1 3.7 %collective-permute-start = (bf16[2,128,1024]{2,1,0:T(8,128)(2,1)}, bf16[2,128,1024]{2,1,0:T(8,128)(2,1)S(1)}, u32[]{:S(2)}, u32[]{:S(2)}) collective-permute-start(bf16[2,128,1024]{2,1,0:T(8,128)(2,1)} %get-tuple-element.14), channel_id=1, source_target_pairs={{0,2},{1,3},{2,0},{3,1},{4,6},{5,7},{6,4},{7,5},{8,10},{9,11},{10,... | collective-permute-start | bytes 1572872 | tf_op jit(solution)/shard_map/ppermute | solution.py:316
  28.8 0.7 collective-permute-start.1
  29.5 1.9 %collective-permute-start.2 = (bf16[2,128,1024]{2,1,0:T(8,128)(2,1)}, bf16[2,128,1024]{2,1,0:T(8,128)(2,1)S(1)}, u32[]{:S(2)}, u32[]{:S(2)}) collective-permute-start(bf16[2,128,1024]{2,1,0:T(8,128)(2,1)} %get-tuple-element.16), channel_id=1, source_target_pairs={{0,3},{1,0},{2,1},{3,2},{4,7},{5,4},{6,5},{7,6},{8,11},{9,8},{10,9... | collective-permute-start | bytes 1572872 | tf_op jit(solution)/shard_map/ppermute | solution.py:316
  31.4 9.8 %collective-permute-done.a = bf16[2,128,1024]{2,1,0:T(8,128)(2,1)S(1)} collective-permute-done((bf16[2,128,1024]{2,1,0:T(8,128)(2,1)}, bf16[2,128,1024]{2,1,0:T(8,128)(2,1)S(1)}, u32[]{:S(2)}, u32[]{:S(2)}) %collective-permute-start) | collective-permute-done | bytes 524320 | tf_op jit(solution)/shard_map/ppermute | solution.py:316
  41.2 11.4 %collective-permute-done.1.b = bf16[2,128,1024]{2,1,0:T(8,128)(2,1)S(1)} collective-permute-done((bf16[2,128,1024]{2,1,0:T(8,128)(2,1)}, bf16[2,128,1024]{2,1,0:T(8,128)(2,1)S(1)}, u32[]{:S(2)}, u32[]{:S(2)}) %collective-permute-start.1) | collective-permute-done | bytes 524320 | tf_op jit(solution)/shard_map/ppermute | solution.py:316
  52.6 0.4 collective-permute-done.2.c
  53.0 0.0 copy-start
  53.0 1.0 %copy-done = bf16[2,128,1024]{2,1,0:T(8,128)(2,1)S(1)} copy-done((bf16[2,128,1024]{2,1,0:T(8,128)(2,1)S(1)}, bf16[2,128,1024]{2,1,0:T(8,128)(2,1)}, u32[]{:S(2)}) %copy-start) | copy-done | bytes 524312
  54.0 0.1 sum_ring.1
  54.2 0.5 collective-permute-start.3
  54.6 6.6 %collective-permute-done.3.other = bf16[128,1024]{1,0:T(8,128)(2,1)S(1)} collective-permute-done((bf16[128,1024]{1,0:T(8,128)(2,1)S(1)}, bf16[128,1024]{1,0:T(8,128)(2,1)S(1)}, u32[]{:S(2)}, u32[]{:S(2)}) %collective-permute-start.3) | collective-permute-done | bytes 262176 | tf_op jit(solution)/shard_map/ppermute | solution.py:326
  61.2 0.0 copy-done.2
  61.2 1.0 %close.1 = (bf16[128,1024]{1,0:T(8,128)(2,1)}, bf16[128,1024]{1,0:T(8,128)(2,1)S(1)}) custom-call(bf16[2,128,1024]{2,1,0:T(8,128)(2,1)S(1)} %copy-done, bf16[2,128,1024]{2,1,0:T(8,128)(2,1)S(1)} %collective-permute-done.a, bf16[2,128,1024]{2,1,0:T(8,128)(2,1)S(1)} %collective-permute-done.1.b, bf16[2,128,1024]{2,1,0:T(8,128)(2,1)S(1)} %collective-permute-done.2.c, ...), custom_call_target="tpu_custom_call" | custom-call | bytes 2097152 | tf_op jit(solution)/shard_map/close/pallas_call | solution.py:327
  62.2 0.0 copy-start.1
  62.2 0.7 copy-done.1
  63.0 0.0 all-to-all-done.got
  63.0 8.3 %all-to-all-start.1 = ((bf16[16,8,1024]{2,1,0:T(8,128)(2,1)}), bf16[16,8,1024]{2,1,0:T(8,128)(2,1)S(1)}, u32[]{:S(2)}, u32[]{:S(2)}) async-start(bf16[16,8,1024]{2,1,0:T(8,128)(2,1)} %bitcast.10), calls=%async_computation.1 | async-start | bytes 524288 | tf_op jit(solution)/shard_map/all_to_all | solution.py:337
  71.3 3.2 %keep_pages.1 = bf16[32,3,2,64,128]{4,3,2,1,0:T(8,128)(2,1)} custom-call(bf16[32,3,2,64,128]{4,3,2,1,0:T(8,128)(2,1)S(1)} %all-to-all-done.got), custom_call_target="tpu_custom_call" | custom-call | bytes 6291456 | tf_op jit(solution)/shard_map/keep_pages/pallas_call | solution.py:349
  74.5 5.4 %all-to-all-done.1 = bf16[16,8,1024]{2,1,0:T(8,128)(2,1)S(1)} async-done(((bf16[16,8,1024]{2,1,0:T(8,128)(2,1)}), bf16[16,8,1024]{2,1,0:T(8,128)(2,1)S(1)}, u32[]{:S(2)}, u32[]{:S(2)}) %all-to-all-start.1) | async-done | bytes 262176 | tf_op jit(solution)/shard_map/all_to_all | solution.py:337
  79.9 0.9 %arrive.1 = bf16[128,1024]{1,0:T(8,128)(2,1)} custom-call(bf16[128,1024]{1,0:T(8,128)(2,1)S(1)} %bitcast.9), custom_call_target="tpu_custom_call" | custom-call | tf_op jit(solution)/shard_map/arrive/pallas_call | solution.py:340
Async XLA Ops:
  5.5 57.4 %all-to-all-start = ((bf16[32,3,2,64,128]{4,3,2,1,0:T(8,128)(2,1)}), bf16[32,3,2,64,128]{4,3,2,1,0:T(8,128)(2,1)S(1)}, u32[]{:S(2)}, u32[]{:S(2)}) async-start(bf16[32,3,2,64,128]{4,3,2,1,0:T(8,128)(2,1)} %get-tuple-element.19), calls=%async_computation | async-start | bytes 6291456 | tf_op jit(solution)/shard_map/all_to_all | solution.py:274
  14.0 47.2 %copy-start.2 = (bf16[256,128]{1,0:T(8,128)(2,1)S(1)}, bf16[256,128]{1,0:T(8,128)(2,1)}, u32[]{:S(2)}) copy-start(bf16[256,128]{1,0:T(8,128)(2,1)} %get-tuple-element.17.pick) | copy-start | bytes 196612
  25.1 16.1 %collective-permute-start = (bf16[2,128,1024]{2,1,0:T(8,128)(2,1)}, bf16[2,128,1024]{2,1,0:T(8,128)(2,1)S(1)}, u32[]{:S(2)}, u32[]{:S(2)}) collective-permute-start(bf16[2,128,1024]{2,1,0:T(8,128)(2,1)} %get-tuple-element.14), channel_id=1, source_target_pairs={{0,2},{1,3},{2,0},{3,1},{4,6},{5,7},{6,4},{7,5},{8,10},{9,11},{10,... | collective-permute-start | bytes 1572872 | tf_op jit(solution)/shard_map/ppermute | solution.py:316
  28.8 23.8 %collective-permute-start.1 = (bf16[2,128,1024]{2,1,0:T(8,128)(2,1)}, bf16[2,128,1024]{2,1,0:T(8,128)(2,1)S(1)}, u32[]{:S(2)}, u32[]{:S(2)}) collective-permute-start(bf16[2,128,1024]{2,1,0:T(8,128)(2,1)} %get-tuple-element.15), channel_id=1, source_target_pairs={{0,1},{1,2},{2,3},{3,0},{4,5},{5,6},{6,7},{7,4},{8,9},{9,10},{10,1... | collective-permute-start | bytes 1572872 | tf_op jit(solution)/shard_map/ppermute | solution.py:316
  29.5 23.5 %collective-permute-start.2 = (bf16[2,128,1024]{2,1,0:T(8,128)(2,1)}, bf16[2,128,1024]{2,1,0:T(8,128)(2,1)S(1)}, u32[]{:S(2)}, u32[]{:S(2)}) collective-permute-start(bf16[2,128,1024]{2,1,0:T(8,128)(2,1)} %get-tuple-element.16), channel_id=1, source_target_pairs={{0,3},{1,0},{2,1},{3,2},{4,7},{5,4},{6,5},{7,6},{8,11},{9,8},{10,9... | collective-permute-start | bytes 1572872 | tf_op jit(solution)/shard_map/ppermute | solution.py:316
  53.0 1.0 %copy-start = (bf16[2,128,1024]{2,1,0:T(8,128)(2,1)S(1)}, bf16[2,128,1024]{2,1,0:T(8,128)(2,1)}, u32[]{:S(2)}) copy-start(bf16[2,128,1024]{2,1,0:T(8,128)(2,1)} %get-tuple-element.13.own) | copy-start | bytes 1572868
  54.2 7.0 %collective-permute-start.3 = (bf16[128,1024]{1,0:T(8,128)(2,1)S(1)}, bf16[128,1024]{1,0:T(8,128)(2,1)S(1)}, u32[]{:S(2)}, u32[]{:S(2)}) collective-permute-start(bf16[128,1024]{1,0:T(8,128)(2,1)S(1)} %sum_ring.1), channel_id=1, source_target_pairs={{0,4},{1,5},{2,6},{3,7},{4,0},{5,1},{6,2},{7,3},{8,12},{9,13},{10,... | collective-permute-start | bytes 786440 | tf_op jit(solution)/shard_map/ppermute | solution.py:326
  62.2 0.7 copy-start.1
  63.0 17.0 %all-to-all-start.1 = ((bf16[16,8,1024]{2,1,0:T(8,128)(2,1)}), bf16[16,8,1024]{2,1,0:T(8,128)(2,1)S(1)}, u32[]{:S(2)}, u32[]{:S(2)}) async-start(bf16[16,8,1024]{2,1,0:T(8,128)(2,1)} %bitcast.10), calls=%async_computation.1 | async-start | bytes 524288 | tf_op jit(solution)/shard_map/all_to_all | solution.py:337

commit v4 on v3

--- a/solution.py
+++ b/solution.py
@@ -53,24 +53,6 @@
         return carry
 
     lax.fori_loop(0, MIG, place, 0)
-    load.wait()
-
-    def ship(s, carry):
-        req = slot_req[s]
-
-        @pl.when(req >= 0)
-        def _():
-            for p in range(MAXP):
-                pltpu.make_async_copy(kv.at[table[p, req]], send.at[s, p], sem).start()
-
-        @pl.when(req < 0)
-        def _():
-            pltpu.make_async_copy(zeros, send.at[s], sem).start()
-
-        return carry
-
-    lax.fori_loop(0, INST * CAP, ship, 0)
-
     rows = lax.broadcasted_iota(jnp.int32, (2 * ROWS, ROWS), 0)
     cols = lax.broadcasted_iota(jnp.int32, (2 * ROWS, ROWS), 1)
     wide[...] = jnp.where(rows == cols, 1.0, 0.0).astype(F32)
@@ -98,13 +80,33 @@
 
     lax.fori_loop(0, MIG, choose, 0)
     pick[...] = wide[...].astype(BF16)
+    load.wait()
+
+    def ship(s, carry):
+        req = slot_req[s]
+
+        @pl.when(req >= 0)
+        def _():
+            for p in range(MAXP):
+                pltpu.make_async_copy(kv.at[table[p, req]], send.at[s, p], sem).start()
+
+        @pl.when(req < 0)
+        def _():
+            pltpu.make_async_copy(zeros, send.at[s], sem).start()
+
+        return carry
+
+    lax.fori_loop(0, INST * CAP, ship, 0)
+
     pltpu.make_async_copy(send, send, sem).wait()
 
 
 def attend_kernel(
-    lengths, table, len_row, freq, hidden, wq, wo, pool, new_kv,
-    near0, near1, near2, near3,
-    x, q_w, o_w, kv, fresh, turned, scores, probs, mixed, outs, acc, x_sem, q_sem, o_sem, kv_sem, out_sem,
+    hidden, wq, wo, pool, new_kv, len_list, page_list, len_line, freq_line,
+    far1, far0, up0, down1, up1, down0, own,
+    x, q_w, o_w, kv, fresh, turned, scores, probs, mixed, outs, acc,
+    recent, lengths, table, len_row, freq,
+    x_sem, q_sem, o_sem, kv_sem, out_sem, small_sem,
 ):
     chunks = x_sem.shape[0]
     depth = x.shape[1] // chunks
@@ -119,11 +121,21 @@
             pltpu.make_async_copy(wq.at[cut], q_w.at[cut], q_sem.at[k]),
         )
 
+    small = [
+        pltpu.make_async_copy(source, target, small_sem.at[i])
+        for i, (source, target) in enumerate((
+            (new_kv, recent), (len_line, len_row), (freq_line, freq), (len_list, lengths), (page_list, table),
+        ))
+    ]
     for k in range(chunks):
         for copy in load(k):
             copy.start()
+        if k == 0:
+            for copy in small:
+                copy.start()
     kv_copy = pltpu.make_async_copy(pool, kv, kv_sem)
-    order = [(k, j) for k in (2, 1, 3, 0) for j in (1, 0)]
+    order = [(2, 1), (2, 0), (1, 0), (3, 1), (1, 1), (3, 0), (0, 1), (0, 0)]
+    into = (far1, far0, up0, down1, up1, down0, own.at[1], own.at[0])
 
     def weight(i):
         k, j = order[i]
@@ -131,20 +143,23 @@
         cut = pl.ds(pl.multiple_of(n * share, share), share)
         return pltpu.make_async_copy(wo.at[:, cut], o_w.at[i], o_sem.at[i])
 
+    for copy in small:
+        copy.wait()
+
     row = lax.broadcasted_iota(jnp.int32, (REQS * 16, ROWS * 2), 0)
     col = lax.broadcasted_iota(jnp.int32, (REQS * 16, ROWS * 2), 1)
-    home = (row % 16) * (2 * REQS) + (row // 16) * 2
-    source = new_kv[...]
+    home = (row & 15) * (2 * REQS) + (row >> 4) * 2
+    source = recent[...]
     for j in range(2):
-        choice = jnp.where((col == home + j) & (row % 16 < STEPS), 1.0, 0.0).astype(BF16)
+        choice = jnp.where((col == home + j) & ((row & 15) < STEPS), 1.0, 0.0).astype(BF16)
         fresh[j] = jnp.dot(choice, source, preferred_element_type=F32).astype(BF16)
 
     at = lax.broadcasted_iota(jnp.int32, (ROWS, REQS), 0)
     req = lax.broadcasted_iota(jnp.int32, (ROWS, REQS), 1)
     base = jnp.sum(
-        jnp.where(at % REQS == req, len_row[...].astype(F32), 0.0), axis=1, keepdims=True
-    )
-    step = (lax.broadcasted_iota(jnp.int32, (ROWS, 1), 0) // REQS).astype(F32)
+        jnp.where((at & (REQS - 1)) == req, len_row[...].astype(F32), 0.0), axis=1, keepdims=True
+    )
+    step = (lax.broadcasted_iota(jnp.int32, (ROWS, 1), 0) >> 5).astype(F32)
     angles = (base + step) * freq[...]
     cos = jnp.cos(angles)
     sin = jnp.sin(angles)
@@ -173,7 +188,7 @@
     kv_copy.wait()
     scale = HD ** -0.5
     spot = lax.broadcasted_iota(jnp.int32, (16, WIDE), 1)
-    when = lax.broadcasted_iota(jnp.int32, (16, WIDE), 0) % STEPS
+    when = lax.broadcasted_iota(jnp.int32, (16, WIDE), 0) & (STEPS - 1)
     causal = (spot >= SPAN) & (spot - SPAN <= when)
     rest = jnp.zeros((WIDE - SPAN - 16, HD), BF16)
 
@@ -203,40 +218,47 @@
     rows = jnp.concatenate(
         [mixed[g * ROWS:(g + 1) * ROWS].astype(BF16) for g in range(GROUP)], axis=1
     )
-    near = (near0, near1, near2, near3)
     stores = []
-    for i, (k, j) in enumerate(order):
+    for i in range(len(order)):
         weight(i).wait()
         outs[i] = jnp.dot(rows, o_w[i], preferred_element_type=F32).astype(BF16)
-        store = pltpu.make_async_copy(outs.at[i], near[k].at[j], out_sem.at[i])
+        store = pltpu.make_async_copy(outs.at[i], into[i], out_sem.at[i])
         store.start()
         stores.append(store)
     for store in stores:
         store.wait()
 
 
-def sum_kernel(own, a, b, c, out):
-    out[...] = (
-        own[1].astype(F32) + a[1].astype(F32) + b[1].astype(F32) + c[1].astype(F32)
-    ).astype(BF16)
-
-
-def close_kernel(own, a, b, c, other, pick, home, slots):
-    total = (
-        own[0].astype(F32) + a[0].astype(F32) + b[0].astype(F32) + c[0].astype(F32)
-        + other[...].astype(F32)
-    ).astype(BF16)
-    both = jnp.dot(pick[...], total, preferred_element_type=F32).astype(BF16)
-    home[...] = both[:ROWS]
-    slots[...] = both[ROWS:]
+def relay_kernel(up1, down0, far1, far0, next_up, next_down):
+    next_up[...] = (up1[...].astype(F32) + far1[...].astype(F32)).astype(BF16)
+    next_down[...] = (down0[...].astype(F32) + far0[...].astype(F32)).astype(BF16)
+
+
+def close_kernel(own, up0, up1, down0, down1, pick, keep, pass_on, slots):
+    y = lax.axis_index("tp") // RING
+    near = own[0].astype(F32) + up0[...].astype(F32) + down0[...].astype(F32)
+    other = (own[1].astype(F32) + up1[...].astype(F32) + down1[...].astype(F32)).astype(BF16)
+    keep[...] = near
+    pass_on[...] = other
+    choice = pick[ROWS:]
+    for j, part in enumerate((near.astype(BF16), other)):
+        taken = jnp.dot(choice, part, preferred_element_type=F32).astype(BF16)
+        slots[:, lax.rem(y + j, 2)] = taken.reshape(INST, STEPS * CAP, taken.shape[-1])
+
+
+def home_kernel(keep, other, pick, home):
+    total = (keep[...] + other[...].astype(F32)).astype(BF16)
+    home[...] = jnp.dot(pick[:ROWS], total, preferred_element_type=F32).astype(BF16)
 
 
 def arrive_kernel(rows, out):
+    total = rows[:, 0].astype(F32) + rows[:, 1].astype(F32)
+    total = total.reshape(ROWS, total.shape[-1]).astype(BF16)
     to = lax.broadcasted_iota(jnp.int32, (ROWS, ROWS), 0)
     come = lax.broadcasted_iota(jnp.int32, (ROWS, ROWS), 1)
-    t, s, c = to // (INST * CAP), (to // CAP) % INST, to % CAP
+    t, s, c = to >> 5, (to >> 1) & (INST - 1), to & (CAP - 1)
     turn = jnp.where(come == s * (STEPS * CAP) + t * CAP + c, 1.0, 0.0).astype(BF16)
-    out[...] = jnp.dot(turn, rows[...], preferred_element_type=F32).astype(BF16)
+    out[...] = jnp.dot(turn, total, preferred_element_type=F32).astype(BF16)
 
 
 def copy_kernel(got, out):
@@ -277,12 +299,12 @@
     inverse = np.float32(ROPE_BASE) ** (-np.arange(half, dtype=np.float32) * np.float32(2.0) / np.float32(HD))
     freq = jnp.asarray(np.concatenate([inverse, inverse])[None, :].astype(np.float32))
     chunks = 8
-    near_shape = jax.ShapeDtypeStruct((2, ROWS, share), BF16)
-    near = pl.pallas_call(
+    piece = jax.ShapeDtypeStruct((ROWS, share), BF16)
+    far1, far0, up0, down1, up1, down0, own = pl.pallas_call(
         attend_kernel,
-        out_shape=(near_shape,) * RING,
-        in_specs=[SMEM, SMEM, VMEM, VMEM, ANY, ANY, ANY, ANY, VMEM],
-        out_specs=(ANY,) * RING,
+        out_shape=(piece,) * 6 + (jax.ShapeDtypeStruct((2, ROWS, share), BF16),),
+        in_specs=[ANY] * 9,
+        out_specs=(ANY,) * 7,
         scratch_shapes=[
             pltpu.VMEM((ROWS, width), BF16),
             pltpu.VMEM(query_weight.shape, BF16),
@@ -295,56 +317,65 @@
             pltpu.VMEM((GROUP * ROWS, HD), F32),
             pltpu.VMEM((2 * RING, ROWS, share), BF16),
             pltpu.VMEM((ROWS, GROUP * HD), F32),
+            pltpu.VMEM((2 * ROWS, HD), BF16),
+            pltpu.SMEM((REQS,), jnp.int32),
+            pltpu.SMEM((MAXP, REQS), jnp.int32),
+            pltpu.VMEM((1, REQS), jnp.int32),
+            pltpu.VMEM((1, HD), F32),
             pltpu.SemaphoreType.DMA((chunks,)),
             pltpu.SemaphoreType.DMA((chunks,)),
             pltpu.SemaphoreType.DMA((2 * RING,)),
             pltpu.SemaphoreType.DMA,
             pltpu.SemaphoreType.DMA((2 * RING,)),
+            pltpu.SemaphoreType.DMA((5,)),
         ],
         compiler_params=pltpu.CompilerParams(vmem_limit_bytes=FULL_VMEM),
         cost_estimate=pl.CostEstimate(flops=2_400_000_000, bytes_accessed=24 << 20, transcendentals=200_000),
         name="attend",
     )(
-        lengths, table, lengths.reshape(1, REQS), freq,
         hidden.reshape(ROWS, width), query_weight, output_weight, kv_pool,
-        new_kv.reshape(2 * ROWS, HD),
+        new_kv.reshape(2 * ROWS, HD), lengths, table, lengths.reshape(1, REQS), freq,
     )
 
     def shift(k):
         return [(s, (s // RING) * RING + (s + k) % RING) for s in range(2 * RING)]
 
-    got = [lax.ppermute(near[k], "tp", shift(k)) for k in (2, 1, 3)]
-    part = pl.pallas_call(
-        sum_kernel,
-        out_shape=jax.ShapeDtypeStruct((ROWS, share), BF16),
-        in_specs=[VMEM] * 4,
-        out_specs=VMEM,
-        compiler_params=pltpu.CompilerParams(vmem_limit_bytes=SMALL_VMEM),
-        cost_estimate=pl.CostEstimate(flops=0, bytes_accessed=2 << 20, transcendentals=0),
-        name="sum_ring",
-    )(near[0], *got)
-    other = lax.ppermute(part, "tp", [(s, (s + RING) % (2 * RING)) for s in range(2 * RING)])
-    home, slots = pl.pallas_call(
+    def small(kernel, out, name):
+        return pl.pallas_call(
+            kernel,
+            out_shape=out,
+            compiler_params=pltpu.CompilerParams(vmem_limit_bytes=SMALL_VMEM),
+            cost_estimate=pl.CostEstimate(flops=0, bytes_accessed=2 << 20, transcendentals=0),
+            name=name,
+        )
+
+    far1 = lax.ppermute(far1, "tp", shift(1))
+    far0 = lax.ppermute(far0, "tp", shift(-1))
+    up0 = lax.ppermute(up0, "tp", shift(1))
+    down1 = lax.ppermute(down1, "tp", shift(-1))
+    next_up, next_down = small(relay_kernel, (piece,) * 2, "relay")(up1, down0, far1, far0)
+    up1 = lax.ppermute(next_up, "tp", shift(1))
+    down0 = lax.ppermute(next_down, "tp", shift(-1))
+    keep, pass_on, slots = small(
         close_kernel,
-        out_shape=(jax.ShapeDtypeStruct((ROWS, share), BF16),) * 2,
-        in_specs=[VMEM] * 6,
-        out_specs=(VMEM,) * 2,
-        compiler_params=pltpu.CompilerParams(vmem_limit_bytes=SMALL_VMEM),
-        cost_estimate=pl.CostEstimate(flops=0, bytes_accessed=2 << 20, transcendentals=0),
-        name="close",
-    )(near[0], *got, other, pick)
-    arrival_cache, slots = lax.optimization_barrier((arrival_cache, slots))
+        (
+            jax.ShapeDtypeStruct((ROWS, share), F32),
+            piece,
+            jax.ShapeDtypeStruct((INST, 2, STEPS * CAP, share), BF16),
+        ),
+        "close",
+    )(own, up0, up1, down0, down1, pick)
+    other = lax.ppermute(pass_on, "tp", [(s, (s + RING) % (2 * RING)) for s in range(2 * RING)])
+    arrival_cache, slots, other = lax.optimization_barrier((arrival_cache, slots, other))
+    home = small(home_kernel, piece, "home")(keep, other, pick)
+    peers = [
+        [i * 2 * RING + y * RING + z for i in range(INST) for y in range(2)] for z in range(RING)
+    ]
     rows = lax.all_to_all(
-        slots.reshape(INST, STEPS * CAP, share), "inst", split_axis=0, concat_axis=0, tiled=True
-    )
-    arrival = pl.pallas_call(
-        arrive_kernel,
-        out_shape=jax.ShapeDtypeStruct((ROWS, share), BF16),
-        in_specs=[VMEM],
-        out_specs=VMEM,
-        compiler_params=pltpu.CompilerParams(vmem_limit_bytes=SMALL_VMEM),
-        name="arrive",
-    )(rows.reshape(ROWS, share))
+        slots.reshape(2 * INST, STEPS * CAP, share), ("inst", "tp"),
+        split_axis=0, concat_axis=0, tiled=True, axis_index_groups=peers,
+    )
+    arrival = small(arrive_kernel, piece, "arrive")(rows.reshape(INST, 2, STEPS * CAP, share))
     block = pl.BlockSpec((4,) + arrival_cache.shape[1:], lambda i: (i, 0, 0, 0, 0))
     arrival_cache = pl.pallas_call(
         copy_kernel,

time: 81.3 us -> 79.7 us (0.980)
  waiting for transfers between devices: 33.6 us -> 23.2 us
  starting transfers between devices: 23.6 us -> 28.4 us
  local copies, waits for them, and re-layouts: 1.75 us -> 4.55 us
    ppermute x4 -> x7, waiting for transfers between devices: 28.1 us -> 16.5 us  [the longest x1 7.14 us: local(): lax.ppermute(pass_on, 'tp', [(s, (s + RING) % (2 * RING)) for s in range(...]
    ppermute x4 -> x7, starting transfers between devices: 6.84 us -> 9.77 us  [the longest x1 2.67 us: local(): down1 = lax.ppermute(down1, 'tp', shift(-1))]
    unnamed x6 -> x14, local copies, waits for them, and re-layouts: 1.75 us -> 4.55 us
    all_to_all x1, starting transfers between devices: 8.3 us -> 10.1 us  [local(): lax.all_to_all(slots.reshape(2 * INST, STEPS * CAP, share), ('inst', 'tp'...]
    all_to_all x1, waiting for transfers between devices: 5.45 us -> 6.71 us  [local(): lax.all_to_all(slots.reshape(2 * INST, STEPS * CAP, share), ('inst', 'tp'...]
    pallas_call x4 -> x5, Pallas kernels: 13.2 us -> 14 us  [the longest x1 10.5 us: local(): pl.pallas_call(attend_kernel, out_shape=(piece,) * 6 + (jax.ShapeDtypeStr...]
  transfers between devices with their start and end apart: 6 -> 9, of which waited for: 5 -> 5; matrix products, arithmetic and copies ran while one was open for 0% -> 0% of each run, Pallas kernels for 19% -> 19%
where the time goes in v4:
time: 79.7 us; the launch traced here: 78.9 us
  starting transfers between devices  28.4 us (36%)
  waiting for transfers between devices  23.2 us (29%)
  Pallas kernels  22.1 us (28%)
  local copies, waits for them, and re-layouts  4.55 us (6%)
    pallas_call x1, Pallas kernels, local(): pl.pallas_call(attend_kernel, out_shape=(piece,) * 6 + (jax.ShapeDtypeStr...  10.5 us
    all_to_all x1, starting transfers between devices, local(): lax.all_to_all(slots.reshape(2 * INST, STEPS * CAP, share), ('inst', 'tp'...  10.1 us
    all_to_all x1, starting transfers between devices, local(): lax.all_to_all(send, 'inst', split_axis=0, concat_axis=0, tiled=True)  8.46 us
    ppermute x1, waiting for transfers between devices, local(): lax.ppermute(pass_on, 'tp', [(s, (s + RING) % (2 * RING)) for s in range(...  7.14 us
    all_to_all x1, waiting for transfers between devices, local(): lax.all_to_all(slots.reshape(2 * INST, STEPS * CAP, share), ('inst', 'tp'...  6.71 us
    pallas_call x1, Pallas kernels, local(): pl.pallas_call(pack_kernel, out_shape=(jax.ShapeDtypeStruct((INST * CAP,)...  4.86 us
    unnamed x14, local copies, waits for them, and re-layouts  4.55 us
    ppermute x1, waiting for transfers between devices, local(): up1 = lax.ppermute(next_up, 'tp', shift(1))  4.51 us
  transfers between devices with their start and end apart: 9, of which 5 were waited for; matrix products, arithmetic and copies ran while one was open for 0% of the time, Pallas kernels for 19%

profile of v4, /device:TPU:1, one launch (start us, length us, event | category | flops | bytes accessed | tf_op | source)
XLA Modules:
  0.0 78.9 jit_solution(4643411753216726244)
XLA Ops:
  0.6 4.9 %pack_pages.1 = (bf16[32,3,2,64,128]{4,3,2,1,0:T(8,128)(2,1)}, bf16[256,128]{1,0:T(8,128)(2,1)}) custom-call(s32[3,32]{1,0:T(4,128)} %bitcast.14, s32[16]{0:T(128)} %mreq.1, s32[16]{0:T(128)} %bitcast.17, s32[16]{0:T(128)} %resume.1, bf16[96,2,64,128]{3,2,1,0:T(8,128)(2,1)} %pool.3), custom_call_target="tpu_custom_call" | custom-call | bytes 6291456 | tf_op jit(solution)/shard_map/pack_pages/pallas_call | solution.py:275
  5.5 8.5 %all-to-all-start = ((bf16[32,3,2,64,128]{4,3,2,1,0:T(8,128)(2,1)}), bf16[32,3,2,64,128]{4,3,2,1,0:T(8,128)(2,1)S(1)}, u32[]{:S(2)}, u32[]{:S(2)}) async-start(bf16[32,3,2,64,128]{4,3,2,1,0:T(8,128)(2,1)} %get-tuple-element.31), calls=%async_computation | async-start | bytes 6291456 | tf_op jit(solution)/shard_map/all_to_all | solution.py:296
  14.0 10.5 %attend.1 = (bf16[128,1024]{1,0:T(8,128)(2,1)}, bf16[128,1024]{1,0:T(8,128)(2,1)}, bf16[128,1024]{1,0:T(8,128)(2,1)}, bf16[128,1024]{1,0:T(8,128)(2,1)}, bf16[12...) custom-call(bf16[128,8192]{1,0:T(8,128)(2,1)} %bitcast.10, bf16[8192,512]{1,0:T(8,128)(2,1)} %wq.1, ...), custom_call_target="tpu_custom_call" | custom-call | flops 2400000000 | bytes 25165824 | tf_op jit(solution)/shard_map/attend/pallas_call | solution.py:303
  24.5 1.7 %collective-permute-start.1 = (bf16[128,1024]{1,0:T(8,128)(2,1)}, bf16[128,1024]{1,0:T(8,128)(2,1)S(1)}, u32[]{:S(2)}, u32[]{:S(2)}) collective-permute-start(bf16[128,1024]{1,0:T(8,128)(2,1)} %get-tuple-element.24), channel_id=1, source_target_pairs={{0,1},{1,2},{2,3},{3,0},{4,5},{5,6},{6,7},{7,4},{8,9},{9,10},{10,1... | collective-permute-start | bytes 786440 | tf_op jit(solution)/shard_map/ppermute | solution.py:352
  26.2 2.2 %collective-permute-start.2 = (bf16[128,1024]{1,0:T(8,128)(2,1)}, bf16[128,1024]{1,0:T(8,128)(2,1)S(1)}, u32[]{:S(2)}, u32[]{:S(2)}) collective-permute-start(bf16[128,1024]{1,0:T(8,128)(2,1)} %get-tuple-element.25), channel_id=1, source_target_pairs={{0,3},{1,0},{2,1},{3,2},{4,7},{5,4},{6,5},{7,6},{8,11},{9,8},{10,9... | collective-permute-start | bytes 786440 | tf_op jit(solution)/shard_map/ppermute | solution.py:353
  28.4 0.0 collective-permute-start
  28.5 2.7 %collective-permute-start.5 = (bf16[128,1024]{1,0:T(8,128)(2,1)}, bf16[128,1024]{1,0:T(8,128)(2,1)S(1)}, u32[]{:S(2)}, u32[]{:S(2)}) collective-permute-start(bf16[128,1024]{1,0:T(8,128)(2,1)} %get-tuple-element.28), channel_id=1, source_target_pairs={{0,3},{1,0},{2,1},{3,2},{4,7},{5,4},{6,5},{7,6},{8,11},{9,8},{10,9... | collective-permute-start | bytes 786440 | tf_op jit(solution)/shard_map/ppermute | solution.py:355
  31.1 4.0 %collective-permute-done.1.far1 = bf16[128,1024]{1,0:T(8,128)(2,1)S(1)} collective-permute-done((bf16[128,1024]{1,0:T(8,128)(2,1)}, bf16[128,1024]{1,0:T(8,128)(2,1)S(1)}, u32[]{:S(2)}, u32[]{:S(2)}) %collective-permute-start.1) | collective-permute-done | bytes 262176 | tf_op jit(solution)/shard_map/ppermute | solution.py:352
  35.1 0.0 collective-permute-done.2.far0
  35.1 0.9 %copy-done.5 = bf16[128,1024]{1,0:T(8,128)(2,1)S(1)} copy-done((bf16[128,1024]{1,0:T(8,128)(2,1)S(1)}, bf16[128,1024]{1,0:T(8,128)(2,1)}, u32[]{:S(2)}) %copy-start.5) | copy-done | bytes 262168
  36.1 0.9 %copy-done.6 = bf16[128,1024]{1,0:T(8,128)(2,1)S(1)} copy-done((bf16[128,1024]{1,0:T(8,128)(2,1)S(1)}, bf16[128,1024]{1,0:T(8,128)(2,1)}, u32[]{:S(2)}) %copy-start.6) | copy-done | bytes 262168
  37.0 0.1 relay.1
  37.2 0.6 collective-permute-start.3
  37.7 2.2 %collective-permute-start.4 = (bf16[128,1024]{1,0:T(8,128)(2,1)S(1)}, bf16[128,1024]{1,0:T(8,128)(2,1)S(1)}, u32[]{:S(2)}, u32[]{:S(2)}) collective-permute-start(bf16[128,1024]{1,0:T(8,128)(2,1)S(1)} %get-tuple-element.27), channel_id=1, source_target_pairs={{0,3},{1,0},{2,1},{3,2},{4,7},{5,4},{6,5},{7,6},{8,11},{9,8},{10,9... | collective-permute-start | bytes 786440 | tf_op jit(solution)/shard_map/ppermute | solution.py:358
  39.9 0.8 %collective-permute-done.up0 = bf16[128,1024]{1,0:T(8,128)(2,1)S(1)} collective-permute-done((bf16[128,1024]{1,0:T(8,128)(2,1)}, bf16[128,1024]{1,0:T(8,128)(2,1)S(1)}, u32[]{:S(2)}, u32[]{:S(2)}) %collective-permute-start) | collective-permute-done | bytes 262176 | tf_op jit(solution)/shard_map/ppermute | solution.py:354
  40.7 0.0 collective-permute-done.5.down1
  40.7 4.5 %collective-permute-done.3.up1 = bf16[128,1024]{1,0:T(8,128)(2,1)S(1)} collective-permute-done((bf16[128,1024]{1,0:T(8,128)(2,1)S(1)}, bf16[128,1024]{1,0:T(8,128)(2,1)S(1)}, u32[]{:S(2)}, u32[]{:S(2)}) %collective-permute-start.3) | collective-permute-done | bytes 262176 | tf_op jit(solution)/shard_map/ppermute | solution.py:357
  45.3 0.0 collective-permute-done.4.down0
  45.3 0.0 copy-done.4
  45.3 1.0 %copy-done = bf16[2,128,1024]{2,1,0:T(8,128)(2,1)S(1)} copy-done((bf16[2,128,1024]{2,1,0:T(8,128)(2,1)S(1)}, bf16[2,128,1024]{2,1,0:T(8,128)(2,1)}, u32[]{:S(2)}) %copy-start) | copy-done | bytes 524312
  46.3 0.4 close.1
  46.7 0.8 %copy-done.1 = bf16[16,2,8,1024]{3,2,1,0:T(8,128)(2,1)} copy-done((bf16[16,2,8,1024]{3,2,1,0:T(8,128)(2,1)}, bf16[16,2,8,1024]{3,2,1,0:T(8,128)(2,1)S(1)}, u32[]{:S(2)}) %copy-start.1) | copy-done | bytes 524312
  47.5 0.8 %copy-done.2 = f32[128,1024]{1,0:T(8,128)} copy-done((f32[128,1024]{1,0:T(8,128)}, f32[128,1024]{1,0:T(8,128)S(1)}, u32[]{:S(2)}) %copy-start.2) | copy-done | bytes 524312
  48.3 0.4 collective-permute-start.6
  48.7 7.1 %collective-permute-done.6.other = bf16[128,1024]{1,0:T(8,128)(2,1)S(1)} collective-permute-done((bf16[128,1024]{1,0:T(8,128)(2,1)S(1)}, bf16[128,1024]{1,0:T(8,128)(2,1)S(1)}, u32[]{:S(2)}, u32[]{:S(2)}) %collective-permute-start.6) | collective-permute-done | bytes 262176 | tf_op jit(solution)/shard_map/ppermute | solution.py:368
  55.9 0.0 all-to-all-done.got
  55.9 10.1 %all-to-all-start.1 = ((bf16[32,8,1024]{2,1,0:T(8,128)(2,1)}), bf16[32,8,1024]{2,1,0:T(8,128)(2,1)}, u32[]{:S(2)}, u32[]{:S(2)}) async-start(bf16[32,8,1024]{2,1,0:T(8,128)(2,1)} %bitcast.9), calls=%async_computation.1 | async-start | bytes 1048576 | tf_op jit(solution)/shard_map/all_to_all | solution.py:374
  66.1 3.2 %keep_pages.1 = bf16[32,3,2,64,128]{4,3,2,1,0:T(8,128)(2,1)} custom-call(bf16[32,3,2,64,128]{4,3,2,1,0:T(8,128)(2,1)S(1)} %all-to-all-done.got), custom_call_target="tpu_custom_call" | custom-call | bytes 6291456 | tf_op jit(solution)/shard_map/keep_pages/pallas_call | solution.py:380
  69.3 0.0 copy-done.3
  69.3 0.9 %home.1 = bf16[128,1024]{1,0:T(8,128)(2,1)} custom-call(f32[128,1024]{1,0:T(8,128)S(1)} %copy-done.3, bf16[128,1024]{1,0:T(8,128)(2,1)S(1)} %collective-permute-done.6.other, bf16[256,128]{1,0:T(8,128)(2,1)S(1)} %copy-done.4), custom_call_target="tpu_custom_call" | custom-call | bytes 2097152 | tf_op jit(solution)/shard_map/home/pallas_call | solution.py:370
  70.2 6.7 %all-to-all-done.1 = bf16[32,8,1024]{2,1,0:T(8,128)(2,1)} async-done(((bf16[32,8,1024]{2,1,0:T(8,128)(2,1)}), bf16[32,8,1024]{2,1,0:T(8,128)(2,1)}, u32[]{:S(2)}, u32[]{:S(2)}) %all-to-all-start.1) | async-done | bytes 524320 | tf_op jit(solution)/shard_map/all_to_all | solution.py:374
  76.9 2.0 %arrive.1 = bf16[128,1024]{1,0:T(8,128)(2,1)} custom-call(bf16[16,2,8,1024]{3,2,1,0:T(8,128)(2,1)} %bitcast.7.rows), custom_call_target="tpu_custom_call" | custom-call | bytes 2097152 | tf_op jit(solution)/shard_map/arrive/pallas_call | solution.py:378
  (7 shorter events, 0.0 us)
Async XLA Ops:
  5.5 50.4 %all-to-all-start = ((bf16[32,3,2,64,128]{4,3,2,1,0:T(8,128)(2,1)}), bf16[32,3,2,64,128]{4,3,2,1,0:T(8,128)(2,1)S(1)}, u32[]{:S(2)}, u32[]{:S(2)}) async-start(bf16[32,3,2,64,128]{4,3,2,1,0:T(8,128)(2,1)} %get-tuple-element.31), calls=%async_computation | async-start | bytes 6291456 | tf_op jit(solution)/shard_map/all_to_all | solution.py:296
  14.0 31.3 %copy-start.4 = (bf16[256,128]{1,0:T(8,128)(2,1)S(1)}, bf16[256,128]{1,0:T(8,128)(2,1)}, u32[]{:S(2)}) copy-start(bf16[256,128]{1,0:T(8,128)(2,1)} %get-tuple-element.29.pick) | copy-start | bytes 196612
  24.5 10.6 %collective-permute-start.1 = (bf16[128,1024]{1,0:T(8,128)(2,1)}, bf16[128,1024]{1,0:T(8,128)(2,1)S(1)}, u32[]{:S(2)}, u32[]{:S(2)}) collective-permute-start(bf16[128,1024]{1,0:T(8,128)(2,1)} %get-tuple-element.24), channel_id=1, source_target_pairs={{0,1},{1,2},{2,3},{3,0},{4,5},{5,6},{6,7},{7,4},{8,9},{9,10},{10,1... | collective-permute-start | bytes 786440 | tf_op jit(solution)/shard_map/ppermute | solution.py:352
  26.2 8.9 %collective-permute-start.2 = (bf16[128,1024]{1,0:T(8,128)(2,1)}, bf16[128,1024]{1,0:T(8,128)(2,1)S(1)}, u32[]{:S(2)}, u32[]{:S(2)}) collective-permute-start(bf16[128,1024]{1,0:T(8,128)(2,1)} %get-tuple-element.25), channel_id=1, source_target_pairs={{0,3},{1,0},{2,1},{3,2},{4,7},{5,4},{6,5},{7,6},{8,11},{9,8},{10,9... | collective-permute-start | bytes 786440 | tf_op jit(solution)/shard_map/ppermute | solution.py:353
  28.4 12.3 %collective-permute-start = (bf16[128,1024]{1,0:T(8,128)(2,1)}, bf16[128,1024]{1,0:T(8,128)(2,1)S(1)}, u32[]{:S(2)}, u32[]{:S(2)}) collective-permute-start(bf16[128,1024]{1,0:T(8,128)(2,1)} %get-tuple-element.21), channel_id=1, source_target_pairs={{0,1},{1,2},{2,3},{3,0},{4,5},{5,6},{6,7},{7,4},{8,9},{9,10},{10,1... | collective-permute-start | bytes 786440 | tf_op jit(solution)/shard_map/ppermute | solution.py:354
  28.5 12.3 %collective-permute-start.5 = (bf16[128,1024]{1,0:T(8,128)(2,1)}, bf16[128,1024]{1,0:T(8,128)(2,1)S(1)}, u32[]{:S(2)}, u32[]{:S(2)}) collective-permute-start(bf16[128,1024]{1,0:T(8,128)(2,1)} %get-tuple-element.28), channel_id=1, source_target_pairs={{0,3},{1,0},{2,1},{3,2},{4,7},{5,4},{6,5},{7,6},{8,11},{9,8},{10,9... | collective-permute-start | bytes 786440 | tf_op jit(solution)/shard_map/ppermute | solution.py:355
  35.1 1.0 %copy-start.5 = (bf16[128,1024]{1,0:T(8,128)(2,1)S(1)}, bf16[128,1024]{1,0:T(8,128)(2,1)}, u32[]{:S(2)}) copy-start(bf16[128,1024]{1,0:T(8,128)(2,1)} %get-tuple-element.22.up1) | copy-start | bytes 786436
  36.1 0.9 %copy-start.6 = (bf16[128,1024]{1,0:T(8,128)(2,1)S(1)}, bf16[128,1024]{1,0:T(8,128)(2,1)}, u32[]{:S(2)}) copy-start(bf16[128,1024]{1,0:T(8,128)(2,1)} %get-tuple-element.23.down0) | copy-start | bytes 786436
  37.2 8.1 %collective-permute-start.3 = (bf16[128,1024]{1,0:T(8,128)(2,1)S(1)}, bf16[128,1024]{1,0:T(8,128)(2,1)S(1)}, u32[]{:S(2)}, u32[]{:S(2)}) collective-permute-start(bf16[128,1024]{1,0:T(8,128)(2,1)S(1)} %get-tuple-element.26), channel_id=1, source_target_pairs={{0,1},{1,2},{2,3},{3,0},{4,5},{5,6},{6,7},{7,4},{8,9},{9,10},{10,1... | collective-permute-start | bytes 786440 | tf_op jit(solution)/shard_map/ppermute | solution.py:357
  37.7 7.5 %collective-permute-start.4 = (bf16[128,1024]{1,0:T(8,128)(2,1)S(1)}, bf16[128,1024]{1,0:T(8,128)(2,1)S(1)}, u32[]{:S(2)}, u32[]{:S(2)}) collective-permute-start(bf16[128,1024]{1,0:T(8,128)(2,1)S(1)} %get-tuple-element.27), channel_id=1, source_target_pairs={{0,3},{1,0},{2,1},{3,2},{4,7},{5,4},{6,5},{7,6},{8,11},{9,8},{10,9... | collective-permute-start | bytes 786440 | tf_op jit(solution)/shard_map/ppermute | solution.py:358
  45.3 1.0 %copy-start = (bf16[2,128,1024]{2,1,0:T(8,128)(2,1)S(1)}, bf16[2,128,1024]{2,1,0:T(8,128)(2,1)}, u32[]{:S(2)}) copy-start(bf16[2,128,1024]{2,1,0:T(8,128)(2,1)} %get-tuple-element.20.own) | copy-start | bytes 1572868
  46.7 0.8 %copy-start.1 = (bf16[16,2,8,1024]{3,2,1,0:T(8,128)(2,1)}, bf16[16,2,8,1024]{3,2,1,0:T(8,128)(2,1)S(1)}, u32[]{:S(2)}) copy-start(bf16[16,2,8,1024]{3,2,1,0:T(8,128)(2,1)S(1)} %get-tuple-element.35) | copy-start | bytes 1572868
  47.5 0.8 %copy-start.2 = (f32[128,1024]{1,0:T(8,128)}, f32[128,1024]{1,0:T(8,128)S(1)}, u32[]{:S(2)}) copy-start(f32[128,1024]{1,0:T(8,128)S(1)} %get-tuple-element.30.keep) | copy-start | bytes 1572868
  48.3 7.6 %collective-permute-start.6 = (bf16[128,1024]{1,0:T(8,128)(2,1)S(1)}, bf16[128,1024]{1,0:T(8,128)(2,1)S(1)}, u32[]{:S(2)}, u32[]{:S(2)}) collective-permute-start(bf16[128,1024]{1,0:T(8,128)(2,1)S(1)} %get-tuple-element.33), channel_id=1, source_target_pairs={{0,4},{1,5},{2,6},{3,7},{4,0},{5,1},{6,2},{7,3},{8,12},{9,13},{10,... | collective-permute-start | bytes 786440 | tf_op jit(solution)/shard_map/ppermute | solution.py:368
  55.9 21.0 %all-to-all-start.1 = ((bf16[32,8,1024]{2,1,0:T(8,128)(2,1)}), bf16[32,8,1024]{2,1,0:T(8,128)(2,1)}, u32[]{:S(2)}, u32[]{:S(2)}) async-start(bf16[32,8,1024]{2,1,0:T(8,128)(2,1)} %bitcast.9), calls=%async_computation.1 | async-start | bytes 1048576 | tf_op jit(solution)/shard_map/all_to_all | solution.py:374
  66.1 3.3 %copy-start.3 = (f32[128,1024]{1,0:T(8,128)S(1)}, f32[128,1024]{1,0:T(8,128)}, u32[]{:S(2)}) copy-start(f32[128,1024]{1,0:T(8,128)} %copy-done.2) | copy-start | bytes 1572868

commit v5 on v4

--- a/solution.py
+++ b/solution.py
@@ -1,3 +1,5 @@
+import functools
+
 import jax
 import jax.numpy as jnp
 import numpy as np
@@ -20,7 +22,7 @@
 ROWS = STEPS * REQS
 WIDE = 256
 ROPE_BASE = 500000.0
-FULL_VMEM = 58 << 20
+FULL_VMEM = 48 << 20
 SMALL_VMEM = 6 << 20
 F32 = jnp.float32
 BF16 = jnp.bfloat16
@@ -29,9 +31,20 @@
 ANY = pl.BlockSpec(memory_space=pl.ANY)
 
 
-def pack_kernel(table, mreq, mdest, resume, pool, send, pick, slot_req, count, kv, zeros, wide, kv_sem, sem):
+def pack_kernel(
+    page_list, req_list, dest_list, resume_list, pool, send, pick,
+    table, mreq, mdest, resume, slot_req, count, kv, zeros, wide, kv_sem, sem, small_sem,
+):
     load = pltpu.make_async_copy(pool, kv, kv_sem)
     load.start()
+    small = [
+        pltpu.make_async_copy(source, target, small_sem.at[i])
+        for i, (source, target) in enumerate((
+            (req_list, mreq), (dest_list, mdest), (resume_list, resume), (page_list, table),
+        ))
+    ]
+    for copy in small:
+        copy.start()
     zeros[...] = jnp.zeros_like(zeros)
 
     def clear(s, carry):
@@ -44,6 +57,9 @@
 
     lax.fori_loop(0, INST * CAP, clear, 0)
     lax.fori_loop(0, INST, fresh, 0)
+
+    for copy in small:
+        copy.wait()
 
     def place(k, carry):
         d = mdest[k]
@@ -104,13 +120,13 @@
 def attend_kernel(
     hidden, wq, wo, pool, new_kv, len_list, page_list, len_line, freq_line,
     far1, far0, up0, down1, up1, down0, own,
-    x, q_w, o_w, kv, fresh, turned, scores, probs, mixed, outs, acc,
+    x, q_w, o_w, kv, fresh, turned, scores, probs, mixed, acc,
     recent, lengths, table, len_row, freq,
-    x_sem, q_sem, o_sem, kv_sem, out_sem, small_sem,
+    x_sem, q_sem, o_sem, kv_sem, small_sem,
 ):
     chunks = x_sem.shape[0]
     depth = x.shape[1] // chunks
-    share = outs.shape[-1]
+    share = own.shape[-1]
     tp = lax.axis_index("tp")
     y, z = tp // RING, tp % RING
 
@@ -218,15 +234,9 @@
     rows = jnp.concatenate(
         [mixed[g * ROWS:(g + 1) * ROWS].astype(BF16) for g in range(GROUP)], axis=1
     )
-    stores = []
     for i in range(len(order)):
         weight(i).wait()
-        outs[i] = jnp.dot(rows, o_w[i], preferred_element_type=F32).astype(BF16)
-        store = pltpu.make_async_copy(outs.at[i], into[i], out_sem.at[i])
-        store.start()
-        stores.append(store)
-    for store in stores:
-        store.wait()
+        into[i][...] = jnp.dot(rows, o_w[i], preferred_element_type=F32).astype(BF16)
 
 
 def relay_kernel(up1, down0, far1, far0, next_up, next_down):
@@ -234,31 +244,25 @@
     next_down[...] = (down0[...].astype(F32) + far0[...].astype(F32)).astype(BF16)
 
 
-def close_kernel(own, up0, up1, down0, down1, pick, keep, pass_on, slots):
-    y = lax.axis_index("tp") // RING
-    near = own[0].astype(F32) + up0[...].astype(F32) + down0[...].astype(F32)
-    other = (own[1].astype(F32) + up1[...].astype(F32) + down1[...].astype(F32)).astype(BF16)
-    keep[...] = near
-    pass_on[...] = other
-    choice = pick[ROWS:]
-    for j, part in enumerate((near.astype(BF16), other)):
-        taken = jnp.dot(choice, part, preferred_element_type=F32).astype(BF16)
-        slots[:, lax.rem(y + j, 2)] = taken.reshape(INST, STEPS * CAP, taken.shape[-1])
-
-
-def home_kernel(keep, other, pick, home):
-    total = (keep[...] + other[...].astype(F32)).astype(BF16)
-    home[...] = jnp.dot(pick[:ROWS], total, preferred_element_type=F32).astype(BF16)
+def sum_kernel(own, up1, down1, out):
+    out[...] = (own[1].astype(F32) + up1[...].astype(F32) + down1[...].astype(F32)).astype(BF16)
+
+
+def close_kernel(own, up0, down0, other, pick, home, slots):
+    total = (
+        own[0].astype(F32) + up0[...].astype(F32) + down0[...].astype(F32) + other[...].astype(F32)
+    ).astype(BF16)
+    both = jnp.dot(pick[...], total, preferred_element_type=F32).astype(BF16)
+    home[...] = both[:ROWS]
+    slots[...] = both[ROWS:]
 
 
 def arrive_kernel(rows, out):
-    total = rows[:, 0].astype(F32) + rows[:, 1].astype(F32)
-    total = total.reshape(ROWS, total.shape[-1]).astype(BF16)
     to = lax.broadcasted_iota(jnp.int32, (ROWS, ROWS), 0)
     come = lax.broadcasted_iota(jnp.int32, (ROWS, ROWS), 1)
     t, s, c = to >> 5, (to >> 1) & (INST - 1), to & (CAP - 1)
     turn = jnp.where(come == s * (STEPS * CAP) + t * CAP + c, 1.0, 0.0).astype(BF16)
-    out[...] = jnp.dot(turn, total, preferred_element_type=F32).astype(BF16)
+    out[...] = jnp.dot(turn, rows[...], preferred_element_type=F32).astype(BF16)
 
 
 def copy_kernel(got, out):
@@ -272,15 +276,20 @@
     width = hidden.shape[-1]
     share = width // lax.axis_size("tp")
     table = page_table.T
+    hbm = functools.partial(pltpu.with_memory_space_constraint, memory_space=pltpu.HBM)
     send, pick = pl.pallas_call(
         pack_kernel,
         out_shape=(
-            jax.ShapeDtypeStruct((INST * CAP,) + (MAXP,) + kv_pool.shape[1:], BF16),
+            pltpu.HBM((INST * CAP, MAXP) + kv_pool.shape[1:], BF16),
             jax.ShapeDtypeStruct((2 * ROWS, ROWS), BF16),
         ),
-        in_specs=[SMEM] * 4 + [ANY],
+        in_specs=[ANY] * 5,
         out_specs=(ANY, VMEM),
         scratch_shapes=[
+            pltpu.SMEM((MAXP, REQS), jnp.int32),
+            pltpu.SMEM((MIG,), jnp.int32),
+            pltpu.SMEM((MIG,), jnp.int32),
+            pltpu.SMEM((MIG,), jnp.int32),
             pltpu.SMEM((INST * CAP,), jnp.int32),
             pltpu.SMEM((INST,), jnp.int32),
             pltpu.VMEM(kv_pool.shape, BF16),
@@ -288,11 +297,12 @@
             pltpu.VMEM((2 * ROWS, ROWS), F32),
             pltpu.SemaphoreType.DMA,
             pltpu.SemaphoreType.DMA,
+            pltpu.SemaphoreType.DMA((4,)),
         ],
         compiler_params=pltpu.CompilerParams(vmem_limit_bytes=FULL_VMEM),
         cost_estimate=pl.CostEstimate(flops=0, bytes_accessed=6 << 20, transcendentals=0),
         name="pack_pages",
-    )(table, mig_req, mig_dest.reshape(-1), resume, kv_pool)
+    )(hbm(table), hbm(mig_req), hbm(mig_dest.reshape(-1)), hbm(resume), hbm(kv_pool))
     arrival_cache = lax.all_to_all(send, "inst", split_axis=0, concat_axis=0, tiled=True)
 
     half = HD // 2
@@ -302,9 +312,9 @@
     piece = jax.ShapeDtypeStruct((ROWS, share), BF16)
     far1, far0, up0, down1, up1, down0, own = pl.pallas_call(
         attend_kernel,
-        out_shape=(piece,) * 6 + (jax.ShapeDtypeStruct((2, ROWS, share), BF16),),
+        out_shape=(pltpu.VMEM((ROWS, share), BF16),) * 6 + (pltpu.VMEM((2, ROWS, share), BF16),),
         in_specs=[ANY] * 9,
-        out_specs=(ANY,) * 7,
+        out_specs=(VMEM,) * 7,
         scratch_shapes=[
             pltpu.VMEM((ROWS, width), BF16),
             pltpu.VMEM(query_weight.shape, BF16),
@@ -315,7 +325,6 @@
             pltpu.VMEM((REQS * 16, WIDE), F32),
             pltpu.VMEM((REQS * 16, WIDE), BF16),
             pltpu.VMEM((GROUP * ROWS, HD), F32),
-            pltpu.VMEM((2 * RING, ROWS, share), BF16),
             pltpu.VMEM((ROWS, GROUP * HD), F32),
             pltpu.VMEM((2 * ROWS, HD), BF16),
             pltpu.SMEM((REQS,), jnp.int32),
@@ -326,15 +335,14 @@
             pltpu.SemaphoreType.DMA((chunks,)),
             pltpu.SemaphoreType.DMA((2 * RING,)),
             pltpu.SemaphoreType.DMA,
-            pltpu.SemaphoreType.DMA((2 * RING,)),
             pltpu.SemaphoreType.DMA((5,)),
         ],
         compiler_params=pltpu.CompilerParams(vmem_limit_bytes=FULL_VMEM),
         cost_estimate=pl.CostEstimate(flops=2_400_000_000, bytes_accessed=24 << 20, transcendentals=200_000),
         name="attend",
     )(
-        hidden.reshape(ROWS, width), query_weight, output_weight, kv_pool,
-        new_kv.reshape(2 * ROWS, HD), lengths, table, lengths.reshape(1, REQS), freq,
+        hbm(hidden.reshape(ROWS, width)), hbm(query_weight), hbm(output_weight), hbm(kv_pool),
+        hbm(new_kv.reshape(2 * ROWS, HD)), hbm(lengths), hbm(table), hbm(lengths.reshape(1, REQS)), hbm(freq),
     )
 
     def shift(k):
@@ -356,26 +364,16 @@
     next_up, next_down = small(relay_kernel, (piece,) * 2, "relay")(up1, down0, far1, far0)
     up1 = lax.ppermute(next_up, "tp", shift(1))
     down0 = lax.ppermute(next_down, "tp", shift(-1))
-    keep, pass_on, slots = small(
-        close_kernel,
-        (
-            jax.ShapeDtypeStruct((ROWS, share), F32),
-            piece,
-            jax.ShapeDtypeStruct((INST, 2, STEPS * CAP, share), BF16),
-        ),
-        "close",
-    )(own, up0, up1, down0, down1, pick)
-    other = lax.ppermute(pass_on, "tp", [(s, (s + RING) % (2 * RING)) for s in range(2 * RING)])
-    arrival_cache, slots, other = lax.optimization_barrier((arrival_cache, slots, other))
-    home = small(home_kernel, piece, "home")(keep, other, pick)
-    peers = [
-        [i * 2 * RING + y * RING + z for i in range(INST) for y in range(2)] for z in range(RING)
-    ]
+    part = small(sum_kernel, piece, "sum_ring")(own, up1, down1)
+    other = lax.ppermute(part, "tp", [(s, (s + RING) % (2 * RING)) for s in range(2 * RING)])
+    home, slots = small(close_kernel, (piece, pltpu.HBM((ROWS, share), BF16)), "close")(
+        own, up0, down0, other, pick
+    )
+    arrival_cache, slots = lax.optimization_barrier((arrival_cache, slots))
     rows = lax.all_to_all(
-        slots.reshape(2 * INST, STEPS * CAP, share), ("inst", "tp"),
-        split_axis=0, concat_axis=0, tiled=True, axis_index_groups=peers,
-    )
-    arrival = small(arrive_kernel, piece, "arrive")(rows.reshape(INST, 2, STEPS * CAP, share))
+        slots.reshape(INST, STEPS * CAP, share), "inst", split_axis=0, concat_axis=0, tiled=True
+    )
+    arrival = small(arrive_kernel, piece, "arrive")(rows.reshape(ROWS, share))
     block = pl.BlockSpec((4,) + arrival_cache.shape[1:], lambda i: (i, 0, 0, 0, 0))
     arrival_cache = pl.pallas_call(
         copy_kernel,

time: 79.7 us -> 74.3 us (0.932)
  local copies, waits for them, and re-layouts: 4.55 us -> 0 us
  waiting for transfers between devices: 23.2 us -> 27.2 us
  Pallas kernels: 22.1 us -> 18.8 us
  starting transfers between devices: 28.4 us -> 27.4 us
    unnamed x14 -> x0, local copies, waits for them, and re-layouts: 4.55 us -> none
    ppermute x1, waiting for transfers between devices: 0.84 us -> 4.96 us  [local(): up0 = lax.ppermute(up0, 'tp', shift(1))]
    pallas_call x5, Pallas kernels: 18.7 us -> 15.4 us  [the longest x1 9.73 us: local(): pl.pallas_call(attend_kernel, out_shape=(pltpu.VMEM((ROWS, share), BF16),...]
    ppermute x1, waiting for transfers between devices: 7.14 us -> 4.74 us  [local(): lax.ppermute(part, 'tp', [(s, (s + RING) % (2 * RING)) for s in range(2 *...]
    all_to_all x1, waiting for transfers between devices: 0.02 us -> 2.17 us  [local(): lax.all_to_all(send, 'inst', split_axis=0, concat_axis=0, tiled=True)]
    ppermute x1, waiting for transfers between devices: 0.01 us -> 1.48 us  [local(): down1 = lax.ppermute(down1, 'tp', shift(-1))]
    ppermute x1, starting transfers between devices: 2.67 us -> 1.38 us  [local(): down1 = lax.ppermute(down1, 'tp', shift(-1))]
    all_to_all x1, waiting for transfers between devices: 6.71 us -> 5.45 us  [local(): lax.all_to_all(slots.reshape(INST, STEPS * CAP, share), 'inst', split_axi...]
  transfers between devices with their start and end apart: 9 -> 9, of which waited for: 5 -> 7; matrix products, arithmetic and copies ran while one was open for 0% -> 0% of each run, Pallas kernels for 19% -> 19%
where the time goes in v5:
time: 74.3 us; the launch traced here: 74 us
  starting transfers between devices  27.4 us (37%)
  waiting for transfers between devices  27.2 us (37%)
  Pallas kernels  18.8 us (25%)
    all_to_all x1, starting transfers between devices, local(): lax.all_to_all(slots.reshape(INST, STEPS * CAP, share), 'inst', split_axi...  9.84 us
    pallas_call x1, Pallas kernels, local(): pl.pallas_call(attend_kernel, out_shape=(pltpu.VMEM((ROWS, share), BF16),...  9.73 us
    all_to_all x1, starting transfers between devices, local(): lax.all_to_all(send, 'inst', split_axis=0, concat_axis=0, tiled=True)  8.46 us
    all_to_all x1, waiting for transfers between devices, local(): lax.all_to_all(slots.reshape(INST, STEPS * CAP, share), 'inst', split_axi...  5.45 us
    ppermute x1, waiting for transfers between devices, local(): far1 = lax.ppermute(far1, 'tp', shift(1))  5.09 us
    ppermute x1, waiting for transfers between devices, local(): up0 = lax.ppermute(up0, 'tp', shift(1))  4.96 us
    ppermute x1, waiting for transfers between devices, local(): lax.ppermute(part, 'tp', [(s, (s + RING) % (2 * RING)) for s in range(2 *...  4.74 us
    pallas_call x1, Pallas kernels, local(): pl.pallas_call(pack_kernel, out_shape=(pltpu.HBM((INST * CAP, MAXP) + kv_...  3.57 us
  transfers between devices with their start and end apart: 9, of which 7 were waited for; matrix products, arithmetic and copies ran while one was open for 0% of the time, Pallas kernels for 19%

profile of v5, /device:TPU:1, one launch (start us, length us, event | category | flops | bytes accessed | tf_op | source)
XLA Modules:
  0.0 74.0 jit_solution(3362207163024058751)
XLA Ops:
  0.6 3.6 %pack_pages.1 = (bf16[32,3,2,64,128]{4,3,2,1,0:T(8,128)(2,1)}, bf16[256,128]{1,0:T(8,128)(2,1)S(1)}) custom-call(s32[3,32]{1,0:T(4,128)} %bitcast.14, s32[16]{0:T(128)} %req_list.1, s32[16]{0:T(128)} %bitcast.17, s32[16]{0:T(128)} %resume_list.1, bf16[96,2,64,128]{3,2,1,0:T(8,128)(2,1)} %pool.3), custom_call_target="tpu_custom_call" | custom-call | bytes 6291456 | tf_op jit(solution)/shard_map/pack_pages/pallas_call | solution.py:280
  4.2 8.5 %all-to-all-start = ((bf16[32,3,2,64,128]{4,3,2,1,0:T(8,128)(2,1)}), bf16[32,3,2,64,128]{4,3,2,1,0:T(8,128)(2,1)S(1)}, u32[]{:S(2)}, u32[]{:S(2)}) async-start(bf16[32,3,2,64,128]{4,3,2,1,0:T(8,128)(2,1)} %get-tuple-element.29), calls=%async_computation | async-start | bytes 6291456 | tf_op jit(solution)/shard_map/all_to_all | solution.py:306
  12.7 9.7 %attend.1 = (bf16[128,1024]{1,0:T(8,128)(2,1)S(1)}, bf16[128,1024]{1,0:T(8,128)(2,1)S(1)}, bf16[128,1024]{1,0:T(8,128)(2,1)S(1)}, bf16[128,1024]{1,0:T(8,128)(2,...) custom-call(bf16[128,8192]{1,0:T(8,128)(2,1)} %bitcast.10, ...), custom_call_target="tpu_custom_call" | custom-call | flops 2400000000 | bytes 25165824 | tf_op jit(solution)/shard_map/attend/pallas_call | solution.py:313
  22.4 1.7 %collective-permute-start.1 = (bf16[128,1024]{1,0:T(8,128)(2,1)S(1)}, bf16[128,1024]{1,0:T(8,128)(2,1)S(1)}, u32[]{:S(2)}, u32[]{:S(2)}) collective-permute-start(bf16[128,1024]{1,0:T(8,128)(2,1)S(1)} %get-tuple-element.22), channel_id=1, source_target_pairs={{0,1},{1,2},{2,3},{3,0},{4,5},{5,6},{6,7},{7,4},{8,9},{9,10},{10,1... | collective-permute-start | bytes 786440 | tf_op jit(solution)/shard_map/ppermute | solution.py:360
  24.2 2.2 %collective-permute-start.2 = (bf16[128,1024]{1,0:T(8,128)(2,1)S(1)}, bf16[128,1024]{1,0:T(8,128)(2,1)S(1)}, u32[]{:S(2)}, u32[]{:S(2)}) collective-permute-start(bf16[128,1024]{1,0:T(8,128)(2,1)S(1)} %get-tuple-element.23), channel_id=1, source_target_pairs={{0,3},{1,0},{2,1},{3,2},{4,7},{5,4},{6,5},{7,6},{8,11},{9,8},{10,9... | collective-permute-start | bytes 786440 | tf_op jit(solution)/shard_map/ppermute | solution.py:361
  26.3 1.4 %collective-permute-start.5 = (bf16[128,1024]{1,0:T(8,128)(2,1)S(1)}, bf16[128,1024]{1,0:T(8,128)(2,1)S(1)}, u32[]{:S(2)}, u32[]{:S(2)}) collective-permute-start(bf16[128,1024]{1,0:T(8,128)(2,1)S(1)} %get-tuple-element.26), channel_id=1, source_target_pairs={{0,3},{1,0},{2,1},{3,2},{4,7},{5,4},{6,5},{7,6},{8,11},{9,8},{10,9... | collective-permute-start | bytes 786440 | tf_op jit(solution)/shard_map/ppermute | solution.py:363
  27.7 5.1 %collective-permute-done.1.far1 = bf16[128,1024]{1,0:T(8,128)(2,1)S(1)} collective-permute-done((bf16[128,1024]{1,0:T(8,128)(2,1)S(1)}, bf16[128,1024]{1,0:T(8,128)(2,1)S(1)}, u32[]{:S(2)}, u32[]{:S(2)}) %collective-permute-start.1) | collective-permute-done | bytes 262176 | tf_op jit(solution)/shard_map/ppermute | solution.py:360
  32.8 0.0 collective-permute-done.2.far0
  32.8 0.1 relay.1
  32.9 0.6 collective-permute-start.4
  33.5 1.2 %collective-permute-start = (bf16[128,1024]{1,0:T(8,128)(2,1)S(1)}, bf16[128,1024]{1,0:T(8,128)(2,1)S(1)}, u32[]{:S(2)}, u32[]{:S(2)}) collective-permute-start(bf16[128,1024]{1,0:T(8,128)(2,1)S(1)} %get-tuple-element.19), channel_id=1, source_target_pairs={{0,1},{1,2},{2,3},{3,0},{4,5},{5,6},{6,7},{7,4},{8,9},{9,10},{10,1... | collective-permute-start | bytes 786440 | tf_op jit(solution)/shard_map/ppermute | solution.py:362
  34.7 1.4 %collective-permute-start.3 = (bf16[128,1024]{1,0:T(8,128)(2,1)S(1)}, bf16[128,1024]{1,0:T(8,128)(2,1)S(1)}, u32[]{:S(2)}, u32[]{:S(2)}) collective-permute-start(bf16[128,1024]{1,0:T(8,128)(2,1)S(1)} %get-tuple-element.24), channel_id=1, source_target_pairs={{0,3},{1,0},{2,1},{3,2},{4,7},{5,4},{6,5},{7,6},{8,11},{9,8},{10,9... | collective-permute-start | bytes 786440 | tf_op jit(solution)/shard_map/ppermute | solution.py:366
  36.2 1.5 %collective-permute-done.5.down1 = bf16[128,1024]{1,0:T(8,128)(2,1)S(1)} collective-permute-done((bf16[128,1024]{1,0:T(8,128)(2,1)S(1)}, bf16[128,1024]{1,0:T(8,128)(2,1)S(1)}, u32[]{:S(2)}, u32[]{:S(2)}) %collective-permute-start.5) | collective-permute-done | bytes 262176 | tf_op jit(solution)/shard_map/ppermute | solution.py:363
  37.7 3.3 %collective-permute-done.4.up1 = bf16[128,1024]{1,0:T(8,128)(2,1)S(1)} collective-permute-done((bf16[128,1024]{1,0:T(8,128)(2,1)S(1)}, bf16[128,1024]{1,0:T(8,128)(2,1)S(1)}, u32[]{:S(2)}, u32[]{:S(2)}) %collective-permute-start.4) | collective-permute-done | bytes 262176 | tf_op jit(solution)/shard_map/ppermute | solution.py:365
  41.0 0.1 sum_ring.1
  41.1 0.6 collective-permute-start.6
  41.6 5.0 %collective-permute-done.up0 = bf16[128,1024]{1,0:T(8,128)(2,1)S(1)} collective-permute-done((bf16[128,1024]{1,0:T(8,128)(2,1)S(1)}, bf16[128,1024]{1,0:T(8,128)(2,1)S(1)}, u32[]{:S(2)}, u32[]{:S(2)}) %collective-permute-start) | collective-permute-done | bytes 262176 | tf_op jit(solution)/shard_map/ppermute | solution.py:362
  46.6 0.0 collective-permute-done.3.down0
  46.6 4.7 %collective-permute-done.6.other = bf16[128,1024]{1,0:T(8,128)(2,1)S(1)} collective-permute-done((bf16[128,1024]{1,0:T(8,128)(2,1)S(1)}, bf16[128,1024]{1,0:T(8,128)(2,1)S(1)}, u32[]{:S(2)}, u32[]{:S(2)}) %collective-permute-start.6) | collective-permute-done | bytes 262176 | tf_op jit(solution)/shard_map/ppermute | solution.py:368
  51.3 1.1 %close.1 = (bf16[128,1024]{1,0:T(8,128)(2,1)}, bf16[128,1024]{1,0:T(8,128)(2,1)}) custom-call(bf16[2,128,1024]{2,1,0:T(8,128)(2,1)S(1)} %get-tuple-element.18.own, bf16[128,1024]{1,0:T(8,128)(2,1)S(1)} %collective-permute-done.up0, bf16[128,1024]{1,0:T(8,128)(2,1)S(1)} %collective-permute-done.3.down0, bf16[128,1024]{1,0:T(8,128)(2,1)S(1)} %collective-permute-done.6.other, ...), custom_call_target="tpu_custom_call" | custom-call | bytes 2097152 | tf_op jit(solution)/shard_map/close/pallas_call | solution.py:369
  52.4 2.2 %all-to-all-done.got = bf16[32,3,2,64,128]{4,3,2,1,0:T(8,128)(2,1)S(1)} async-done(((bf16[32,3,2,64,128]{4,3,2,1,0:T(8,128)(2,1)}), bf16[32,3,2,64,128]{4,3,2,1,0:T(8,128)(2,1)S(1)}, u32[]{:S(2)}, u32[]{:S(2)}) %all-to-all-start) | async-done | bytes 3145760 | tf_op jit(solution)/shard_map/all_to_all | solution.py:306
  54.6 9.8 %all-to-all-start.1 = ((bf16[16,8,1024]{2,1,0:T(8,128)(2,1)}), bf16[16,8,1024]{2,1,0:T(8,128)(2,1)S(1)}, u32[]{:S(2)}, u32[]{:S(2)}) async-start(bf16[16,8,1024]{2,1,0:T(8,128)(2,1)} %bitcast.11), calls=%async_computation.1 | async-start | bytes 524288 | tf_op jit(solution)/shard_map/all_to_all | solution.py:373
  64.4 3.2 %keep_pages.1 = bf16[32,3,2,64,128]{4,3,2,1,0:T(8,128)(2,1)} custom-call(bf16[32,3,2,64,128]{4,3,2,1,0:T(8,128)(2,1)S(1)} %all-to-all-done.got), custom_call_target="tpu_custom_call" | custom-call | bytes 6291456 | tf_op jit(solution)/shard_map/keep_pages/pallas_call | solution.py:378
  67.7 5.4 %all-to-all-done.1 = bf16[16,8,1024]{2,1,0:T(8,128)(2,1)S(1)} async-done(((bf16[16,8,1024]{2,1,0:T(8,128)(2,1)}), bf16[16,8,1024]{2,1,0:T(8,128)(2,1)S(1)}, u32[]{:S(2)}, u32[]{:S(2)}) %all-to-all-start.1) | async-done | bytes 262176 | tf_op jit(solution)/shard_map/all_to_all | solution.py:373
  73.1 0.9 %arrive.1 = bf16[128,1024]{1,0:T(8,128)(2,1)} custom-call(bf16[128,1024]{1,0:T(8,128)(2,1)S(1)} %bitcast.9), custom_call_target="tpu_custom_call" | custom-call | bytes 2097152 | tf_op jit(solution)/shard_map/arrive/pallas_call | solution.py:376
Async XLA Ops:
  4.2 50.4 %all-to-all-start = ((bf16[32,3,2,64,128]{4,3,2,1,0:T(8,128)(2,1)}), bf16[32,3,2,64,128]{4,3,2,1,0:T(8,128)(2,1)S(1)}, u32[]{:S(2)}, u32[]{:S(2)}) async-start(bf16[32,3,2,64,128]{4,3,2,1,0:T(8,128)(2,1)} %get-tuple-element.29), calls=%async_computation | async-start | bytes 6291456 | tf_op jit(solution)/shard_map/all_to_all | solution.py:306
  22.4 10.4 %collective-permute-start.1 = (bf16[128,1024]{1,0:T(8,128)(2,1)S(1)}, bf16[128,1024]{1,0:T(8,128)(2,1)S(1)}, u32[]{:S(2)}, u32[]{:S(2)}) collective-permute-start(bf16[128,1024]{1,0:T(8,128)(2,1)S(1)} %get-tuple-element.22), channel_id=1, source_target_pairs={{0,1},{1,2},{2,3},{3,0},{4,5},{5,6},{6,7},{7,4},{8,9},{9,10},{10,1... | collective-permute-start | bytes 786440 | tf_op jit(solution)/shard_map/ppermute | solution.py:360
  24.2 8.6 %collective-permute-start.2 = (bf16[128,1024]{1,0:T(8,128)(2,1)S(1)}, bf16[128,1024]{1,0:T(8,128)(2,1)S(1)}, u32[]{:S(2)}, u32[]{:S(2)}) collective-permute-start(bf16[128,1024]{1,0:T(8,128)(2,1)S(1)} %get-tuple-element.23), channel_id=1, source_target_pairs={{0,3},{1,0},{2,1},{3,2},{4,7},{5,4},{6,5},{7,6},{8,11},{9,8},{10,9... | collective-permute-start | bytes 786440 | tf_op jit(solution)/shard_map/ppermute | solution.py:361
  26.3 11.3 %collective-permute-start.5 = (bf16[128,1024]{1,0:T(8,128)(2,1)S(1)}, bf16[128,1024]{1,0:T(8,128)(2,1)S(1)}, u32[]{:S(2)}, u32[]{:S(2)}) collective-permute-start(bf16[128,1024]{1,0:T(8,128)(2,1)S(1)} %get-tuple-element.26), channel_id=1, source_target_pairs={{0,3},{1,0},{2,1},{3,2},{4,7},{5,4},{6,5},{7,6},{8,11},{9,8},{10,9... | collective-permute-start | bytes 786440 | tf_op jit(solution)/shard_map/ppermute | solution.py:363
  32.9 8.0 %collective-permute-start.4 = (bf16[128,1024]{1,0:T(8,128)(2,1)S(1)}, bf16[128,1024]{1,0:T(8,128)(2,1)S(1)}, u32[]{:S(2)}, u32[]{:S(2)}) collective-permute-start(bf16[128,1024]{1,0:T(8,128)(2,1)S(1)} %get-tuple-element.25), channel_id=1, source_target_pairs={{0,1},{1,2},{2,3},{3,0},{4,5},{5,6},{6,7},{7,4},{8,9},{9,10},{10,1... | collective-permute-start | bytes 786440 | tf_op jit(solution)/shard_map/ppermute | solution.py:365
  33.5 13.1 %collective-permute-start = (bf16[128,1024]{1,0:T(8,128)(2,1)S(1)}, bf16[128,1024]{1,0:T(8,128)(2,1)S(1)}, u32[]{:S(2)}, u32[]{:S(2)}) collective-permute-start(bf16[128,1024]{1,0:T(8,128)(2,1)S(1)} %get-tuple-element.19), channel_id=1, source_target_pairs={{0,1},{1,2},{2,3},{3,0},{4,5},{5,6},{6,7},{7,4},{8,9},{9,10},{10,1... | collective-permute-start | bytes 786440 | tf_op jit(solution)/shard_map/ppermute | solution.py:362
  34.7 11.8 %collective-permute-start.3 = (bf16[128,1024]{1,0:T(8,128)(2,1)S(1)}, bf16[128,1024]{1,0:T(8,128)(2,1)S(1)}, u32[]{:S(2)}, u32[]{:S(2)}) collective-permute-start(bf16[128,1024]{1,0:T(8,128)(2,1)S(1)} %get-tuple-element.24), channel_id=1, source_target_pairs={{0,3},{1,0},{2,1},{3,2},{4,7},{5,4},{6,5},{7,6},{8,11},{9,8},{10,9... | collective-permute-start | bytes 786440 | tf_op jit(solution)/shard_map/ppermute | solution.py:366
  41.1 10.3 %collective-permute-start.6 = (bf16[128,1024]{1,0:T(8,128)(2,1)S(1)}, bf16[128,1024]{1,0:T(8,128)(2,1)S(1)}, u32[]{:S(2)}, u32[]{:S(2)}) collective-permute-start(bf16[128,1024]{1,0:T(8,128)(2,1)S(1)} %sum_ring.1), channel_id=1, source_target_pairs={{0,4},{1,5},{2,6},{3,7},{4,0},{5,1},{6,2},{7,3},{8,12},{9,13},{10,... | collective-permute-start | bytes 786440 | tf_op jit(solution)/shard_map/ppermute | solution.py:368
  54.6 18.5 %all-to-all-start.1 = ((bf16[16,8,1024]{2,1,0:T(8,128)(2,1)}), bf16[16,8,1024]{2,1,0:T(8,128)(2,1)S(1)}, u32[]{:S(2)}, u32[]{:S(2)}) async-start(bf16[16,8,1024]{2,1,0:T(8,128)(2,1)} %bitcast.11), calls=%async_computation.1 | async-start | bytes 524288 | tf_op jit(solution)/shard_map/all_to_all | solution.py:373

commit v6 on v5

--- a/solution.py
+++ b/solution.py
@@ -69,6 +69,7 @@
         return carry
 
     lax.fori_loop(0, MIG, place, 0)
+    here_at = lax.axis_index("inst")
     rows = lax.broadcasted_iota(jnp.int32, (2 * ROWS, ROWS), 0)
     cols = lax.broadcasted_iota(jnp.int32, (2 * ROWS, ROWS), 1)
     wide[...] = jnp.where(rows == cols, 1.0, 0.0).astype(F32)
@@ -86,12 +87,16 @@
         count[d] = c + 1
         req = mreq[k]
         first = resume[k]
+        far = (d >> 3) ^ (here_at >> 3)
+        cross = (d ^ here_at) & 1
+        ahead = ((d >> 1) - (here_at >> 1)) & (RING - 1)
+        block = ROWS + far * (ROWS // 2) + cross * (ROWS // 4) + ahead * (STEPS * CAP)
         for t in range(STEPS):
             at = t * REQS + req
             here = jnp.where(lane == at, 1.0, 0.0).astype(F32)
             stay = jnp.where(t < first, 1.0, 0.0).astype(F32)
             wide[pl.ds(at, 1), :] = here * stay
-            wide[pl.ds(ROWS + d * (STEPS * CAP) + t * CAP + c, 1), :] = here * (1.0 - stay)
+            wide[pl.ds(block + t * CAP + c, 1), :] = here * (1.0 - stay)
         return carry
 
     lax.fori_loop(0, MIG, choose, 0)
@@ -244,25 +249,55 @@
     next_down[...] = (down0[...].astype(F32) + far0[...].astype(F32)).astype(BF16)
 
 
-def sum_kernel(own, up1, down1, out):
-    out[...] = (own[1].astype(F32) + up1[...].astype(F32) + down1[...].astype(F32)).astype(BF16)
-
-
-def close_kernel(own, up0, down0, other, pick, home, slots):
-    total = (
-        own[0].astype(F32) + up0[...].astype(F32) + down0[...].astype(F32) + other[...].astype(F32)
-    ).astype(BF16)
-    both = jnp.dot(pick[...], total, preferred_element_type=F32).astype(BF16)
-    home[...] = both[:ROWS]
-    slots[...] = both[ROWS:]
-
-
-def arrive_kernel(rows, out):
+def close_kernel(
+    own, up0, up1, down0, down1, pick, keep, pass_on, near0, near1, far0, far1
+):
+    choice = pick[ROWS:]
+    mine = (own[0].astype(F32) + up0[...].astype(F32) + down0[...].astype(F32)).astype(BF16)
+    other = (own[1].astype(F32) + up1[...].astype(F32) + down1[...].astype(F32)).astype(BF16)
+    keep[...] = mine
+    pass_on[...] = other
+    for part, near, far in ((mine, near0, far0), (other, near1, far1)):
+        taken = jnp.dot(choice, part, preferred_element_type=F32).astype(BF16)
+        near[...] = taken[:ROWS // 2]
+        far[...] = taken[ROWS // 2:]
+
+
+def home_kernel(keep, other, pick, home):
+    total = (keep[...].astype(F32) + other[...].astype(F32)).astype(BF16)
+    home[...] = jnp.dot(pick[:ROWS], total, preferred_element_type=F32).astype(BF16)
+
+
+def join_kernel(near0, near1, far0, far1, kept, same, cross):
+    near = (near0[...].astype(F32) + near1[...].astype(F32)).astype(BF16)
+    far = (far0[...].astype(F32) + far1[...].astype(F32)).astype(BF16)
+    to = lax.broadcasted_iota(jnp.int32, (ROWS, ROWS), 0)
+    come = lax.broadcasted_iota(jnp.int32, (ROWS, ROWS), 1)
+    source = ((to >> 3) & 1) * (ROWS // 2) + (to >> 4) * (STEPS * CAP) + (to & 7)
+    turn = jnp.where(come == source, 1.0, 0.0).astype(BF16)
+    rows = jnp.dot(turn, jnp.concatenate([near, far], axis=0), preferred_element_type=F32).astype(BF16)
+    same[...] = rows[:ROWS // 2]
+    cross[...] = rows[ROWS // 2:]
+
+
+def split_kernel(same, crossed, *ahead):
+    for k in range(RING):
+        ahead[k][:16] = same[k * 16:(k + 1) * 16]
+        ahead[k][16:] = crossed[k * 16:(k + 1) * 16]
+
+
+def arrive_kernel(k0, k1, k2, k3, out):
+    here_at = lax.axis_index("inst")
+    rows = jnp.concatenate([k0[...], k1[...], k2[...], k3[...]], axis=0)
     to = lax.broadcasted_iota(jnp.int32, (ROWS, ROWS), 0)
     come = lax.broadcasted_iota(jnp.int32, (ROWS, ROWS), 1)
     t, s, c = to >> 5, (to >> 1) & (INST - 1), to & (CAP - 1)
-    turn = jnp.where(come == s * (STEPS * CAP) + t * CAP + c, 1.0, 0.0).astype(BF16)
-    out[...] = jnp.dot(turn, rows[...], preferred_element_type=F32).astype(BF16)
+    behind = ((here_at >> 1) - (s >> 1)) & (RING - 1)
+    cross = (s ^ here_at) & 1
+    far = ((s ^ here_at) >> 3) & 1
+    source = behind * 32 + cross * 16 + far * 8 + t * CAP + c
+    turn = jnp.where(come == source, 1.0, 0.0).astype(BF16)
+    out[...] = jnp.dot(turn, rows, preferred_element_type=F32).astype(BF16)
 
 
 def copy_kernel(got, out):
@@ -348,10 +383,11 @@
     def shift(k):
         return [(s, (s // RING) * RING + (s + k) % RING) for s in range(2 * RING)]
 
-    def small(kernel, out, name):
+    def small(kernel, out, name, **specs):
         return pl.pallas_call(
             kernel,
             out_shape=out,
+            **specs,
             compiler_params=pltpu.CompilerParams(vmem_limit_bytes=SMALL_VMEM),
             cost_estimate=pl.CostEstimate(flops=0, bytes_accessed=2 << 20, transcendentals=0),
             name=name,
@@ -364,16 +400,19 @@
     next_up, next_down = small(relay_kernel, (piece,) * 2, "relay")(up1, down0, far1, far0)
     up1 = lax.ppermute(next_up, "tp", shift(1))
     down0 = lax.ppermute(next_down, "tp", shift(-1))
-    part = small(sum_kernel, piece, "sum_ring")(own, up1, down1)
-    other = lax.ppermute(part, "tp", [(s, (s + RING) % (2 * RING)) for s in range(2 * RING)])
-    home, slots = small(close_kernel, (piece, pltpu.HBM((ROWS, share), BF16)), "close")(
-        own, up0, down0, other, pick
-    )
-    arrival_cache, slots = lax.optimization_barrier((arrival_cache, slots))
-    rows = lax.all_to_all(
-        slots.reshape(INST, STEPS * CAP, share), "inst", split_axis=0, concat_axis=0, tiled=True
-    )
-    arrival = small(arrive_kernel, piece, "arrive")(rows.reshape(ROWS, share))
+    half_piece = jax.ShapeDtypeStruct((ROWS // 2, share), BF16)
+    keep, pass_on, near0, near1, far0, far1 = small(
+        close_kernel, (piece,) * 2 + (half_piece,) * 4, "close"
+    )(own, up0, up1, down0, down1, pick)
+    flip_y = [(s, (s + RING) % (2 * RING)) for s in range(2 * RING)]
+    flip_far = [(s, s ^ 8) for s in range(INST)]
+    both = [
+        (i * 2 * RING + s, (i ^ 8) * 2 * RING + (s + RING) % (2 * RING))
+        for i in range(INST) for s in range(2 * RING)
+    ]
+    far0 = lax.ppermute(far0, "inst", flip_far)
+    near1 = lax.ppermute(near1, "tp", flip_y)
+    far1 = lax.ppermute(far1, ("inst", "tp"), both)
     block = pl.BlockSpec((4,) + arrival_cache.shape[1:], lambda i: (i, 0, 0, 0, 0))
     arrival_cache = pl.pallas_call(
         copy_kernel,
@@ -385,6 +424,19 @@
         cost_estimate=pl.CostEstimate(flops=0, bytes_accessed=6 << 20, transcendentals=0),
         name="keep_pages",
     )(arrival_cache)
+    same, cross = small(join_kernel, (half_piece,) * 2, "join", in_specs=[VMEM] * 4 + [ANY])(near0, near1, far0, far1, hbm(arrival_cache))
+    other = lax.ppermute(pass_on, "tp", flip_y)
+    crossed = lax.ppermute(cross, "inst", [(s, s ^ 1) for s in range(INST)])
+    ahead = small(
+        split_kernel, (jax.ShapeDtypeStruct((ROWS // RING, share), BF16),) * RING, "split"
+    )(same, crossed)
+
+    def along(k):
+        return [(s, (s & 9) + (((s >> 1) + k) & (RING - 1)) * 2) for s in range(INST)]
+
+    ahead = [ahead[0]] + [lax.ppermute(ahead[k], "inst", along(k)) for k in range(1, RING)]
+    home = small(home_kernel, piece, "home")(keep, other, pick)
+    arrival = small(arrive_kernel, piece, "arrive")(*ahead)
     return (
         home.reshape(STEPS, REQS, share),
         arrival.reshape(STEPS, INST * CAP, share),

time: 74.3 us -> 71.1 us (0.957)
  waiting for transfers between devices: 27.2 us -> 18.9 us
  Pallas kernels: 18.8 us -> 21.9 us
  starting transfers between devices: 27.4 us -> 28.3 us
    ppermute x1 -> x8, starting transfers between devices: 0.55 us -> 10.5 us  [the longest x3 4.83 us: local(): lax.ppermute(ahead[k], 'inst', along(k))]
    all_to_all x1 -> x0, starting transfers between devices: 9.84 us -> none  [local(): lax.all_to_all(slots.reshape(INST, STEPS * CAP, share), 'inst', split_axi...]
    all_to_all x1 -> x0, waiting for transfers between devices: 5.45 us -> none  [local(): lax.all_to_all(slots.reshape(INST, STEPS * CAP, share), 'inst', split_axi...]
    pallas_call x3 -> x5, Pallas kernels: 2.12 us -> 5.26 us  [the longest x1 1.88 us: local(): home = small(home_kernel, piece, 'home')(keep, other, pick)]
    ppermute x1 -> x8, waiting for transfers between devices: 4.74 us -> 1.79 us  [the longest x1 0.99 us: local(): crossed = lax.ppermute(cross, 'inst', [(s, s ^ 1) for s in range(INST)])]
    all_to_all x1, waiting for transfers between devices: 2.17 us -> 4.93 us  [local(): lax.all_to_all(send, 'inst', split_axis=0, concat_axis=0, tiled=True)]
    ppermute x1, waiting for transfers between devices: 3.29 us -> 5.61 us  [local(): up1 = lax.ppermute(next_up, 'tp', shift(1))]
    ppermute x1, waiting for transfers between devices: 4.96 us -> 2.74 us  [local(): up0 = lax.ppermute(up0, 'tp', shift(1))]
  transfers between devices with their start and end apart: 9 -> 15, of which waited for: 7 -> 7; matrix products, arithmetic and copies ran while one was open for 0% -> 0% of each run, Pallas kernels for 19% -> 25%
where the time goes in v6:
time: 71.1 us; the launch traced here: 70.4 us
  starting transfers between devices  28.3 us (40%)
  Pallas kernels  21.9 us (31%)
  waiting for transfers between devices  18.9 us (27%)
    pallas_call x1, Pallas kernels, local(): pl.pallas_call(attend_kernel, out_shape=(pltpu.VMEM((ROWS, share), BF16),...  9.73 us
    all_to_all x1, starting transfers between devices, local(): lax.all_to_all(send, 'inst', split_axis=0, concat_axis=0, tiled=True)  8.46 us
    ppermute x1, waiting for transfers between devices, local(): up1 = lax.ppermute(next_up, 'tp', shift(1))  5.61 us
    all_to_all x1, waiting for transfers between devices, local(): lax.all_to_all(send, 'inst', split_axis=0, concat_axis=0, tiled=True)  4.93 us
    ppermute x3, starting transfers between devices, local(): lax.ppermute(ahead[k], 'inst', along(k))  4.83 us
    ppermute x1, waiting for transfers between devices, local(): far1 = lax.ppermute(far1, 'tp', shift(1))  3.8 us
    pallas_call x1, Pallas kernels, local(): pl.pallas_call(pack_kernel, out_shape=(pltpu.HBM((INST * CAP, MAXP) + kv_...  3.57 us
    ppermute x1, starting transfers between devices, local(): far0 = lax.ppermute(far0, 'inst', flip_far)  3.31 us
  transfers between devices with their start and end apart: 15, of which 7 were waited for; matrix products, arithmetic and copies ran while one was open for 0% of the time, Pallas kernels for 25%

profile of v6, /device:TPU:1, one launch (start us, length us, event | category | flops | bytes accessed | tf_op | source)
XLA Modules:
  0.0 70.4 jit_solution(15434321528365846422)
XLA Ops:
  0.6 3.6 %pack_pages.1 = (bf16[32,3,2,64,128]{4,3,2,1,0:T(8,128)(2,1)}, bf16[256,128]{1,0:T(8,128)(2,1)S(1)}) custom-call(s32[3,32]{1,0:T(4,128)} %bitcast.11, s32[16]{0:T(128)} %req_list.1, s32[16]{0:T(128)} %bitcast.14, s32[16]{0:T(128)} %resume_list.1, bf16[96,2,64,128]{3,2,1,0:T(8,128)(2,1)} %pool.3), custom_call_target="tpu_custom_call" | custom-call | bytes 6291456 | tf_op jit(solution)/shard_map/pack_pages/pallas_call | solution.py:315
  4.2 8.5 %all-to-all-start = ((bf16[32,3,2,64,128]{4,3,2,1,0:T(8,128)(2,1)}), bf16[32,3,2,64,128]{4,3,2,1,0:T(8,128)(2,1)S(1)}, u32[]{:S(2)}, u32[]{:S(2)}) async-start(bf16[32,3,2,64,128]{4,3,2,1,0:T(8,128)(2,1)} %get-tuple-element.42), calls=%async_computation | async-start | bytes 6291456 | tf_op jit(solution)/shard_map/all_to_all | solution.py:341
  12.7 9.7 %attend.1 = (bf16[128,1024]{1,0:T(8,128)(2,1)S(1)}, bf16[128,1024]{1,0:T(8,128)(2,1)S(1)}, bf16[128,1024]{1,0:T(8,128)(2,1)S(1)}, bf16[128,1024]{1,0:T(8,128)(2,...) custom-call(bf16[128,8192]{1,0:T(8,128)(2,1)} %bitcast.7, ...), custom_call_target="tpu_custom_call" | custom-call | flops 2400000000 | bytes 25165824 | tf_op jit(solution)/shard_map/attend/pallas_call | solution.py:348
  22.4 1.7 %collective-permute-start.1 = (bf16[128,1024]{1,0:T(8,128)(2,1)S(1)}, bf16[128,1024]{1,0:T(8,128)(2,1)S(1)}, u32[]{:S(2)}, u32[]{:S(2)}) collective-permute-start(bf16[128,1024]{1,0:T(8,128)(2,1)S(1)} %get-tuple-element.30), channel_id=1, source_target_pairs={{0,1},{1,2},{2,3},{3,0},{4,5},{5,6},{6,7},{7,4},{8,9},{9,10},{10,1... | collective-permute-start | bytes 786440 | tf_op jit(solution)/shard_map/ppermute | solution.py:396
  24.1 2.2 %collective-permute-start.2 = (bf16[128,1024]{1,0:T(8,128)(2,1)S(1)}, bf16[128,1024]{1,0:T(8,128)(2,1)S(1)}, u32[]{:S(2)}, u32[]{:S(2)}) collective-permute-start(bf16[128,1024]{1,0:T(8,128)(2,1)S(1)} %get-tuple-element.31), channel_id=1, source_target_pairs={{0,3},{1,0},{2,1},{3,2},{4,7},{5,4},{6,5},{7,6},{8,11},{9,8},{10,9... | collective-permute-start | bytes 786440 | tf_op jit(solution)/shard_map/ppermute | solution.py:397
  26.3 0.0 collective-permute-start
  26.3 2.7 %collective-permute-start.5 = (bf16[128,1024]{1,0:T(8,128)(2,1)S(1)}, bf16[128,1024]{1,0:T(8,128)(2,1)S(1)}, u32[]{:S(2)}, u32[]{:S(2)}) collective-permute-start(bf16[128,1024]{1,0:T(8,128)(2,1)S(1)} %get-tuple-element.34), channel_id=1, source_target_pairs={{0,3},{1,0},{2,1},{3,2},{4,7},{5,4},{6,5},{7,6},{8,11},{9,8},{10,9... | collective-permute-start | bytes 786440 | tf_op jit(solution)/shard_map/ppermute | solution.py:399
  29.0 3.8 %collective-permute-done.1.far1 = bf16[128,1024]{1,0:T(8,128)(2,1)S(1)} collective-permute-done((bf16[128,1024]{1,0:T(8,128)(2,1)S(1)}, bf16[128,1024]{1,0:T(8,128)(2,1)S(1)}, u32[]{:S(2)}, u32[]{:S(2)}) %collective-permute-start.1) | collective-permute-done | bytes 262176 | tf_op jit(solution)/shard_map/ppermute | solution.py:396
  32.8 0.1 relay.1
  32.9 0.6 collective-permute-start.3
  33.5 2.2 %collective-permute-start.4 = (bf16[128,1024]{1,0:T(8,128)(2,1)S(1)}, bf16[128,1024]{1,0:T(8,128)(2,1)S(1)}, u32[]{:S(2)}, u32[]{:S(2)}) collective-permute-start(bf16[128,1024]{1,0:T(8,128)(2,1)S(1)} %get-tuple-element.33), channel_id=1, source_target_pairs={{0,3},{1,0},{2,1},{3,2},{4,7},{5,4},{6,5},{7,6},{8,11},{9,8},{10,9... | collective-permute-start | bytes 786440 | tf_op jit(solution)/shard_map/ppermute | solution.py:402
  35.7 2.7 %collective-permute-done.up0 = bf16[128,1024]{1,0:T(8,128)(2,1)S(1)} collective-permute-done((bf16[128,1024]{1,0:T(8,128)(2,1)S(1)}, bf16[128,1024]{1,0:T(8,128)(2,1)S(1)}, u32[]{:S(2)}, u32[]{:S(2)}) %collective-permute-start) | collective-permute-done | bytes 262176 | tf_op jit(solution)/shard_map/ppermute | solution.py:398
  38.4 0.0 collective-permute-done.5.down1
  38.4 5.6 %collective-permute-done.3.up1 = bf16[128,1024]{1,0:T(8,128)(2,1)S(1)} collective-permute-done((bf16[128,1024]{1,0:T(8,128)(2,1)S(1)}, bf16[128,1024]{1,0:T(8,128)(2,1)S(1)}, u32[]{:S(2)}, u32[]{:S(2)}) %collective-permute-start.3) | collective-permute-done | bytes 262176 | tf_op jit(solution)/shard_map/ppermute | solution.py:401
  44.0 1.1 %close.1 = (bf16[128,1024]{1,0:T(8,128)(2,1)S(1)}, bf16[128,1024]{1,0:T(8,128)(2,1)}, bf16[64,1024]{1,0:T(8,128)(2,1)S(1)}, bf16[64,1024]{1,0:T(8,128)(2,1)}, bf...) custom-call(bf16[2,128,1024]{2,1,0:T(8,128)(2,1)S(1)} %get-tuple-element.26.own, ...), custom_call_target="tpu_custom_call" | custom-call | bytes 2097152 | tf_op jit(solution)/shard_map/close/pallas_call | solution.py:404
  45.2 0.7 copy-done
  45.8 0.4 collective-permute-start.7
  46.3 3.3 %collective-permute-start.8 = (bf16[64,1024]{1,0:T(8,128)(2,1)}, bf16[64,1024]{1,0:T(8,128)(2,1)}, u32[]{:S(2)}, u32[]{:S(2)}) collective-permute-start(bf16[64,1024]{1,0:T(8,128)(2,1)} %get-tuple-element.40), channel_id=1, source_target_pairs={{0,64},{8,72},{16,80},{24,88},{32,96},{40,104},{48,112},{56,120},{... | collective-permute-start | bytes 393224 | tf_op jit(solution)/shard_map/ppermute | solution.py:413
  49.6 0.1 collective-permute-start.9
  49.7 0.0 collective-permute-start.6
  49.7 4.9 %all-to-all-done.got = bf16[32,3,2,64,128]{4,3,2,1,0:T(8,128)(2,1)S(1)} async-done(((bf16[32,3,2,64,128]{4,3,2,1,0:T(8,128)(2,1)}), bf16[32,3,2,64,128]{4,3,2,1,0:T(8,128)(2,1)S(1)}, u32[]{:S(2)}, u32[]{:S(2)}) %all-to-all-start) | async-done | bytes 3145760 | tf_op jit(solution)/shard_map/all_to_all | solution.py:341
  54.6 3.2 %keep_pages.1.kept = bf16[32,3,2,64,128]{4,3,2,1,0:T(8,128)(2,1)} custom-call(bf16[32,3,2,64,128]{4,3,2,1,0:T(8,128)(2,1)S(1)} %all-to-all-done.got), custom_call_target="tpu_custom_call" | custom-call | bytes 6291456 | tf_op jit(solution)/shard_map/keep_pages/pallas_call | solution.py:417
  57.8 0.7 collective-permute-done.8.far0
  58.6 1.3 %join.1 = (bf16[64,1024]{1,0:T(8,128)(2,1)S(1)}, bf16[64,1024]{1,0:T(8,128)(2,1)S(1)}) custom-call(bf16[64,1024]{1,0:T(8,128)(2,1)S(1)} %copy-done.1, bf16[64,1024]{1,0:T(8,128)(2,1)} %collective-permute-done.7.near1, bf16[64,1024]{1,0:T(8,128)(2,1)} %collective-permute-done.8.far0, bf16[64,1024]{1,0:T(8,128)(2,1)} %collective-permute-done.9.far1, ...), custom_call_target="tpu_custom_call" | custom-call | bytes 2097152 | tf_op jit(solution)/shard_map/join/pallas_call | solution.py:427
  59.8 1.8 %collective-permute-start.10 = (bf16[64,1024]{1,0:T(8,128)(2,1)S(1)}, bf16[64,1024]{1,0:T(8,128)(2,1)S(1)}, u32[]{:S(2)}, u32[]{:S(2)}) collective-permute-start(bf16[64,1024]{1,0:T(8,128)(2,1)S(1)} %get-tuple-element.44), channel_id=1, source_target_pairs={{0,8},{8,0},{16,24},{24,16},{32,40},{40,32},{48,56},{56,48},{64,72... | collective-permute-start | bytes 393224 | tf_op jit(solution)/shard_map/ppermute | solution.py:429
  61.7 1.0 %collective-permute-done.10.crossed = bf16[64,1024]{1,0:T(8,128)(2,1)S(1)} collective-permute-done((bf16[64,1024]{1,0:T(8,128)(2,1)S(1)}, bf16[64,1024]{1,0:T(8,128)(2,1)S(1)}, u32[]{:S(2)}, u32[]{:S(2)}) %collective-permute-start.10) | collective-permute-done | bytes 131104 | tf_op jit(solution)/shard_map/ppermute | solution.py:429
  62.7 0.3 collective-permute-start.11
  63.0 2.5 %collective-permute-start.12 = (bf16[32,1024]{1,0:T(8,128)(2,1)S(1)}, bf16[32,1024]{1,0:T(8,128)(2,1)S(1)}, u32[]{:S(2)}, u32[]{:S(2)}) collective-permute-start(bf16[32,1024]{1,0:T(8,128)(2,1)S(1)} %get-tuple-element.47), channel_id=1, source_target_pairs={{0,32},{8,40},{16,48},{24,56},{32,0},{40,8},{48,16},{56,24},{64,96... | collective-permute-start | bytes 196616 | tf_op jit(solution)/shard_map/ppermute | solution.py:437
  65.5 2.0 %collective-permute-start.13 = (bf16[32,1024]{1,0:T(8,128)(2,1)S(1)}, bf16[32,1024]{1,0:T(8,128)(2,1)S(1)}, u32[]{:S(2)}, u32[]{:S(2)}) collective-permute-start(bf16[32,1024]{1,0:T(8,128)(2,1)S(1)} %get-tuple-element.48), channel_id=1, source_target_pairs={{0,48},{8,56},{16,0},{24,8},{32,16},{40,24},{48,32},{56,40},{64,11... | collective-permute-start | bytes 196616 | tf_op jit(solution)/shard_map/ppermute | solution.py:437
  67.5 1.9 %home.1 = bf16[128,1024]{1,0:T(8,128)(2,1)} custom-call(bf16[128,1024]{1,0:T(8,128)(2,1)S(1)} %get-tuple-element.36.keep, bf16[128,1024]{1,0:T(8,128)(2,1)} %collective-permute-done.6.other, bf16[256,128]{1,0:T(8,128)(2,1)S(1)} %get-tuple-element.35.pick), custom_call_target="tpu_custom_call" | custom-call | bytes 2097152 | tf_op jit(solution)/shard_map/home/pallas_call | solution.py:438
  69.4 0.1 collective-permute-done.13.k3
  69.5 0.9 %arrive.1 = bf16[128,1024]{1,0:T(8,128)(2,1)} custom-call(bf16[32,1024]{1,0:T(8,128)(2,1)S(1)} %get-tuple-element.45.k0, bf16[32,1024]{1,0:T(8,128)(2,1)S(1)} %collective-permute-done.11.k1, bf16[32,1024]{1,0:T(8,128)(2,1)S(1)} %collective-permute-done.12.k2, bf16[32,1024]{1,0:T(8,128)(2,1)S(1)} %collective-permute-done.13.k3), custom_call_target="tpu_custom_call" | custom-call | bytes 2097152 | tf_op jit(solution)/shard_map/arrive/pallas_call | solution.py:439
  (11 shorter events, 0.0 us)
Async XLA Ops:
  4.2 50.4 %all-to-all-start = ((bf16[32,3,2,64,128]{4,3,2,1,0:T(8,128)(2,1)}), bf16[32,3,2,64,128]{4,3,2,1,0:T(8,128)(2,1)S(1)}, u32[]{:S(2)}, u32[]{:S(2)}) async-start(bf16[32,3,2,64,128]{4,3,2,1,0:T(8,128)(2,1)} %get-tuple-element.42), calls=%async_computation | async-start | bytes 6291456 | tf_op jit(solution)/shard_map/all_to_all | solution.py:341
  22.4 10.4 %collective-permute-start.1 = (bf16[128,1024]{1,0:T(8,128)(2,1)S(1)}, bf16[128,1024]{1,0:T(8,128)(2,1)S(1)}, u32[]{:S(2)}, u32[]{:S(2)}) collective-permute-start(bf16[128,1024]{1,0:T(8,128)(2,1)S(1)} %get-tuple-element.30), channel_id=1, source_target_pairs={{0,1},{1,2},{2,3},{3,0},{4,5},{5,6},{6,7},{7,4},{8,9},{9,10},{10,1... | collective-permute-start | bytes 786440 | tf_op jit(solution)/shard_map/ppermute | solution.py:396
  24.1 8.7 %collective-permute-start.2 = (bf16[128,1024]{1,0:T(8,128)(2,1)S(1)}, bf16[128,1024]{1,0:T(8,128)(2,1)S(1)}, u32[]{:S(2)}, u32[]{:S(2)}) collective-permute-start(bf16[128,1024]{1,0:T(8,128)(2,1)S(1)} %get-tuple-element.31), channel_id=1, source_target_pairs={{0,3},{1,0},{2,1},{3,2},{4,7},{5,4},{6,5},{7,6},{8,11},{9,8},{10,9... | collective-permute-start | bytes 786440 | tf_op jit(solution)/shard_map/ppermute | solution.py:397
  26.3 12.1 %collective-permute-start = (bf16[128,1024]{1,0:T(8,128)(2,1)S(1)}, bf16[128,1024]{1,0:T(8,128)(2,1)S(1)}, u32[]{:S(2)}, u32[]{:S(2)}) collective-permute-start(bf16[128,1024]{1,0:T(8,128)(2,1)S(1)} %get-tuple-element.27), channel_id=1, source_target_pairs={{0,1},{1,2},{2,3},{3,0},{4,5},{5,6},{6,7},{7,4},{8,9},{9,10},{10,1... | collective-permute-start | bytes 786440 | tf_op jit(solution)/shard_map/ppermute | solution.py:398
  26.3 12.1 %collective-permute-start.5 = (bf16[128,1024]{1,0:T(8,128)(2,1)S(1)}, bf16[128,1024]{1,0:T(8,128)(2,1)S(1)}, u32[]{:S(2)}, u32[]{:S(2)}) collective-permute-start(bf16[128,1024]{1,0:T(8,128)(2,1)S(1)} %get-tuple-element.34), channel_id=1, source_target_pairs={{0,3},{1,0},{2,1},{3,2},{4,7},{5,4},{6,5},{7,6},{8,11},{9,8},{10,9... | collective-permute-start | bytes 786440 | tf_op jit(solution)/shard_map/ppermute | solution.py:399
  32.9 11.1 %collective-permute-start.3 = (bf16[128,1024]{1,0:T(8,128)(2,1)S(1)}, bf16[128,1024]{1,0:T(8,128)(2,1)S(1)}, u32[]{:S(2)}, u32[]{:S(2)}) collective-permute-start(bf16[128,1024]{1,0:T(8,128)(2,1)S(1)} %get-tuple-element.32), channel_id=1, source_target_pairs={{0,1},{1,2},{2,3},{3,0},{4,5},{5,6},{6,7},{7,4},{8,9},{9,10},{10,1... | collective-permute-start | bytes 786440 | tf_op jit(solution)/shard_map/ppermute | solution.py:401
  33.5 10.5 %collective-permute-start.4 = (bf16[128,1024]{1,0:T(8,128)(2,1)S(1)}, bf16[128,1024]{1,0:T(8,128)(2,1)S(1)}, u32[]{:S(2)}, u32[]{:S(2)}) collective-permute-start(bf16[128,1024]{1,0:T(8,128)(2,1)S(1)} %get-tuple-element.33), channel_id=1, source_target_pairs={{0,3},{1,0},{2,1},{3,2},{4,7},{5,4},{6,5},{7,6},{8,11},{9,8},{10,9... | collective-permute-start | bytes 786440 | tf_op jit(solution)/shard_map/ppermute | solution.py:402
  45.2 0.7 copy-start
  45.8 12.0 %collective-permute-start.7 = (bf16[64,1024]{1,0:T(8,128)(2,1)}, bf16[64,1024]{1,0:T(8,128)(2,1)}, u32[]{:S(2)}, u32[]{:S(2)}) collective-permute-start(bf16[64,1024]{1,0:T(8,128)(2,1)} %get-tuple-element.39), channel_id=1, source_target_pairs={{0,4},{1,5},{2,6},{3,7},{4,0},{5,1},{6,2},{7,3},{8,12},{9,13},{10,... | collective-permute-start | bytes 393224 | tf_op jit(solution)/shard_map/ppermute | solution.py:414
  46.3 12.3 %collective-permute-start.8 = (bf16[64,1024]{1,0:T(8,128)(2,1)}, bf16[64,1024]{1,0:T(8,128)(2,1)}, u32[]{:S(2)}, u32[]{:S(2)}) collective-permute-start(bf16[64,1024]{1,0:T(8,128)(2,1)} %get-tuple-element.40), channel_id=1, source_target_pairs={{0,64},{8,72},{16,80},{24,88},{32,96},{40,104},{48,112},{56,120},{... | collective-permute-start | bytes 393224 | tf_op jit(solution)/shard_map/ppermute | solution.py:413
  49.6 9.0 %collective-permute-start.9 = (bf16[64,1024]{1,0:T(8,128)(2,1)}, bf16[64,1024]{1,0:T(8,128)(2,1)}, u32[]{:S(2)}, u32[]{:S(2)}) collective-permute-start(bf16[64,1024]{1,0:T(8,128)(2,1)} %get-tuple-element.41), channel_id=1, source_target_pairs={{0,68},{1,69},{2,70},{3,71},{4,64},{5,65},{6,66},{7,67},{8,76},{9,... | collective-permute-start | bytes 393224 | tf_op jit(solution)/shard_map/ppermute | solution.py:415
  49.7 17.8 %collective-permute-start.6 = (bf16[128,1024]{1,0:T(8,128)(2,1)}, bf16[128,1024]{1,0:T(8,128)(2,1)}, u32[]{:S(2)}, u32[]{:S(2)}) collective-permute-start(bf16[128,1024]{1,0:T(8,128)(2,1)} %get-tuple-element.37), channel_id=1, source_target_pairs={{0,4},{1,5},{2,6},{3,7},{4,0},{5,1},{6,2},{7,3},{8,12},{9,13},{10,... | collective-permute-start | bytes 786440 | tf_op jit(solution)/shard_map/ppermute | solution.py:428
  54.6 3.9 %copy-start.1 = (bf16[64,1024]{1,0:T(8,128)(2,1)S(1)}, bf16[64,1024]{1,0:T(8,128)(2,1)}, u32[]{:S(2)}) copy-start(bf16[64,1024]{1,0:T(8,128)(2,1)} %copy-done) | copy-start | bytes 393220
  59.8 2.8 %collective-permute-start.10 = (bf16[64,1024]{1,0:T(8,128)(2,1)S(1)}, bf16[64,1024]{1,0:T(8,128)(2,1)S(1)}, u32[]{:S(2)}, u32[]{:S(2)}) collective-permute-start(bf16[64,1024]{1,0:T(8,128)(2,1)S(1)} %get-tuple-element.44), channel_id=1, source_target_pairs={{0,8},{8,0},{16,24},{24,16},{32,40},{40,32},{48,56},{56,48},{64,72... | collective-permute-start | bytes 393224 | tf_op jit(solution)/shard_map/ppermute | solution.py:429
  62.7 6.7 %collective-permute-start.11 = (bf16[32,1024]{1,0:T(8,128)(2,1)S(1)}, bf16[32,1024]{1,0:T(8,128)(2,1)S(1)}, u32[]{:S(2)}, u32[]{:S(2)}) collective-permute-start(bf16[32,1024]{1,0:T(8,128)(2,1)S(1)} %get-tuple-element.46), channel_id=1, source_target_pairs={{0,16},{8,24},{16,32},{24,40},{32,48},{40,56},{48,0},{56,8},{64,80... | collective-permute-start | bytes 196616 | tf_op jit(solution)/shard_map/ppermute | solution.py:437
  63.0 6.4 %collective-permute-start.12 = (bf16[32,1024]{1,0:T(8,128)(2,1)S(1)}, bf16[32,1024]{1,0:T(8,128)(2,1)S(1)}, u32[]{:S(2)}, u32[]{:S(2)}) collective-permute-start(bf16[32,1024]{1,0:T(8,128)(2,1)S(1)} %get-tuple-element.47), channel_id=1, source_target_pairs={{0,32},{8,40},{16,48},{24,56},{32,0},{40,8},{48,16},{56,24},{64,96... | collective-permute-start | bytes 196616 | tf_op jit(solution)/shard_map/ppermute | solution.py:437
  65.5 4.0 %collective-permute-start.13 = (bf16[32,1024]{1,0:T(8,128)(2,1)S(1)}, bf16[32,1024]{1,0:T(8,128)(2,1)S(1)}, u32[]{:S(2)}, u32[]{:S(2)}) collective-permute-start(bf16[32,1024]{1,0:T(8,128)(2,1)S(1)} %get-tuple-element.48), channel_id=1, source_target_pairs={{0,48},{8,56},{16,0},{24,8},{32,16},{40,24},{48,32},{56,40},{64,11... | collective-permute-start | bytes 196616 | tf_op jit(solution)/shard_map/ppermute | solution.py:437

commit v7 on v6

--- a/solution.py
+++ b/solution.py
@@ -21,6 +21,7 @@
 SPAN = MAXP * PAGE
 ROWS = STEPS * REQS
 WIDE = 256
+LANES = 8
 ROPE_BASE = 500000.0
 FULL_VMEM = 48 << 20
 SMALL_VMEM = 6 << 20
@@ -33,10 +34,13 @@
 
 def pack_kernel(
     page_list, req_list, dest_list, resume_list, pool, send, pick,
-    table, mreq, mdest, resume, slot_req, count, kv, zeros, wide, kv_sem, sem, small_sem,
+    table, mreq, mdest, resume, slot_of, filled, count, kv, zeros, wide, kv_sem, sem, small_sem,
 ):
-    load = pltpu.make_async_copy(pool, kv, kv_sem)
-    load.start()
+    size = pool.shape[0] // LANES
+    load = [
+        pltpu.make_async_copy(pool.at[pl.ds(i * size, size)], kv.at[pl.ds(i * size, size)], kv_sem.at[i])
+        for i in range(LANES)
+    ]
     small = [
         pltpu.make_async_copy(source, target, small_sem.at[i])
         for i, (source, target) in enumerate((
@@ -45,46 +49,44 @@
     ]
     for copy in small:
         copy.start()
+    for copy in load:
+        copy.start()
     zeros[...] = jnp.zeros_like(zeros)
-
-    def clear(s, carry):
-        slot_req[s] = -1
-        return carry
-
-    def fresh(d, carry):
+    for s in range(INST * CAP):
+        filled[s] = 0
+    for d in range(INST):
         count[d] = 0
-        return carry
-
-    lax.fori_loop(0, INST * CAP, clear, 0)
-    lax.fori_loop(0, INST, fresh, 0)
-
     for copy in small:
         copy.wait()
-
-    def place(k, carry):
+    for k in range(MIG):
         d = mdest[k]
         c = count[d]
         count[d] = c + 1
-        slot_req[d * CAP + c] = mreq[k]
+        slot_of[k] = d * CAP + c
+        filled[d * CAP + c] = 1
+
+    def clear(s, carry):
+        @pl.when(filled[s] == 0)
+        def _():
+            pltpu.make_async_copy(zeros, send.at[s], sem).start()
+
         return carry
 
-    lax.fori_loop(0, MIG, place, 0)
+    lax.fori_loop(0, INST * CAP, clear, 0)
+    for copy in load:
+        copy.wait()
+    for k in range(MIG):
+        for p in range(MAXP):
+            pltpu.make_async_copy(kv.at[table[p, mreq[k]]], send.at[slot_of[k], p], sem).start()
+
     here_at = lax.axis_index("inst")
     rows = lax.broadcasted_iota(jnp.int32, (2 * ROWS, ROWS), 0)
     cols = lax.broadcasted_iota(jnp.int32, (2 * ROWS, ROWS), 1)
     wide[...] = jnp.where(rows == cols, 1.0, 0.0).astype(F32)
     lane = lax.broadcasted_iota(jnp.int32, (1, ROWS), 1)
-
-    def clear_count(d, carry):
-        count[d] = 0
-        return carry
-
-    lax.fori_loop(0, INST, clear_count, 0)
-
-    def choose(k, carry):
-        d = mdest[k]
-        c = count[d]
-        count[d] = c + 1
+    for k in range(MIG):
+        slot = slot_of[k]
+        d, c = slot >> 1, slot & 1
         req = mreq[k]
         first = resume[k]
         far = (d >> 3) ^ (here_at >> 3)
@@ -93,32 +95,9 @@
         block = ROWS + far * (ROWS // 2) + cross * (ROWS // 4) + ahead * (STEPS * CAP)
         for t in range(STEPS):
             at = t * REQS + req
-            here = jnp.where(lane == at, 1.0, 0.0).astype(F32)
-            stay = jnp.where(t < first, 1.0, 0.0).astype(F32)
-            wide[pl.ds(at, 1), :] = here * stay
-            wide[pl.ds(block + t * CAP + c, 1), :] = here * (1.0 - stay)
-        return carry
-
-    lax.fori_loop(0, MIG, choose, 0)
+            wide[pl.ds(at, 1), :] = jnp.where((lane == at) & (t < first), 1.0, 0.0).astype(F32)
+            wide[pl.ds(block + t * CAP + c, 1), :] = jnp.where((lane == at) & (t >= first), 1.0, 0.0).astype(F32)
     pick[...] = wide[...].astype(BF16)
-    load.wait()
-
-    def ship(s, carry):
-        req = slot_req[s]
-
-        @pl.when(req >= 0)
-        def _():
-            for p in range(MAXP):
-                pltpu.make_async_copy(kv.at[table[p, req]], send.at[s, p], sem).start()
-
-        @pl.when(req < 0)
-        def _():
-            pltpu.make_async_copy(zeros, send.at[s], sem).start()
-
-        return carry
-
-    lax.fori_loop(0, INST * CAP, ship, 0)
-
     pltpu.make_async_copy(send, send, sem).wait()
 
 
@@ -268,7 +247,7 @@
     home[...] = jnp.dot(pick[:ROWS], total, preferred_element_type=F32).astype(BF16)
 
 
-def join_kernel(near0, near1, far0, far1, kept, same, cross):
+def join_kernel(near0, near1, far0, far1, same, cross):
     near = (near0[...].astype(F32) + near1[...].astype(F32)).astype(BF16)
     far = (far0[...].astype(F32) + far1[...].astype(F32)).astype(BF16)
     to = lax.broadcasted_iota(jnp.int32, (ROWS, ROWS), 0)
@@ -286,7 +265,7 @@
         ahead[k][16:] = crossed[k * 16:(k + 1) * 16]
 
 
-def arrive_kernel(k0, k1, k2, k3, out):
+def arrive_kernel(k0, k1, k2, k3, kept, out):
     here_at = lax.axis_index("inst")
     rows = jnp.concatenate([k0[...], k1[...], k2[...], k3[...]], axis=0)
     to = lax.broadcasted_iota(jnp.int32, (ROWS, ROWS), 0)
@@ -300,8 +279,16 @@
     out[...] = jnp.dot(turn, rows, preferred_element_type=F32).astype(BF16)
 
 
-def copy_kernel(got, out):
-    out[...] = got[...]
+def keep_kernel(got, after, out, sem):
+    size = got.shape[0] // LANES
+    copies = [
+        pltpu.make_async_copy(got.at[pl.ds(i * size, size)], out.at[pl.ds(i * size, size)], sem.at[i])
+        for i in range(LANES)
+    ]
+    for copy in copies:
+        copy.start()
+    for copy in copies:
+        copy.wait()
 
 
 def local(
@@ -325,12 +312,13 @@
             pltpu.SMEM((MIG,), jnp.int32),
             pltpu.SMEM((MIG,), jnp.int32),
             pltpu.SMEM((MIG,), jnp.int32),
+            pltpu.SMEM((MIG,), jnp.int32),
             pltpu.SMEM((INST * CAP,), jnp.int32),
             pltpu.SMEM((INST,), jnp.int32),
             pltpu.VMEM(kv_pool.shape, BF16),
             pltpu.VMEM((MAXP,) + kv_pool.shape[1:], BF16),
             pltpu.VMEM((2 * ROWS, ROWS), F32),
-            pltpu.SemaphoreType.DMA,
+            pltpu.SemaphoreType.DMA((LANES,)),
             pltpu.SemaphoreType.DMA,
             pltpu.SemaphoreType.DMA((4,)),
         ],
@@ -413,18 +401,7 @@
     far0 = lax.ppermute(far0, "inst", flip_far)
     near1 = lax.ppermute(near1, "tp", flip_y)
     far1 = lax.ppermute(far1, ("inst", "tp"), both)
-    block = pl.BlockSpec((4,) + arrival_cache.shape[1:], lambda i: (i, 0, 0, 0, 0))
-    arrival_cache = pl.pallas_call(
-        copy_kernel,
-        out_shape=jax.ShapeDtypeStruct(arrival_cache.shape, BF16),
-        grid=(INST * CAP // 4,),
-        in_specs=[block],
-        out_specs=block,
-        compiler_params=pltpu.CompilerParams(vmem_limit_bytes=SMALL_VMEM),
-        cost_estimate=pl.CostEstimate(flops=0, bytes_accessed=6 << 20, transcendentals=0),
-        name="keep_pages",
-    )(arrival_cache)
-    same, cross = small(join_kernel, (half_piece,) * 2, "join", in_specs=[VMEM] * 4 + [ANY])(near0, near1, far0, far1, hbm(arrival_cache))
+    same, cross = small(join_kernel, (half_piece,) * 2, "join")(near0, near1, far0, far1)
     other = lax.ppermute(pass_on, "tp", flip_y)
     crossed = lax.ppermute(cross, "inst", [(s, s ^ 1) for s in range(INST)])
     ahead = small(
@@ -436,7 +413,11 @@
 
     ahead = [ahead[0]] + [lax.ppermute(ahead[k], "inst", along(k)) for k in range(1, RING)]
     home = small(home_kernel, piece, "home")(keep, other, pick)
-    arrival = small(arrive_kernel, piece, "arrive")(*ahead)
+    arrival_cache = small(
+        keep_kernel, pltpu.HBM(arrival_cache.shape, BF16), "keep_pages",
+        in_specs=[ANY] * 2, out_specs=ANY, scratch_shapes=[pltpu.SemaphoreType.DMA((LANES,))],
+    )(arrival_cache, hbm(home))
+    arrival = small(arrive_kernel, piece, "arrive", in_specs=[VMEM] * RING + [ANY])(*ahead, hbm(arrival_cache))
     return (
         home.reshape(STEPS, REQS, share),
         arrival.reshape(STEPS, INST * CAP, share),

time: 71.1 us -> 69.9 us (0.983)
  waiting for transfers between devices: 18.9 us -> 23.1 us
  Pallas kernels: 21.9 us -> 18 us
    all_to_all x1, waiting for transfers between devices: 4.93 us -> 0.01 us  [local(): lax.all_to_all(send, 'inst', split_axis=0, concat_axis=0, tiled=True)]
    ppermute x1, waiting for transfers between devices: 0.01 us -> 4.82 us  [local(): near1 = lax.ppermute(near1, 'tp', flip_y)]
    ppermute x1, waiting for transfers between devices: 0.7 us -> 5.1 us  [local(): far0 = lax.ppermute(far0, 'inst', flip_far)]
    pallas_call x3, Pallas kernels: 5.43 us -> 2.91 us  [the longest x1 1.72 us: local(): small(keep_kernel, pltpu.HBM(arrival_cache.shape, BF16), 'keep_pages', in...]
    ppermute x1, starting transfers between devices: 1.82 us -> 0.78 us  [local(): crossed = lax.ppermute(cross, 'inst', [(s, s ^ 1) for s in range(INST)])]
    pallas_call x1, Pallas kernels: 1.88 us -> 0.94 us  [local(): home = small(home_kernel, piece, 'home')(keep, other, pick)]
    pallas_call x1, Pallas kernels: 1.14 us -> 0.42 us  [local(): small(close_kernel, (piece,) * 2 + (half_piece,) * 4, 'close')]
  transfers between devices with their start and end apart: 15 -> 15, of which waited for: 7 -> 6; matrix products, arithmetic and copies ran while one was open for 0% -> 0% of each run, Pallas kernels for 25% -> 20%
where the time goes in v7:
time: 69.9 us; the launch traced here: 69.8 us
  starting transfers between devices  27.9 us (40%)
  waiting for transfers between devices  23.1 us (33%)
  Pallas kernels  18 us (26%)
  between operations  0.71 us (1%)
    pallas_call x1, Pallas kernels, local(): pl.pallas_call(attend_kernel, out_shape=(pltpu.VMEM((ROWS, share), BF16),...  9.74 us
    all_to_all x1, starting transfers between devices, local(): lax.all_to_all(send, 'inst', split_axis=0, concat_axis=0, tiled=True)  8.46 us
    ppermute x1, waiting for transfers between devices, local(): up1 = lax.ppermute(next_up, 'tp', shift(1))  5.61 us
    ppermute x3, starting transfers between devices, local(): lax.ppermute(ahead[k], 'inst', along(k))  5.4 us
    ppermute x1, waiting for transfers between devices, local(): far0 = lax.ppermute(far0, 'inst', flip_far)  5.1 us
    ppermute x1, waiting for transfers between devices, local(): near1 = lax.ppermute(near1, 'tp', flip_y)  4.82 us
    ppermute x1, waiting for transfers between devices, local(): far1 = lax.ppermute(far1, 'tp', shift(1))  3.79 us
    ppermute x1, starting transfers between devices, local(): far0 = lax.ppermute(far0, 'inst', flip_far)  3.32 us
  transfers between devices with their start and end apart: 15, of which 6 were waited for; matrix products, arithmetic and copies ran while one was open for 0% of the time, Pallas kernels for 20%

profile of v7, /device:TPU:1, one launch (start us, length us, event | category | flops | bytes accessed | tf_op | source)
XLA Modules:
  0.0 69.8 jit_solution(2375937268950180044)
XLA Ops:
  0.6 3.3 %pack_pages.1 = (bf16[32,3,2,64,128]{4,3,2,1,0:T(8,128)(2,1)}, bf16[256,128]{1,0:T(8,128)(2,1)S(1)}) custom-call(s32[3,32]{1,0:T(4,128)} %bitcast.11, s32[16]{0:T(128)} %req_list.1, s32[16]{0:T(128)} %bitcast.14, s32[16]{0:T(128)} %resume_list.1, bf16[96,2,64,128]{3,2,1,0:T(8,128)(2,1)} %pool.3), custom_call_target="tpu_custom_call" | custom-call | bytes 6291456 | tf_op jit(solution)/shard_map/pack_pages/pallas_call | solution.py:302
  3.9 8.5 %all-to-all-start = ((bf16[32,3,2,64,128]{4,3,2,1,0:T(8,128)(2,1)}), bf16[32,3,2,64,128]{4,3,2,1,0:T(8,128)(2,1)S(1)}, u32[]{:S(2)}, u32[]{:S(2)}) async-start(bf16[32,3,2,64,128]{4,3,2,1,0:T(8,128)(2,1)} %get-tuple-element.48), calls=%async_computation | async-start | bytes 6291456 | tf_op jit(solution)/shard_map/all_to_all | solution.py:329
  12.4 9.7 %attend.1 = (bf16[128,1024]{1,0:T(8,128)(2,1)S(1)}, bf16[128,1024]{1,0:T(8,128)(2,1)S(1)}, bf16[128,1024]{1,0:T(8,128)(2,1)S(1)}, bf16[128,1024]{1,0:T(8,128)(2,...) custom-call(bf16[128,8192]{1,0:T(8,128)(2,1)} %bitcast.7, ...), custom_call_target="tpu_custom_call" | custom-call | flops 2400000000 | bytes 25165824 | tf_op jit(solution)/shard_map/attend/pallas_call | solution.py:336
  22.1 1.7 %collective-permute-start.1 = (bf16[128,1024]{1,0:T(8,128)(2,1)S(1)}, bf16[128,1024]{1,0:T(8,128)(2,1)S(1)}, u32[]{:S(2)}, u32[]{:S(2)}) collective-permute-start(bf16[128,1024]{1,0:T(8,128)(2,1)S(1)} %get-tuple-element.30), channel_id=1, source_target_pairs={{0,1},{1,2},{2,3},{3,0},{4,5},{5,6},{6,7},{7,4},{8,9},{9,10},{10,1... | collective-permute-start | bytes 786440 | tf_op jit(solution)/shard_map/ppermute | solution.py:384
  23.8 2.2 %collective-permute-start.2 = (bf16[128,1024]{1,0:T(8,128)(2,1)S(1)}, bf16[128,1024]{1,0:T(8,128)(2,1)S(1)}, u32[]{:S(2)}, u32[]{:S(2)}) collective-permute-start(bf16[128,1024]{1,0:T(8,128)(2,1)S(1)} %get-tuple-element.31), channel_id=1, source_target_pairs={{0,3},{1,0},{2,1},{3,2},{4,7},{5,4},{6,5},{7,6},{8,11},{9,8},{10,9... | collective-permute-start | bytes 786440 | tf_op jit(solution)/shard_map/ppermute | solution.py:385
  26.0 0.0 collective-permute-start
  26.0 2.7 %collective-permute-start.5 = (bf16[128,1024]{1,0:T(8,128)(2,1)S(1)}, bf16[128,1024]{1,0:T(8,128)(2,1)S(1)}, u32[]{:S(2)}, u32[]{:S(2)}) collective-permute-start(bf16[128,1024]{1,0:T(8,128)(2,1)S(1)} %get-tuple-element.34), channel_id=1, source_target_pairs={{0,3},{1,0},{2,1},{3,2},{4,7},{5,4},{6,5},{7,6},{8,11},{9,8},{10,9... | collective-permute-start | bytes 786440 | tf_op jit(solution)/shard_map/ppermute | solution.py:387
  28.7 3.8 %collective-permute-done.1.far1 = bf16[128,1024]{1,0:T(8,128)(2,1)S(1)} collective-permute-done((bf16[128,1024]{1,0:T(8,128)(2,1)S(1)}, bf16[128,1024]{1,0:T(8,128)(2,1)S(1)}, u32[]{:S(2)}, u32[]{:S(2)}) %collective-permute-start.1) | collective-permute-done | bytes 262176 | tf_op jit(solution)/shard_map/ppermute | solution.py:384
  32.5 0.1 relay.1
  32.6 0.6 collective-permute-start.3
  33.2 2.2 %collective-permute-start.4 = (bf16[128,1024]{1,0:T(8,128)(2,1)S(1)}, bf16[128,1024]{1,0:T(8,128)(2,1)S(1)}, u32[]{:S(2)}, u32[]{:S(2)}) collective-permute-start(bf16[128,1024]{1,0:T(8,128)(2,1)S(1)} %get-tuple-element.33), channel_id=1, source_target_pairs={{0,3},{1,0},{2,1},{3,2},{4,7},{5,4},{6,5},{7,6},{8,11},{9,8},{10,9... | collective-permute-start | bytes 786440 | tf_op jit(solution)/shard_map/ppermute | solution.py:390
  35.4 2.7 %collective-permute-done.up0 = bf16[128,1024]{1,0:T(8,128)(2,1)S(1)} collective-permute-done((bf16[128,1024]{1,0:T(8,128)(2,1)S(1)}, bf16[128,1024]{1,0:T(8,128)(2,1)S(1)}, u32[]{:S(2)}, u32[]{:S(2)}) %collective-permute-start) | collective-permute-done | bytes 262176 | tf_op jit(solution)/shard_map/ppermute | solution.py:386
  38.1 0.0 collective-permute-done.5.down1
  38.1 5.6 %collective-permute-done.3.up1 = bf16[128,1024]{1,0:T(8,128)(2,1)S(1)} collective-permute-done((bf16[128,1024]{1,0:T(8,128)(2,1)S(1)}, bf16[128,1024]{1,0:T(8,128)(2,1)S(1)}, u32[]{:S(2)}, u32[]{:S(2)}) %collective-permute-start.3) | collective-permute-done | bytes 262176 | tf_op jit(solution)/shard_map/ppermute | solution.py:389
  43.7 0.4 close.1
  44.2 0.5 collective-permute-start.7
  44.6 3.3 %collective-permute-start.8 = (bf16[64,1024]{1,0:T(8,128)(2,1)S(1)}, bf16[64,1024]{1,0:T(8,128)(2,1)S(1)}, u32[]{:S(2)}, u32[]{:S(2)}) collective-permute-start(bf16[64,1024]{1,0:T(8,128)(2,1)S(1)} %get-tuple-element.40), channel_id=1, source_target_pairs={{0,64},{8,72},{16,80},{24,88},{32,96},{40,104},{48,112},{56,120},{... | collective-permute-start | bytes 393224 | tf_op jit(solution)/shard_map/ppermute | solution.py:401
  47.9 0.2 collective-permute-start.9
  48.1 0.0 collective-permute-start.6
  48.1 4.8 %collective-permute-done.7.near1 = bf16[64,1024]{1,0:T(8,128)(2,1)S(1)} collective-permute-done((bf16[64,1024]{1,0:T(8,128)(2,1)S(1)}, bf16[64,1024]{1,0:T(8,128)(2,1)S(1)}, u32[]{:S(2)}, u32[]{:S(2)}) %collective-permute-start.7) | collective-permute-done | bytes 131104 | tf_op jit(solution)/shard_map/ppermute | solution.py:402
  52.9 5.1 %collective-permute-done.8.far0 = bf16[64,1024]{1,0:T(8,128)(2,1)S(1)} collective-permute-done((bf16[64,1024]{1,0:T(8,128)(2,1)S(1)}, bf16[64,1024]{1,0:T(8,128)(2,1)S(1)}, u32[]{:S(2)}, u32[]{:S(2)}) %collective-permute-start.8) | collective-permute-done | bytes 131104 | tf_op jit(solution)/shard_map/ppermute | solution.py:401
  58.0 0.0 collective-permute-done.9.far1
  58.0 0.2 join.1
  58.3 0.8 %collective-permute-start.10 = (bf16[64,1024]{1,0:T(8,128)(2,1)S(1)}, bf16[64,1024]{1,0:T(8,128)(2,1)S(1)}, u32[]{:S(2)}, u32[]{:S(2)}) collective-permute-start(bf16[64,1024]{1,0:T(8,128)(2,1)S(1)} %get-tuple-element.43), channel_id=1, source_target_pairs={{0,8},{8,0},{16,24},{24,16},{32,40},{40,32},{48,56},{56,48},{64,72... | collective-permute-start | bytes 393224 | tf_op jit(solution)/shard_map/ppermute | solution.py:406
  59.0 1.0 %collective-permute-done.10.crossed = bf16[64,1024]{1,0:T(8,128)(2,1)S(1)} collective-permute-done((bf16[64,1024]{1,0:T(8,128)(2,1)S(1)}, bf16[64,1024]{1,0:T(8,128)(2,1)S(1)}, u32[]{:S(2)}, u32[]{:S(2)}) %collective-permute-start.10) | collective-permute-done | bytes 131104 | tf_op jit(solution)/shard_map/ppermute | solution.py:406
  60.0 0.7 split.1
  60.7 0.5 collective-permute-start.11
  61.2 2.9 %collective-permute-start.12 = (bf16[32,1024]{1,0:T(8,128)(2,1)}, bf16[32,1024]{1,0:T(8,128)(2,1)S(1)}, u32[]{:S(2)}, u32[]{:S(2)}) collective-permute-start(bf16[32,1024]{1,0:T(8,128)(2,1)} %get-tuple-element.46), channel_id=1, source_target_pairs={{0,32},{8,40},{16,48},{24,56},{32,0},{40,8},{48,16},{56,24},{64,96... | collective-permute-start | bytes 196616 | tf_op jit(solution)/shard_map/ppermute | solution.py:414
  64.0 2.1 %collective-permute-start.13 = (bf16[32,1024]{1,0:T(8,128)(2,1)S(1)}, bf16[32,1024]{1,0:T(8,128)(2,1)S(1)}, u32[]{:S(2)}, u32[]{:S(2)}) collective-permute-start(bf16[32,1024]{1,0:T(8,128)(2,1)S(1)} %get-tuple-element.47), channel_id=1, source_target_pairs={{0,48},{8,56},{16,0},{24,8},{32,16},{40,24},{48,32},{56,40},{64,11... | collective-permute-start | bytes 196616 | tf_op jit(solution)/shard_map/ppermute | solution.py:414
  66.1 0.9 %home.1.after = bf16[128,1024]{1,0:T(8,128)(2,1)} custom-call(bf16[128,1024]{1,0:T(8,128)(2,1)S(1)} %get-tuple-element.36.keep, bf16[128,1024]{1,0:T(8,128)(2,1)S(1)} %collective-permute-done.6.other, bf16[256,128]{1,0:T(8,128)(2,1)S(1)} %get-tuple-element.35.pick), custom_call_target="tpu_custom_call" | custom-call | bytes 2097152 | tf_op jit(solution)/shard_map/home/pallas_call | solution.py:415
  67.0 1.7 %keep_pages.1.kept = bf16[32,3,2,64,128]{4,3,2,1,0:T(8,128)(2,1)} custom-call(bf16[32,3,2,64,128]{4,3,2,1,0:T(8,128)(2,1)S(1)} %all-to-all-done.got, bf16[128,1024]{1,0:T(8,128)(2,1)} %home.1.after), custom_call_target="tpu_custom_call" | custom-call | bytes 2097152 | tf_op jit(solution)/shard_map/keep_pages/pallas_call | solution.py:416
  68.8 0.9 %arrive.1 = bf16[128,1024]{1,0:T(8,128)(2,1)} custom-call(bf16[32,1024]{1,0:T(8,128)(2,1)S(1)} %get-tuple-element.44.k0, bf16[32,1024]{1,0:T(8,128)(2,1)S(1)} %collective-permute-done.11.k1, bf16[32,1024]{1,0:T(8,128)(2,1)S(1)} %collective-permute-done.12.k2, bf16[32,1024]{1,0:T(8,128)(2,1)S(1)} %collective-permute-done.13.k3, ...), custom_call_target="tpu_custom_call" | custom-call | bytes 2097152 | tf_op jit(solution)/shard_map/arrive/pallas_call | solution.py:420
  (7 shorter events, 0.0 us)
Async XLA Ops:
  3.9 63.2 %all-to-all-start = ((bf16[32,3,2,64,128]{4,3,2,1,0:T(8,128)(2,1)}), bf16[32,3,2,64,128]{4,3,2,1,0:T(8,128)(2,1)S(1)}, u32[]{:S(2)}, u32[]{:S(2)}) async-start(bf16[32,3,2,64,128]{4,3,2,1,0:T(8,128)(2,1)} %get-tuple-element.48), calls=%async_computation | async-start | bytes 6291456 | tf_op jit(solution)/shard_map/all_to_all | solution.py:329
  22.1 10.4 %collective-permute-start.1 = (bf16[128,1024]{1,0:T(8,128)(2,1)S(1)}, bf16[128,1024]{1,0:T(8,128)(2,1)S(1)}, u32[]{:S(2)}, u32[]{:S(2)}) collective-permute-start(bf16[128,1024]{1,0:T(8,128)(2,1)S(1)} %get-tuple-element.30), channel_id=1, source_target_pairs={{0,1},{1,2},{2,3},{3,0},{4,5},{5,6},{6,7},{7,4},{8,9},{9,10},{10,1... | collective-permute-start | bytes 786440 | tf_op jit(solution)/shard_map/ppermute | solution.py:384
  23.8 8.7 %collective-permute-start.2 = (bf16[128,1024]{1,0:T(8,128)(2,1)S(1)}, bf16[128,1024]{1,0:T(8,128)(2,1)S(1)}, u32[]{:S(2)}, u32[]{:S(2)}) collective-permute-start(bf16[128,1024]{1,0:T(8,128)(2,1)S(1)} %get-tuple-element.31), channel_id=1, source_target_pairs={{0,3},{1,0},{2,1},{3,2},{4,7},{5,4},{6,5},{7,6},{8,11},{9,8},{10,9... | collective-permute-start | bytes 786440 | tf_op jit(solution)/shard_map/ppermute | solution.py:385
  26.0 12.1 %collective-permute-start = (bf16[128,1024]{1,0:T(8,128)(2,1)S(1)}, bf16[128,1024]{1,0:T(8,128)(2,1)S(1)}, u32[]{:S(2)}, u32[]{:S(2)}) collective-permute-start(bf16[128,1024]{1,0:T(8,128)(2,1)S(1)} %get-tuple-element.27), channel_id=1, source_target_pairs={{0,1},{1,2},{2,3},{3,0},{4,5},{5,6},{6,7},{7,4},{8,9},{9,10},{10,1... | collective-permute-start | bytes 786440 | tf_op jit(solution)/shard_map/ppermute | solution.py:386
  26.0 12.1 %collective-permute-start.5 = (bf16[128,1024]{1,0:T(8,128)(2,1)S(1)}, bf16[128,1024]{1,0:T(8,128)(2,1)S(1)}, u32[]{:S(2)}, u32[]{:S(2)}) collective-permute-start(bf16[128,1024]{1,0:T(8,128)(2,1)S(1)} %get-tuple-element.34), channel_id=1, source_target_pairs={{0,3},{1,0},{2,1},{3,2},{4,7},{5,4},{6,5},{7,6},{8,11},{9,8},{10,9... | collective-permute-start | bytes 786440 | tf_op jit(solution)/shard_map/ppermute | solution.py:387
  32.6 11.1 %collective-permute-start.3 = (bf16[128,1024]{1,0:T(8,128)(2,1)S(1)}, bf16[128,1024]{1,0:T(8,128)(2,1)S(1)}, u32[]{:S(2)}, u32[]{:S(2)}) collective-permute-start(bf16[128,1024]{1,0:T(8,128)(2,1)S(1)} %get-tuple-element.32), channel_id=1, source_target_pairs={{0,1},{1,2},{2,3},{3,0},{4,5},{5,6},{6,7},{7,4},{8,9},{9,10},{10,1... | collective-permute-start | bytes 786440 | tf_op jit(solution)/shard_map/ppermute | solution.py:389
  33.2 10.5 %collective-permute-start.4 = (bf16[128,1024]{1,0:T(8,128)(2,1)S(1)}, bf16[128,1024]{1,0:T(8,128)(2,1)S(1)}, u32[]{:S(2)}, u32[]{:S(2)}) collective-permute-start(bf16[128,1024]{1,0:T(8,128)(2,1)S(1)} %get-tuple-element.33), channel_id=1, source_target_pairs={{0,3},{1,0},{2,1},{3,2},{4,7},{5,4},{6,5},{7,6},{8,11},{9,8},{10,9... | collective-permute-start | bytes 786440 | tf_op jit(solution)/shard_map/ppermute | solution.py:390
  44.2 8.8 %collective-permute-start.7 = (bf16[64,1024]{1,0:T(8,128)(2,1)S(1)}, bf16[64,1024]{1,0:T(8,128)(2,1)S(1)}, u32[]{:S(2)}, u32[]{:S(2)}) collective-permute-start(bf16[64,1024]{1,0:T(8,128)(2,1)S(1)} %get-tuple-element.39), channel_id=1, source_target_pairs={{0,4},{1,5},{2,6},{3,7},{4,0},{5,1},{6,2},{7,3},{8,12},{9,13},{10,... | collective-permute-start | bytes 393224 | tf_op jit(solution)/shard_map/ppermute | solution.py:402
  44.6 13.4 %collective-permute-start.8 = (bf16[64,1024]{1,0:T(8,128)(2,1)S(1)}, bf16[64,1024]{1,0:T(8,128)(2,1)S(1)}, u32[]{:S(2)}, u32[]{:S(2)}) collective-permute-start(bf16[64,1024]{1,0:T(8,128)(2,1)S(1)} %get-tuple-element.40), channel_id=1, source_target_pairs={{0,64},{8,72},{16,80},{24,88},{32,96},{40,104},{48,112},{56,120},{... | collective-permute-start | bytes 393224 | tf_op jit(solution)/shard_map/ppermute | solution.py:401
  47.9 10.1 %collective-permute-start.9 = (bf16[64,1024]{1,0:T(8,128)(2,1)S(1)}, bf16[64,1024]{1,0:T(8,128)(2,1)S(1)}, u32[]{:S(2)}, u32[]{:S(2)}) collective-permute-start(bf16[64,1024]{1,0:T(8,128)(2,1)S(1)} %get-tuple-element.41), channel_id=1, source_target_pairs={{0,68},{1,69},{2,70},{3,71},{4,64},{5,65},{6,66},{7,67},{8,76},{9,... | collective-permute-start | bytes 393224 | tf_op jit(solution)/shard_map/ppermute | solution.py:403
  48.1 18.0 %collective-permute-start.6 = (bf16[128,1024]{1,0:T(8,128)(2,1)S(1)}, bf16[128,1024]{1,0:T(8,128)(2,1)S(1)}, u32[]{:S(2)}, u32[]{:S(2)}) collective-permute-start(bf16[128,1024]{1,0:T(8,128)(2,1)S(1)} %get-tuple-element.37), channel_id=1, source_target_pairs={{0,4},{1,5},{2,6},{3,7},{4,0},{5,1},{6,2},{7,3},{8,12},{9,13},{10,... | collective-permute-start | bytes 786440 | tf_op jit(solution)/shard_map/ppermute | solution.py:405
  58.3 1.8 %collective-permute-start.10 = (bf16[64,1024]{1,0:T(8,128)(2,1)S(1)}, bf16[64,1024]{1,0:T(8,128)(2,1)S(1)}, u32[]{:S(2)}, u32[]{:S(2)}) collective-permute-start(bf16[64,1024]{1,0:T(8,128)(2,1)S(1)} %get-tuple-element.43), channel_id=1, source_target_pairs={{0,8},{8,0},{16,24},{24,16},{32,40},{40,32},{48,56},{56,48},{64,72... | collective-permute-start | bytes 393224 | tf_op jit(solution)/shard_map/ppermute | solution.py:406
  60.7 8.1 %collective-permute-start.11 = (bf16[32,1024]{1,0:T(8,128)(2,1)}, bf16[32,1024]{1,0:T(8,128)(2,1)S(1)}, u32[]{:S(2)}, u32[]{:S(2)}) collective-permute-start(bf16[32,1024]{1,0:T(8,128)(2,1)} %get-tuple-element.45), channel_id=1, source_target_pairs={{0,16},{8,24},{16,32},{24,40},{32,48},{40,56},{48,0},{56,8},{64,80... | collective-permute-start | bytes 196616 | tf_op jit(solution)/shard_map/ppermute | solution.py:414
  61.2 7.6 %collective-permute-start.12 = (bf16[32,1024]{1,0:T(8,128)(2,1)}, bf16[32,1024]{1,0:T(8,128)(2,1)S(1)}, u32[]{:S(2)}, u32[]{:S(2)}) collective-permute-start(bf16[32,1024]{1,0:T(8,128)(2,1)} %get-tuple-element.46), channel_id=1, source_target_pairs={{0,32},{8,40},{16,48},{24,56},{32,0},{40,8},{48,16},{56,24},{64,96... | collective-permute-start | bytes 196616 | tf_op jit(solution)/shard_map/ppermute | solution.py:414
  64.0 4.8 %collective-permute-start.13 = (bf16[32,1024]{1,0:T(8,128)(2,1)S(1)}, bf16[32,1024]{1,0:T(8,128)(2,1)S(1)}, u32[]{:S(2)}, u32[]{:S(2)}) collective-permute-start(bf16[32,1024]{1,0:T(8,128)(2,1)S(1)} %get-tuple-element.47), channel_id=1, source_target_pairs={{0,48},{8,56},{16,0},{24,8},{32,16},{40,24},{48,32},{56,40},{64,11... | collective-permute-start | bytes 196616 | tf_op jit(solution)/shard_map/ppermute | solution.py:414

commit v8 on v7

--- a/solution.py
+++ b/solution.py
@@ -265,7 +265,7 @@
         ahead[k][16:] = crossed[k * 16:(k + 1) * 16]
 
 
-def arrive_kernel(k0, k1, k2, k3, kept, out):
+def arrive_kernel(k0, k1, k3, k2, kept, out):
     here_at = lax.axis_index("inst")
     rows = jnp.concatenate([k0[...], k1[...], k2[...], k3[...]], axis=0)
     to = lax.broadcasted_iota(jnp.int32, (ROWS, ROWS), 0)
@@ -411,7 +411,7 @@
     def along(k):
         return [(s, (s & 9) + (((s >> 1) + k) & (RING - 1)) * 2) for s in range(INST)]
 
-    ahead = [ahead[0]] + [lax.ppermute(ahead[k], "inst", along(k)) for k in range(1, RING)]
+    ahead = [ahead[0]] + [lax.ppermute(ahead[k], "inst", along(k)) for k in (1, 3, 2)]
     home = small(home_kernel, piece, "home")(keep, other, pick)
     arrival_cache = small(
         keep_kernel, pltpu.HBM(arrival_cache.shape, BF16), "keep_pages",

time: 69.9 us -> 69.8 us (level)
  no operation moved by 1% of the time
where the time goes in v8:
time: 69.8 us; the launch traced here: 69.1 us
  starting transfers between devices  27.3 us (39%)
  waiting for transfers between devices  23.1 us (33%)
  Pallas kernels  18 us (26%)
  between operations  0.71 us (1%)
    pallas_call x1, Pallas kernels, local(): pl.pallas_call(attend_kernel, out_shape=(pltpu.VMEM((ROWS, share), BF16),...  9.74 us
    all_to_all x1, starting transfers between devices, local(): lax.all_to_all(send, 'inst', split_axis=0, concat_axis=0, tiled=True)  8.46 us
    ppermute x1, waiting for transfers between devices, local(): up1 = lax.ppermute(next_up, 'tp', shift(1))  5.61 us
    ppermute x1, waiting for transfers between devices, local(): far0 = lax.ppermute(far0, 'inst', flip_far)  5.1 us
    ppermute x1, waiting for transfers between devices, local(): near1 = lax.ppermute(near1, 'tp', flip_y)  4.82 us
    ppermute x3, starting transfers between devices, local(): lax.ppermute(ahead[k], 'inst', along(k))  4.79 us
    ppermute x1, waiting for transfers between devices, local(): far1 = lax.ppermute(far1, 'tp', shift(1))  3.79 us
    ppermute x1, starting transfers between devices, local(): far0 = lax.ppermute(far0, 'inst', flip_far)  3.32 us
  transfers between devices with their start and end apart: 15, of which 6 were waited for; matrix products, arithmetic and copies ran while one was open for 0% of the time, Pallas kernels for 20%

profile of v8, /device:TPU:1, one launch (start us, length us, event | category | flops | bytes accessed | tf_op | source)
XLA Modules:
  0.0 69.1 jit_solution(12405197250938021314)
XLA Ops:
  0.6 3.3 %pack_pages.1 = (bf16[32,3,2,64,128]{4,3,2,1,0:T(8,128)(2,1)}, bf16[256,128]{1,0:T(8,128)(2,1)S(1)}) custom-call(s32[3,32]{1,0:T(4,128)} %bitcast.11, s32[16]{0:T(128)} %req_list.1, s32[16]{0:T(128)} %bitcast.14, s32[16]{0:T(128)} %resume_list.1, bf16[96,2,64,128]{3,2,1,0:T(8,128)(2,1)} %pool.3), custom_call_target="tpu_custom_call" | custom-call | bytes 6291456 | tf_op jit(solution)/shard_map/pack_pages/pallas_call | solution.py:302
  3.9 8.5 %all-to-all-start = ((bf16[32,3,2,64,128]{4,3,2,1,0:T(8,128)(2,1)}), bf16[32,3,2,64,128]{4,3,2,1,0:T(8,128)(2,1)S(1)}, u32[]{:S(2)}, u32[]{:S(2)}) async-start(bf16[32,3,2,64,128]{4,3,2,1,0:T(8,128)(2,1)} %get-tuple-element.48), calls=%async_computation | async-start | bytes 6291456 | tf_op jit(solution)/shard_map/all_to_all | solution.py:329
  12.4 9.7 %attend.1 = (bf16[128,1024]{1,0:T(8,128)(2,1)S(1)}, bf16[128,1024]{1,0:T(8,128)(2,1)S(1)}, bf16[128,1024]{1,0:T(8,128)(2,1)S(1)}, bf16[128,1024]{1,0:T(8,128)(2,...) custom-call(bf16[128,8192]{1,0:T(8,128)(2,1)} %bitcast.7, ...), custom_call_target="tpu_custom_call" | custom-call | flops 2400000000 | bytes 25165824 | tf_op jit(solution)/shard_map/attend/pallas_call | solution.py:336
  22.1 1.7 %collective-permute-start.1 = (bf16[128,1024]{1,0:T(8,128)(2,1)S(1)}, bf16[128,1024]{1,0:T(8,128)(2,1)S(1)}, u32[]{:S(2)}, u32[]{:S(2)}) collective-permute-start(bf16[128,1024]{1,0:T(8,128)(2,1)S(1)} %get-tuple-element.30), channel_id=1, source_target_pairs={{0,1},{1,2},{2,3},{3,0},{4,5},{5,6},{6,7},{7,4},{8,9},{9,10},{10,1... | collective-permute-start | bytes 786440 | tf_op jit(solution)/shard_map/ppermute | solution.py:384
  23.8 2.2 %collective-permute-start.2 = (bf16[128,1024]{1,0:T(8,128)(2,1)S(1)}, bf16[128,1024]{1,0:T(8,128)(2,1)S(1)}, u32[]{:S(2)}, u32[]{:S(2)}) collective-permute-start(bf16[128,1024]{1,0:T(8,128)(2,1)S(1)} %get-tuple-element.31), channel_id=1, source_target_pairs={{0,3},{1,0},{2,1},{3,2},{4,7},{5,4},{6,5},{7,6},{8,11},{9,8},{10,9... | collective-permute-start | bytes 786440 | tf_op jit(solution)/shard_map/ppermute | solution.py:385
  26.0 0.0 collective-permute-start
  26.0 2.7 %collective-permute-start.5 = (bf16[128,1024]{1,0:T(8,128)(2,1)S(1)}, bf16[128,1024]{1,0:T(8,128)(2,1)S(1)}, u32[]{:S(2)}, u32[]{:S(2)}) collective-permute-start(bf16[128,1024]{1,0:T(8,128)(2,1)S(1)} %get-tuple-element.34), channel_id=1, source_target_pairs={{0,3},{1,0},{2,1},{3,2},{4,7},{5,4},{6,5},{7,6},{8,11},{9,8},{10,9... | collective-permute-start | bytes 786440 | tf_op jit(solution)/shard_map/ppermute | solution.py:387
  28.7 3.8 %collective-permute-done.1.far1 = bf16[128,1024]{1,0:T(8,128)(2,1)S(1)} collective-permute-done((bf16[128,1024]{1,0:T(8,128)(2,1)S(1)}, bf16[128,1024]{1,0:T(8,128)(2,1)S(1)}, u32[]{:S(2)}, u32[]{:S(2)}) %collective-permute-start.1) | collective-permute-done | bytes 262176 | tf_op jit(solution)/shard_map/ppermute | solution.py:384
  32.5 0.0 collective-permute-done.2.far0
  32.5 0.1 relay.1
  32.6 0.6 collective-permute-start.3
  33.2 2.2 %collective-permute-start.4 = (bf16[128,1024]{1,0:T(8,128)(2,1)S(1)}, bf16[128,1024]{1,0:T(8,128)(2,1)S(1)}, u32[]{:S(2)}, u32[]{:S(2)}) collective-permute-start(bf16[128,1024]{1,0:T(8,128)(2,1)S(1)} %get-tuple-element.33), channel_id=1, source_target_pairs={{0,3},{1,0},{2,1},{3,2},{4,7},{5,4},{6,5},{7,6},{8,11},{9,8},{10,9... | collective-permute-start | bytes 786440 | tf_op jit(solution)/shard_map/ppermute | solution.py:390
  35.4 2.7 %collective-permute-done.up0 = bf16[128,1024]{1,0:T(8,128)(2,1)S(1)} collective-permute-done((bf16[128,1024]{1,0:T(8,128)(2,1)S(1)}, bf16[128,1024]{1,0:T(8,128)(2,1)S(1)}, u32[]{:S(2)}, u32[]{:S(2)}) %collective-permute-start) | collective-permute-done | bytes 262176 | tf_op jit(solution)/shard_map/ppermute | solution.py:386
  38.1 0.0 collective-permute-done.5.down1
  38.1 5.6 %collective-permute-done.3.up1 = bf16[128,1024]{1,0:T(8,128)(2,1)S(1)} collective-permute-done((bf16[128,1024]{1,0:T(8,128)(2,1)S(1)}, bf16[128,1024]{1,0:T(8,128)(2,1)S(1)}, u32[]{:S(2)}, u32[]{:S(2)}) %collective-permute-start.3) | collective-permute-done | bytes 262176 | tf_op jit(solution)/shard_map/ppermute | solution.py:389
  43.7 0.0 collective-permute-done.4.down0
  43.7 0.4 close.1
  44.2 0.5 collective-permute-start.7
  44.6 3.3 %collective-permute-start.8 = (bf16[64,1024]{1,0:T(8,128)(2,1)S(1)}, bf16[64,1024]{1,0:T(8,128)(2,1)S(1)}, u32[]{:S(2)}, u32[]{:S(2)}) collective-permute-start(bf16[64,1024]{1,0:T(8,128)(2,1)S(1)} %get-tuple-element.40), channel_id=1, source_target_pairs={{0,64},{8,72},{16,80},{24,88},{32,96},{40,104},{48,112},{56,120},{... | collective-permute-start | bytes 393224 | tf_op jit(solution)/shard_map/ppermute | solution.py:401
  47.9 0.2 collective-permute-start.9
  48.1 4.8 %collective-permute-done.7.near1 = bf16[64,1024]{1,0:T(8,128)(2,1)S(1)} collective-permute-done((bf16[64,1024]{1,0:T(8,128)(2,1)S(1)}, bf16[64,1024]{1,0:T(8,128)(2,1)S(1)}, u32[]{:S(2)}, u32[]{:S(2)}) %collective-permute-start.7) | collective-permute-done | bytes 131104 | tf_op jit(solution)/shard_map/ppermute | solution.py:402
  52.9 5.1 %collective-permute-done.8.far0 = bf16[64,1024]{1,0:T(8,128)(2,1)S(1)} collective-permute-done((bf16[64,1024]{1,0:T(8,128)(2,1)S(1)}, bf16[64,1024]{1,0:T(8,128)(2,1)S(1)}, u32[]{:S(2)}, u32[]{:S(2)}) %collective-permute-start.8) | collective-permute-done | bytes 131104 | tf_op jit(solution)/shard_map/ppermute | solution.py:401
  58.0 0.2 join.1
  58.3 0.8 %collective-permute-start.10 = (bf16[64,1024]{1,0:T(8,128)(2,1)S(1)}, bf16[64,1024]{1,0:T(8,128)(2,1)S(1)}, u32[]{:S(2)}, u32[]{:S(2)}) collective-permute-start(bf16[64,1024]{1,0:T(8,128)(2,1)S(1)} %get-tuple-element.43), channel_id=1, source_target_pairs={{0,8},{8,0},{16,24},{24,16},{32,40},{40,32},{48,56},{56,48},{64,72... | collective-permute-start | bytes 393224 | tf_op jit(solution)/shard_map/ppermute | solution.py:406
  59.0 1.0 %collective-permute-done.10.crossed = bf16[64,1024]{1,0:T(8,128)(2,1)S(1)} collective-permute-done((bf16[64,1024]{1,0:T(8,128)(2,1)S(1)}, bf16[64,1024]{1,0:T(8,128)(2,1)S(1)}, u32[]{:S(2)}, u32[]{:S(2)}) %collective-permute-start.10) | collective-permute-done | bytes 131104 | tf_op jit(solution)/shard_map/ppermute | solution.py:406
  60.0 0.7 split.1
  60.7 0.5 collective-permute-start.11
  61.2 2.2 %collective-permute-start.12 = (bf16[32,1024]{1,0:T(8,128)(2,1)}, bf16[32,1024]{1,0:T(8,128)(2,1)S(1)}, u32[]{:S(2)}, u32[]{:S(2)}) collective-permute-start(bf16[32,1024]{1,0:T(8,128)(2,1)} %get-tuple-element.46), channel_id=1, source_target_pairs={{0,48},{8,56},{16,0},{24,8},{32,16},{40,24},{48,32},{56,40},{64,11... | collective-permute-start | bytes 196616 | tf_op jit(solution)/shard_map/ppermute | solution.py:414
  63.4 2.1 %collective-permute-start.13 = (bf16[32,1024]{1,0:T(8,128)(2,1)S(1)}, bf16[32,1024]{1,0:T(8,128)(2,1)S(1)}, u32[]{:S(2)}, u32[]{:S(2)}) collective-permute-start(bf16[32,1024]{1,0:T(8,128)(2,1)S(1)} %get-tuple-element.47), channel_id=1, source_target_pairs={{0,32},{8,40},{16,48},{24,56},{32,0},{40,8},{48,16},{56,24},{64,96... | collective-permute-start | bytes 196616 | tf_op jit(solution)/shard_map/ppermute | solution.py:414
  65.5 0.9 %home.1.after = bf16[128,1024]{1,0:T(8,128)(2,1)} custom-call(bf16[128,1024]{1,0:T(8,128)(2,1)S(1)} %get-tuple-element.36.keep, bf16[128,1024]{1,0:T(8,128)(2,1)S(1)} %collective-permute-done.6.other, bf16[256,128]{1,0:T(8,128)(2,1)S(1)} %get-tuple-element.35.pick), custom_call_target="tpu_custom_call" | custom-call | bytes 2097152 | tf_op jit(solution)/shard_map/home/pallas_call | solution.py:415
  66.4 1.7 %keep_pages.1.kept = bf16[32,3,2,64,128]{4,3,2,1,0:T(8,128)(2,1)} custom-call(bf16[32,3,2,64,128]{4,3,2,1,0:T(8,128)(2,1)S(1)} %all-to-all-done.got, bf16[128,1024]{1,0:T(8,128)(2,1)} %home.1.after), custom_call_target="tpu_custom_call" | custom-call | bytes 2097152 | tf_op jit(solution)/shard_map/keep_pages/pallas_call | solution.py:416
  68.2 0.9 %arrive.1 = bf16[128,1024]{1,0:T(8,128)(2,1)} custom-call(bf16[32,1024]{1,0:T(8,128)(2,1)S(1)} %get-tuple-element.44.k0, bf16[32,1024]{1,0:T(8,128)(2,1)S(1)} %collective-permute-done.11.k1, bf16[32,1024]{1,0:T(8,128)(2,1)S(1)} %collective-permute-done.12.k3, bf16[32,1024]{1,0:T(8,128)(2,1)S(1)} %collective-permute-done.13.k2, ...), custom_call_target="tpu_custom_call" | custom-call | bytes 2097152 | tf_op jit(solution)/shard_map/arrive/pallas_call | solution.py:420
  (7 shorter events, 0.0 us)
Async XLA Ops:
  3.9 62.5 %all-to-all-start = ((bf16[32,3,2,64,128]{4,3,2,1,0:T(8,128)(2,1)}), bf16[32,3,2,64,128]{4,3,2,1,0:T(8,128)(2,1)S(1)}, u32[]{:S(2)}, u32[]{:S(2)}) async-start(bf16[32,3,2,64,128]{4,3,2,1,0:T(8,128)(2,1)} %get-tuple-element.48), calls=%async_computation | async-start | bytes 6291456 | tf_op jit(solution)/shard_map/all_to_all | solution.py:329
  22.1 10.4 %collective-permute-start.1 = (bf16[128,1024]{1,0:T(8,128)(2,1)S(1)}, bf16[128,1024]{1,0:T(8,128)(2,1)S(1)}, u32[]{:S(2)}, u32[]{:S(2)}) collective-permute-start(bf16[128,1024]{1,0:T(8,128)(2,1)S(1)} %get-tuple-element.30), channel_id=1, source_target_pairs={{0,1},{1,2},{2,3},{3,0},{4,5},{5,6},{6,7},{7,4},{8,9},{9,10},{10,1... | collective-permute-start | bytes 786440 | tf_op jit(solution)/shard_map/ppermute | solution.py:384
  23.8 8.7 %collective-permute-start.2 = (bf16[128,1024]{1,0:T(8,128)(2,1)S(1)}, bf16[128,1024]{1,0:T(8,128)(2,1)S(1)}, u32[]{:S(2)}, u32[]{:S(2)}) collective-permute-start(bf16[128,1024]{1,0:T(8,128)(2,1)S(1)} %get-tuple-element.31), channel_id=1, source_target_pairs={{0,3},{1,0},{2,1},{3,2},{4,7},{5,4},{6,5},{7,6},{8,11},{9,8},{10,9... | collective-permute-start | bytes 786440 | tf_op jit(solution)/shard_map/ppermute | solution.py:385
  26.0 12.1 %collective-permute-start = (bf16[128,1024]{1,0:T(8,128)(2,1)S(1)}, bf16[128,1024]{1,0:T(8,128)(2,1)S(1)}, u32[]{:S(2)}, u32[]{:S(2)}) collective-permute-start(bf16[128,1024]{1,0:T(8,128)(2,1)S(1)} %get-tuple-element.27), channel_id=1, source_target_pairs={{0,1},{1,2},{2,3},{3,0},{4,5},{5,6},{6,7},{7,4},{8,9},{9,10},{10,1... | collective-permute-start | bytes 786440 | tf_op jit(solution)/shard_map/ppermute | solution.py:386
  26.0 12.1 %collective-permute-start.5 = (bf16[128,1024]{1,0:T(8,128)(2,1)S(1)}, bf16[128,1024]{1,0:T(8,128)(2,1)S(1)}, u32[]{:S(2)}, u32[]{:S(2)}) collective-permute-start(bf16[128,1024]{1,0:T(8,128)(2,1)S(1)} %get-tuple-element.34), channel_id=1, source_target_pairs={{0,3},{1,0},{2,1},{3,2},{4,7},{5,4},{6,5},{7,6},{8,11},{9,8},{10,9... | collective-permute-start | bytes 786440 | tf_op jit(solution)/shard_map/ppermute | solution.py:387
  32.6 11.1 %collective-permute-start.3 = (bf16[128,1024]{1,0:T(8,128)(2,1)S(1)}, bf16[128,1024]{1,0:T(8,128)(2,1)S(1)}, u32[]{:S(2)}, u32[]{:S(2)}) collective-permute-start(bf16[128,1024]{1,0:T(8,128)(2,1)S(1)} %get-tuple-element.32), channel_id=1, source_target_pairs={{0,1},{1,2},{2,3},{3,0},{4,5},{5,6},{6,7},{7,4},{8,9},{9,10},{10,1... | collective-permute-start | bytes 786440 | tf_op jit(solution)/shard_map/ppermute | solution.py:389
  33.2 10.5 %collective-permute-start.4 = (bf16[128,1024]{1,0:T(8,128)(2,1)S(1)}, bf16[128,1024]{1,0:T(8,128)(2,1)S(1)}, u32[]{:S(2)}, u32[]{:S(2)}) collective-permute-start(bf16[128,1024]{1,0:T(8,128)(2,1)S(1)} %get-tuple-element.33), channel_id=1, source_target_pairs={{0,3},{1,0},{2,1},{3,2},{4,7},{5,4},{6,5},{7,6},{8,11},{9,8},{10,9... | collective-permute-start | bytes 786440 | tf_op jit(solution)/shard_map/ppermute | solution.py:390
  44.2 8.8 %collective-permute-start.7 = (bf16[64,1024]{1,0:T(8,128)(2,1)S(1)}, bf16[64,1024]{1,0:T(8,128)(2,1)S(1)}, u32[]{:S(2)}, u32[]{:S(2)}) collective-permute-start(bf16[64,1024]{1,0:T(8,128)(2,1)S(1)} %get-tuple-element.39), channel_id=1, source_target_pairs={{0,4},{1,5},{2,6},{3,7},{4,0},{5,1},{6,2},{7,3},{8,12},{9,13},{10,... | collective-permute-start | bytes 393224 | tf_op jit(solution)/shard_map/ppermute | solution.py:402
  44.6 13.4 %collective-permute-start.8 = (bf16[64,1024]{1,0:T(8,128)(2,1)S(1)}, bf16[64,1024]{1,0:T(8,128)(2,1)S(1)}, u32[]{:S(2)}, u32[]{:S(2)}) collective-permute-start(bf16[64,1024]{1,0:T(8,128)(2,1)S(1)} %get-tuple-element.40), channel_id=1, source_target_pairs={{0,64},{8,72},{16,80},{24,88},{32,96},{40,104},{48,112},{56,120},{... | collective-permute-start | bytes 393224 | tf_op jit(solution)/shard_map/ppermute | solution.py:401
  47.9 10.1 %collective-permute-start.9 = (bf16[64,1024]{1,0:T(8,128)(2,1)S(1)}, bf16[64,1024]{1,0:T(8,128)(2,1)S(1)}, u32[]{:S(2)}, u32[]{:S(2)}) collective-permute-start(bf16[64,1024]{1,0:T(8,128)(2,1)S(1)} %get-tuple-element.41), channel_id=1, source_target_pairs={{0,68},{1,69},{2,70},{3,71},{4,64},{5,65},{6,66},{7,67},{8,76},{9,... | collective-permute-start | bytes 393224 | tf_op jit(solution)/shard_map/ppermute | solution.py:403
  48.1 17.4 %collective-permute-start.6 = (bf16[128,1024]{1,0:T(8,128)(2,1)S(1)}, bf16[128,1024]{1,0:T(8,128)(2,1)S(1)}, u32[]{:S(2)}, u32[]{:S(2)}) collective-permute-start(bf16[128,1024]{1,0:T(8,128)(2,1)S(1)} %get-tuple-element.37), channel_id=1, source_target_pairs={{0,4},{1,5},{2,6},{3,7},{4,0},{5,1},{6,2},{7,3},{8,12},{9,13},{10,... | collective-permute-start | bytes 786440 | tf_op jit(solution)/shard_map/ppermute | solution.py:405
  58.3 1.8 %collective-permute-start.10 = (bf16[64,1024]{1,0:T(8,128)(2,1)S(1)}, bf16[64,1024]{1,0:T(8,128)(2,1)S(1)}, u32[]{:S(2)}, u32[]{:S(2)}) collective-permute-start(bf16[64,1024]{1,0:T(8,128)(2,1)S(1)} %get-tuple-element.43), channel_id=1, source_target_pairs={{0,8},{8,0},{16,24},{24,16},{32,40},{40,32},{48,56},{56,48},{64,72... | collective-permute-start | bytes 393224 | tf_op jit(solution)/shard_map/ppermute | solution.py:406
  60.7 7.5 %collective-permute-start.11 = (bf16[32,1024]{1,0:T(8,128)(2,1)}, bf16[32,1024]{1,0:T(8,128)(2,1)S(1)}, u32[]{:S(2)}, u32[]{:S(2)}) collective-permute-start(bf16[32,1024]{1,0:T(8,128)(2,1)} %get-tuple-element.45), channel_id=1, source_target_pairs={{0,16},{8,24},{16,32},{24,40},{32,48},{40,56},{48,0},{56,8},{64,80... | collective-permute-start | bytes 196616 | tf_op jit(solution)/shard_map/ppermute | solution.py:414
  61.2 7.0 %collective-permute-start.12 = (bf16[32,1024]{1,0:T(8,128)(2,1)}, bf16[32,1024]{1,0:T(8,128)(2,1)S(1)}, u32[]{:S(2)}, u32[]{:S(2)}) collective-permute-start(bf16[32,1024]{1,0:T(8,128)(2,1)} %get-tuple-element.46), channel_id=1, source_target_pairs={{0,48},{8,56},{16,0},{24,8},{32,16},{40,24},{48,32},{56,40},{64,11... | collective-permute-start | bytes 196616 | tf_op jit(solution)/shard_map/ppermute | solution.py:414
  63.4 4.8 %collective-permute-start.13 = (bf16[32,1024]{1,0:T(8,128)(2,1)S(1)}, bf16[32,1024]{1,0:T(8,128)(2,1)S(1)}, u32[]{:S(2)}, u32[]{:S(2)}) collective-permute-start(bf16[32,1024]{1,0:T(8,128)(2,1)S(1)} %get-tuple-element.47), channel_id=1, source_target_pairs={{0,32},{8,40},{16,48},{24,56},{32,0},{40,8},{48,16},{56,24},{64,96... | collective-permute-start | bytes 196616 | tf_op jit(solution)/shard_map/ppermute | solution.py:414

commit v9 on v8

--- a/solution.py
+++ b/solution.py
@@ -33,8 +33,8 @@
 
 
 def pack_kernel(
-    page_list, req_list, dest_list, resume_list, pool, send, pick,
-    table, mreq, mdest, resume, slot_of, filled, count, kv, zeros, wide, kv_sem, sem, small_sem,
+    page_list, req_list, dest_list, pool, send,
+    table, mreq, mdest, slot_of, filled, count, kv, zeros, kv_sem, sem, small_sem,
 ):
     size = pool.shape[0] // LANES
     load = [
@@ -44,7 +44,7 @@
     small = [
         pltpu.make_async_copy(source, target, small_sem.at[i])
         for i, (source, target) in enumerate((
-            (req_list, mreq), (dest_list, mdest), (resume_list, resume), (page_list, table),
+            (req_list, mreq), (dest_list, mdest), (page_list, table),
         ))
     ]
     for copy in small:
@@ -79,14 +79,21 @@
         for p in range(MAXP):
             pltpu.make_async_copy(kv.at[table[p, mreq[k]]], send.at[slot_of[k], p], sem).start()
 
+    pltpu.make_async_copy(send, send, sem).wait()
+
+
+def choose_kernel(mreq, mdest, resume, pick, count, wide):
+    for d in range(INST):
+        count[d] = 0
     here_at = lax.axis_index("inst")
     rows = lax.broadcasted_iota(jnp.int32, (2 * ROWS, ROWS), 0)
     cols = lax.broadcasted_iota(jnp.int32, (2 * ROWS, ROWS), 1)
     wide[...] = jnp.where(rows == cols, 1.0, 0.0).astype(F32)
     lane = lax.broadcasted_iota(jnp.int32, (1, ROWS), 1)
     for k in range(MIG):
-        slot = slot_of[k]
-        d, c = slot >> 1, slot & 1
+        d = mdest[k]
+        c = count[d]
+        count[d] = c + 1
         req = mreq[k]
         first = resume[k]
         far = (d >> 3) ^ (here_at >> 3)
@@ -98,7 +105,6 @@
             wide[pl.ds(at, 1), :] = jnp.where((lane == at) & (t < first), 1.0, 0.0).astype(F32)
             wide[pl.ds(block + t * CAP + c, 1), :] = jnp.where((lane == at) & (t >= first), 1.0, 0.0).astype(F32)
     pick[...] = wide[...].astype(BF16)
-    pltpu.make_async_copy(send, send, sem).wait()
 
 
 def attend_kernel(
@@ -299,17 +305,13 @@
     share = width // lax.axis_size("tp")
     table = page_table.T
     hbm = functools.partial(pltpu.with_memory_space_constraint, memory_space=pltpu.HBM)
-    send, pick = pl.pallas_call(
+    send = pl.pallas_call(
         pack_kernel,
-        out_shape=(
-            pltpu.HBM((INST * CAP, MAXP) + kv_pool.shape[1:], BF16),
-            jax.ShapeDtypeStruct((2 * ROWS, ROWS), BF16),
-        ),
-        in_specs=[ANY] * 5,
-        out_specs=(ANY, VMEM),
+        out_shape=pltpu.HBM((INST * CAP, MAXP) + kv_pool.shape[1:], BF16),
+        in_specs=[ANY] * 4,
+        out_specs=ANY,
         scratch_shapes=[
             pltpu.SMEM((MAXP, REQS), jnp.int32),
-            pltpu.SMEM((MIG,), jnp.int32),
             pltpu.SMEM((MIG,), jnp.int32),
             pltpu.SMEM((MIG,), jnp.int32),
             pltpu.SMEM((MIG,), jnp.int32),
@@ -317,15 +319,14 @@
             pltpu.SMEM((INST,), jnp.int32),
             pltpu.VMEM(kv_pool.shape, BF16),
             pltpu.VMEM((MAXP,) + kv_pool.shape[1:], BF16),
-            pltpu.VMEM((2 * ROWS, ROWS), F32),
             pltpu.SemaphoreType.DMA((LANES,)),
             pltpu.SemaphoreType.DMA,
-            pltpu.SemaphoreType.DMA((4,)),
+            pltpu.SemaphoreType.DMA((3,)),
         ],
         compiler_params=pltpu.CompilerParams(vmem_limit_bytes=FULL_VMEM),
         cost_estimate=pl.CostEstimate(flops=0, bytes_accessed=6 << 20, transcendentals=0),
         name="pack_pages",
-    )(hbm(table), hbm(mig_req), hbm(mig_dest.reshape(-1)), hbm(resume), hbm(kv_pool))
+    )(hbm(table), hbm(mig_req), hbm(mig_dest.reshape(-1)), hbm(kv_pool))
     arrival_cache = lax.all_to_all(send, "inst", split_axis=0, concat_axis=0, tiled=True)
 
     half = HD // 2
@@ -388,6 +389,10 @@
     next_up, next_down = small(relay_kernel, (piece,) * 2, "relay")(up1, down0, far1, far0)
     up1 = lax.ppermute(next_up, "tp", shift(1))
     down0 = lax.ppermute(next_down, "tp", shift(-1))
+    pick = small(
+        choose_kernel, jax.ShapeDtypeStruct((2 * ROWS, ROWS), BF16), "choose", in_specs=[SMEM] * 3,
+        scratch_shapes=[pltpu.SMEM((INST,), jnp.int32), pltpu.VMEM((2 * ROWS, ROWS), F32)],
+    )(mig_req, mig_dest.reshape(-1), resume)
     half_piece = jax.ShapeDtypeStruct((ROWS // 2, share), BF16)
     keep, pass_on, near0, near1, far0, far1 = small(
         close_kernel, (piece,) * 2 + (half_piece,) * 4, "close"

time: 69.8 us -> 69.5 us (level)
  waiting for transfers between devices: 23.1 us -> 22.3 us
    ppermute x1, waiting for transfers between devices: 2.74 us -> 1.93 us  [local(): up0 = lax.ppermute(up0, 'tp', shift(1))]
    pallas_call x1 -> x2, Pallas kernels: 3.26 us -> 3.83 us  [the longest x1 3.04 us: local(): pl.pallas_call(pack_kernel, out_shape=pltpu.HBM((INST * CAP, MAXP) + kv_p...]
  transfers between devices with their start and end apart: 15 -> 15, of which waited for: 6 -> 6; matrix products, arithmetic and copies ran while one was open for 0% -> 0% of each run, Pallas kernels for 20% -> 21%
where the time goes in v9:
time: 69.5 us; the launch traced here: 68.9 us
  starting transfers between devices  27.3 us (39%)
  waiting for transfers between devices  22.3 us (32%)
  Pallas kernels  18.6 us (27%)
  between operations  0.74 us (1%)
    pallas_call x1, Pallas kernels, local(): pl.pallas_call(attend_kernel, out_shape=(pltpu.VMEM((ROWS, share), BF16),...  9.75 us
    all_to_all x1, starting transfers between devices, local(): lax.all_to_all(send, 'inst', split_axis=0, concat_axis=0, tiled=True)  8.46 us
    ppermute x1, waiting for transfers between devices, local(): up1 = lax.ppermute(next_up, 'tp', shift(1))  5.61 us
    ppermute x1, waiting for transfers between devices, local(): far0 = lax.ppermute(far0, 'inst', flip_far)  5.09 us
    ppermute x1, waiting for transfers between devices, local(): near1 = lax.ppermute(near1, 'tp', flip_y)  4.82 us
    ppermute x3, starting transfers between devices, local(): lax.ppermute(ahead[k], 'inst', along(k))  4.8 us
    ppermute x1, waiting for transfers between devices, local(): far1 = lax.ppermute(far1, 'tp', shift(1))  3.8 us
    ppermute x1, starting transfers between devices, local(): far0 = lax.ppermute(far0, 'inst', flip_far)  3.3 us
  transfers between devices with their start and end apart: 15, of which 6 were waited for; matrix products, arithmetic and copies ran while one was open for 0% of the time, Pallas kernels for 21%

profile of v9, /device:TPU:1, one launch (start us, length us, event | category | flops | bytes accessed | tf_op | source)
XLA Modules:
  0.0 68.9 jit_solution(13268198790346456870)
XLA Ops:
  0.6 3.0 %pack_pages.1 = bf16[32,3,2,64,128]{4,3,2,1,0:T(8,128)(2,1)} custom-call(s32[3,32]{1,0:T(4,128)} %bitcast.13, s32[16]{0:T(128)} %req_list.1, s32[16]{0:T(128)} %bitcast.7, bf16[96,2,64,128]{3,2,1,0:T(8,128)(2,1)} %pool.3), custom_call_target="tpu_custom_call" | custom-call | bytes 6291456 | tf_op jit(solution)/shard_map/pack_pages/pallas_call | solution.py:308
  3.7 8.5 %all-to-all-start = ((bf16[32,3,2,64,128]{4,3,2,1,0:T(8,128)(2,1)}), bf16[32,3,2,64,128]{4,3,2,1,0:T(8,128)(2,1)S(1)}, u32[]{:S(2)}, u32[]{:S(2)}) async-start(bf16[32,3,2,64,128]{4,3,2,1,0:T(8,128)(2,1)} %pack_pages.1), calls=%async_computation | async-start | bytes 6291456 | tf_op jit(solution)/shard_map/all_to_all | solution.py:330
  12.1 0.0 copy-start.1
  12.2 0.0 copy-start.2
  12.2 9.8 %attend.1 = (bf16[128,1024]{1,0:T(8,128)(2,1)S(1)}, bf16[128,1024]{1,0:T(8,128)(2,1)S(1)}, bf16[128,1024]{1,0:T(8,128)(2,1)S(1)}, bf16[128,1024]{1,0:T(8,128)(2,...) custom-call(bf16[128,8192]{1,0:T(8,128)(2,1)} %bitcast.9, ...), custom_call_target="tpu_custom_call" | custom-call | flops 2400000000 | bytes 25165824 | tf_op jit(solution)/shard_map/attend/pallas_call | solution.py:337
  21.9 1.7 %collective-permute-start.1 = (bf16[128,1024]{1,0:T(8,128)(2,1)S(1)}, bf16[128,1024]{1,0:T(8,128)(2,1)S(1)}, u32[]{:S(2)}, u32[]{:S(2)}) collective-permute-start(bf16[128,1024]{1,0:T(8,128)(2,1)S(1)} %get-tuple-element.28), channel_id=1, source_target_pairs={{0,1},{1,2},{2,3},{3,0},{4,5},{5,6},{6,7},{7,4},{8,9},{9,10},{10,1... | collective-permute-start | bytes 786440 | tf_op jit(solution)/shard_map/ppermute | solution.py:385
  23.7 2.2 %collective-permute-start.2 = (bf16[128,1024]{1,0:T(8,128)(2,1)S(1)}, bf16[128,1024]{1,0:T(8,128)(2,1)S(1)}, u32[]{:S(2)}, u32[]{:S(2)}) collective-permute-start(bf16[128,1024]{1,0:T(8,128)(2,1)S(1)} %get-tuple-element.29), channel_id=1, source_target_pairs={{0,3},{1,0},{2,1},{3,2},{4,7},{5,4},{6,5},{7,6},{8,11},{9,8},{10,9... | collective-permute-start | bytes 786440 | tf_op jit(solution)/shard_map/ppermute | solution.py:386
  25.9 2.7 %collective-permute-start.5 = (bf16[128,1024]{1,0:T(8,128)(2,1)S(1)}, bf16[128,1024]{1,0:T(8,128)(2,1)S(1)}, u32[]{:S(2)}, u32[]{:S(2)}) collective-permute-start(bf16[128,1024]{1,0:T(8,128)(2,1)S(1)} %get-tuple-element.32), channel_id=1, source_target_pairs={{0,3},{1,0},{2,1},{3,2},{4,7},{5,4},{6,5},{7,6},{8,11},{9,8},{10,9... | collective-permute-start | bytes 786440 | tf_op jit(solution)/shard_map/ppermute | solution.py:388
  28.5 3.8 %collective-permute-done.1.far1 = bf16[128,1024]{1,0:T(8,128)(2,1)S(1)} collective-permute-done((bf16[128,1024]{1,0:T(8,128)(2,1)S(1)}, bf16[128,1024]{1,0:T(8,128)(2,1)S(1)}, u32[]{:S(2)}, u32[]{:S(2)}) %collective-permute-start.1) | collective-permute-done | bytes 262176 | tf_op jit(solution)/shard_map/ppermute | solution.py:385
  32.3 0.0 collective-permute-done.2.far0
  32.3 0.1 relay.1
  32.5 0.6 collective-permute-start.3
  33.0 2.2 %collective-permute-start.4 = (bf16[128,1024]{1,0:T(8,128)(2,1)S(1)}, bf16[128,1024]{1,0:T(8,128)(2,1)S(1)}, u32[]{:S(2)}, u32[]{:S(2)}) collective-permute-start(bf16[128,1024]{1,0:T(8,128)(2,1)S(1)} %get-tuple-element.31), channel_id=1, source_target_pairs={{0,3},{1,0},{2,1},{3,2},{4,7},{5,4},{6,5},{7,6},{8,11},{9,8},{10,9... | collective-permute-start | bytes 786440 | tf_op jit(solution)/shard_map/ppermute | solution.py:391
  35.2 0.8 %choose.1.pick = bf16[256,128]{1,0:T(8,128)(2,1)S(1)} custom-call(s32[16]{0:T(128)S(1)} %copy-done, s32[16]{0:T(128)S(1)} %bitcast.8, s32[16]{0:T(128)S(1)} %copy-done.2), custom_call_target="tpu_custom_call" | custom-call | bytes 2097152 | tf_op jit(solution)/shard_map/choose/pallas_call | solution.py:392
  36.0 1.9 %collective-permute-done.up0 = bf16[128,1024]{1,0:T(8,128)(2,1)S(1)} collective-permute-done((bf16[128,1024]{1,0:T(8,128)(2,1)S(1)}, bf16[128,1024]{1,0:T(8,128)(2,1)S(1)}, u32[]{:S(2)}, u32[]{:S(2)}) %collective-permute-start) | collective-permute-done | bytes 262176 | tf_op jit(solution)/shard_map/ppermute | solution.py:387
  38.0 5.6 %collective-permute-done.3.up1 = bf16[128,1024]{1,0:T(8,128)(2,1)S(1)} collective-permute-done((bf16[128,1024]{1,0:T(8,128)(2,1)S(1)}, bf16[128,1024]{1,0:T(8,128)(2,1)S(1)}, u32[]{:S(2)}, u32[]{:S(2)}) %collective-permute-start.3) | collective-permute-done | bytes 262176 | tf_op jit(solution)/shard_map/ppermute | solution.py:390
  43.6 0.4 close.1
  44.0 0.5 collective-permute-start.7
  44.5 3.3 %collective-permute-start.8 = (bf16[64,1024]{1,0:T(8,128)(2,1)S(1)}, bf16[64,1024]{1,0:T(8,128)(2,1)S(1)}, u32[]{:S(2)}, u32[]{:S(2)}) collective-permute-start(bf16[64,1024]{1,0:T(8,128)(2,1)S(1)} %get-tuple-element.37), channel_id=1, source_target_pairs={{0,64},{8,72},{16,80},{24,88},{32,96},{40,104},{48,112},{56,120},{... | collective-permute-start | bytes 393224 | tf_op jit(solution)/shard_map/ppermute | solution.py:406
  47.8 0.2 collective-permute-start.9
  47.9 4.8 %collective-permute-done.7.near1 = bf16[64,1024]{1,0:T(8,128)(2,1)S(1)} collective-permute-done((bf16[64,1024]{1,0:T(8,128)(2,1)S(1)}, bf16[64,1024]{1,0:T(8,128)(2,1)S(1)}, u32[]{:S(2)}, u32[]{:S(2)}) %collective-permute-start.7) | collective-permute-done | bytes 131104 | tf_op jit(solution)/shard_map/ppermute | solution.py:407
  52.8 5.1 %collective-permute-done.8.far0 = bf16[64,1024]{1,0:T(8,128)(2,1)S(1)} collective-permute-done((bf16[64,1024]{1,0:T(8,128)(2,1)S(1)}, bf16[64,1024]{1,0:T(8,128)(2,1)S(1)}, u32[]{:S(2)}, u32[]{:S(2)}) %collective-permute-start.8) | collective-permute-done | bytes 131104 | tf_op jit(solution)/shard_map/ppermute | solution.py:406
  57.9 0.2 join.1
  58.1 0.7 %collective-permute-start.10 = (bf16[64,1024]{1,0:T(8,128)(2,1)S(1)}, bf16[64,1024]{1,0:T(8,128)(2,1)S(1)}, u32[]{:S(2)}, u32[]{:S(2)}) collective-permute-start(bf16[64,1024]{1,0:T(8,128)(2,1)S(1)} %get-tuple-element.40), channel_id=1, source_target_pairs={{0,8},{8,0},{16,24},{24,16},{32,40},{40,32},{48,56},{56,48},{64,72... | collective-permute-start | bytes 393224 | tf_op jit(solution)/shard_map/ppermute | solution.py:411
  58.8 1.0 %collective-permute-done.10.crossed = bf16[64,1024]{1,0:T(8,128)(2,1)S(1)} collective-permute-done((bf16[64,1024]{1,0:T(8,128)(2,1)S(1)}, bf16[64,1024]{1,0:T(8,128)(2,1)S(1)}, u32[]{:S(2)}, u32[]{:S(2)}) %collective-permute-start.10) | collective-permute-done | bytes 131104 | tf_op jit(solution)/shard_map/ppermute | solution.py:411
  59.8 0.6 split.1
  60.5 0.5 collective-permute-start.11
  61.0 2.2 %collective-permute-start.12 = (bf16[32,1024]{1,0:T(8,128)(2,1)S(1)}, bf16[32,1024]{1,0:T(8,128)(2,1)S(1)}, u32[]{:S(2)}, u32[]{:S(2)}) collective-permute-start(bf16[32,1024]{1,0:T(8,128)(2,1)S(1)} %get-tuple-element.43), channel_id=1, source_target_pairs={{0,48},{8,56},{16,0},{24,8},{32,16},{40,24},{48,32},{56,40},{64,11... | collective-permute-start | bytes 196616 | tf_op jit(solution)/shard_map/ppermute | solution.py:419
  63.1 2.1 %collective-permute-start.13 = (bf16[32,1024]{1,0:T(8,128)(2,1)S(1)}, bf16[32,1024]{1,0:T(8,128)(2,1)S(1)}, u32[]{:S(2)}, u32[]{:S(2)}) collective-permute-start(bf16[32,1024]{1,0:T(8,128)(2,1)S(1)} %get-tuple-element.44), channel_id=1, source_target_pairs={{0,32},{8,40},{16,48},{24,56},{32,0},{40,8},{48,16},{56,24},{64,96... | collective-permute-start | bytes 196616 | tf_op jit(solution)/shard_map/ppermute | solution.py:419
  65.3 0.9 %home.1.after = bf16[128,1024]{1,0:T(8,128)(2,1)} custom-call(bf16[128,1024]{1,0:T(8,128)(2,1)S(1)} %get-tuple-element.33.keep, bf16[128,1024]{1,0:T(8,128)(2,1)S(1)} %collective-permute-done.6.other, bf16[256,128]{1,0:T(8,128)(2,1)S(1)} %choose.1.pick), custom_call_target="tpu_custom_call" | custom-call | bytes 2097152 | tf_op jit(solution)/shard_map/home/pallas_call | solution.py:420
  66.2 1.7 %keep_pages.1.kept = bf16[32,3,2,64,128]{4,3,2,1,0:T(8,128)(2,1)} custom-call(bf16[32,3,2,64,128]{4,3,2,1,0:T(8,128)(2,1)S(1)} %all-to-all-done.got, bf16[128,1024]{1,0:T(8,128)(2,1)} %home.1.after), custom_call_target="tpu_custom_call" | custom-call | bytes 2097152 | tf_op jit(solution)/shard_map/keep_pages/pallas_call | solution.py:421
  68.0 0.9 %arrive.1 = bf16[128,1024]{1,0:T(8,128)(2,1)} custom-call(bf16[32,1024]{1,0:T(8,128)(2,1)S(1)} %get-tuple-element.41.k0, bf16[32,1024]{1,0:T(8,128)(2,1)S(1)} %collective-permute-done.11.k1, bf16[32,1024]{1,0:T(8,128)(2,1)S(1)} %collective-permute-done.12.k3, bf16[32,1024]{1,0:T(8,128)(2,1)S(1)} %collective-permute-done.13.k2, ...), custom_call_target="tpu_custom_call" | custom-call | bytes 2097152 | tf_op jit(solution)/shard_map/arrive/pallas_call | solution.py:425
  (14 shorter events, 0.0 us)
Async XLA Ops:
  3.7 62.5 %all-to-all-start = ((bf16[32,3,2,64,128]{4,3,2,1,0:T(8,128)(2,1)}), bf16[32,3,2,64,128]{4,3,2,1,0:T(8,128)(2,1)S(1)}, u32[]{:S(2)}, u32[]{:S(2)}) async-start(bf16[32,3,2,64,128]{4,3,2,1,0:T(8,128)(2,1)} %pack_pages.1), calls=%async_computation | async-start | bytes 6291456 | tf_op jit(solution)/shard_map/all_to_all | solution.py:330
  12.1 23.1 %copy-start = (s32[16]{0:T(128)S(1)}, s32[16]{0:T(128)}, u32[]{:S(2)}) copy-start(s32[16]{0:T(128)} %req_list.1) | copy-start | bytes 196
  12.1 23.1 %copy-start.1 = (s32[16,1]{0,1:T(1,128)S(1)}, s32[16,1]{0,1:T(1,128)}, u32[]{:S(2)}) copy-start(s32[16,1]{0,1:T(1,128)} %param.19) | copy-start | bytes 196
  12.2 23.1 %copy-start.2 = (s32[16]{0:T(128)S(1)}, s32[16]{0:T(128)}, u32[]{:S(2)}) copy-start(s32[16]{0:T(128)} %resume.1) | copy-start | bytes 196
  21.9 10.4 %collective-permute-start.1 = (bf16[128,1024]{1,0:T(8,128)(2,1)S(1)}, bf16[128,1024]{1,0:T(8,128)(2,1)S(1)}, u32[]{:S(2)}, u32[]{:S(2)}) collective-permute-start(bf16[128,1024]{1,0:T(8,128)(2,1)S(1)} %get-tuple-element.28), channel_id=1, source_target_pairs={{0,1},{1,2},{2,3},{3,0},{4,5},{5,6},{6,7},{7,4},{8,9},{9,10},{10,1... | collective-permute-start | bytes 786440 | tf_op jit(solution)/shard_map/ppermute | solution.py:385
  23.7 8.7 %collective-permute-start.2 = (bf16[128,1024]{1,0:T(8,128)(2,1)S(1)}, bf16[128,1024]{1,0:T(8,128)(2,1)S(1)}, u32[]{:S(2)}, u32[]{:S(2)}) collective-permute-start(bf16[128,1024]{1,0:T(8,128)(2,1)S(1)} %get-tuple-element.29), channel_id=1, source_target_pairs={{0,3},{1,0},{2,1},{3,2},{4,7},{5,4},{6,5},{7,6},{8,11},{9,8},{10,9... | collective-permute-start | bytes 786440 | tf_op jit(solution)/shard_map/ppermute | solution.py:386
  25.9 12.1 %collective-permute-start = (bf16[128,1024]{1,0:T(8,128)(2,1)S(1)}, bf16[128,1024]{1,0:T(8,128)(2,1)S(1)}, u32[]{:S(2)}, u32[]{:S(2)}) collective-permute-start(bf16[128,1024]{1,0:T(8,128)(2,1)S(1)} %get-tuple-element.25), channel_id=1, source_target_pairs={{0,1},{1,2},{2,3},{3,0},{4,5},{5,6},{6,7},{7,4},{8,9},{9,10},{10,1... | collective-permute-start | bytes 786440 | tf_op jit(solution)/shard_map/ppermute | solution.py:387
  25.9 12.1 %collective-permute-start.5 = (bf16[128,1024]{1,0:T(8,128)(2,1)S(1)}, bf16[128,1024]{1,0:T(8,128)(2,1)S(1)}, u32[]{:S(2)}, u32[]{:S(2)}) collective-permute-start(bf16[128,1024]{1,0:T(8,128)(2,1)S(1)} %get-tuple-element.32), channel_id=1, source_target_pairs={{0,3},{1,0},{2,1},{3,2},{4,7},{5,4},{6,5},{7,6},{8,11},{9,8},{10,9... | collective-permute-start | bytes 786440 | tf_op jit(solution)/shard_map/ppermute | solution.py:388
  32.5 11.1 %collective-permute-start.3 = (bf16[128,1024]{1,0:T(8,128)(2,1)S(1)}, bf16[128,1024]{1,0:T(8,128)(2,1)S(1)}, u32[]{:S(2)}, u32[]{:S(2)}) collective-permute-start(bf16[128,1024]{1,0:T(8,128)(2,1)S(1)} %get-tuple-element.30), channel_id=1, source_target_pairs={{0,1},{1,2},{2,3},{3,0},{4,5},{5,6},{6,7},{7,4},{8,9},{9,10},{10,1... | collective-permute-start | bytes 786440 | tf_op jit(solution)/shard_map/ppermute | solution.py:390
  33.0 10.5 %collective-permute-start.4 = (bf16[128,1024]{1,0:T(8,128)(2,1)S(1)}, bf16[128,1024]{1,0:T(8,128)(2,1)S(1)}, u32[]{:S(2)}, u32[]{:S(2)}) collective-permute-start(bf16[128,1024]{1,0:T(8,128)(2,1)S(1)} %get-tuple-element.31), channel_id=1, source_target_pairs={{0,3},{1,0},{2,1},{3,2},{4,7},{5,4},{6,5},{7,6},{8,11},{9,8},{10,9... | collective-permute-start | bytes 786440 | tf_op jit(solution)/shard_map/ppermute | solution.py:391
  44.0 8.8 %collective-permute-start.7 = (bf16[64,1024]{1,0:T(8,128)(2,1)S(1)}, bf16[64,1024]{1,0:T(8,128)(2,1)S(1)}, u32[]{:S(2)}, u32[]{:S(2)}) collective-permute-start(bf16[64,1024]{1,0:T(8,128)(2,1)S(1)} %get-tuple-element.36), channel_id=1, source_target_pairs={{0,4},{1,5},{2,6},{3,7},{4,0},{5,1},{6,2},{7,3},{8,12},{9,13},{10,... | collective-permute-start | bytes 393224 | tf_op jit(solution)/shard_map/ppermute | solution.py:407
  44.5 13.4 %collective-permute-start.8 = (bf16[64,1024]{1,0:T(8,128)(2,1)S(1)}, bf16[64,1024]{1,0:T(8,128)(2,1)S(1)}, u32[]{:S(2)}, u32[]{:S(2)}) collective-permute-start(bf16[64,1024]{1,0:T(8,128)(2,1)S(1)} %get-tuple-element.37), channel_id=1, source_target_pairs={{0,64},{8,72},{16,80},{24,88},{32,96},{40,104},{48,112},{56,120},{... | collective-permute-start | bytes 393224 | tf_op jit(solution)/shard_map/ppermute | solution.py:406
  47.8 10.1 %collective-permute-start.9 = (bf16[64,1024]{1,0:T(8,128)(2,1)S(1)}, bf16[64,1024]{1,0:T(8,128)(2,1)S(1)}, u32[]{:S(2)}, u32[]{:S(2)}) collective-permute-start(bf16[64,1024]{1,0:T(8,128)(2,1)S(1)} %get-tuple-element.38), channel_id=1, source_target_pairs={{0,68},{1,69},{2,70},{3,71},{4,64},{5,65},{6,66},{7,67},{8,76},{9,... | collective-permute-start | bytes 393224 | tf_op jit(solution)/shard_map/ppermute | solution.py:408
  47.9 17.3 %collective-permute-start.6 = (bf16[128,1024]{1,0:T(8,128)(2,1)S(1)}, bf16[128,1024]{1,0:T(8,128)(2,1)S(1)}, u32[]{:S(2)}, u32[]{:S(2)}) collective-permute-start(bf16[128,1024]{1,0:T(8,128)(2,1)S(1)} %get-tuple-element.34), channel_id=1, source_target_pairs={{0,4},{1,5},{2,6},{3,7},{4,0},{5,1},{6,2},{7,3},{8,12},{9,13},{10,... | collective-permute-start | bytes 786440 | tf_op jit(solution)/shard_map/ppermute | solution.py:410
  58.1 1.7 %collective-permute-start.10 = (bf16[64,1024]{1,0:T(8,128)(2,1)S(1)}, bf16[64,1024]{1,0:T(8,128)(2,1)S(1)}, u32[]{:S(2)}, u32[]{:S(2)}) collective-permute-start(bf16[64,1024]{1,0:T(8,128)(2,1)S(1)} %get-tuple-element.40), channel_id=1, source_target_pairs={{0,8},{8,0},{16,24},{24,16},{32,40},{40,32},{48,56},{56,48},{64,72... | collective-permute-start | bytes 393224 | tf_op jit(solution)/shard_map/ppermute | solution.py:411
  60.5 7.5 %collective-permute-start.11 = (bf16[32,1024]{1,0:T(8,128)(2,1)}, bf16[32,1024]{1,0:T(8,128)(2,1)S(1)}, u32[]{:S(2)}, u32[]{:S(2)}) collective-permute-start(bf16[32,1024]{1,0:T(8,128)(2,1)} %get-tuple-element.42), channel_id=1, source_target_pairs={{0,16},{8,24},{16,32},{24,40},{32,48},{40,56},{48,0},{56,8},{64,80... | collective-permute-start | bytes 196616 | tf_op jit(solution)/shard_map/ppermute | solution.py:419
  61.0 7.0 %collective-permute-start.12 = (bf16[32,1024]{1,0:T(8,128)(2,1)S(1)}, bf16[32,1024]{1,0:T(8,128)(2,1)S(1)}, u32[]{:S(2)}, u32[]{:S(2)}) collective-permute-start(bf16[32,1024]{1,0:T(8,128)(2,1)S(1)} %get-tuple-element.43), channel_id=1, source_target_pairs={{0,48},{8,56},{16,0},{24,8},{32,16},{40,24},{48,32},{56,40},{64,11... | collective-permute-start | bytes 196616 | tf_op jit(solution)/shard_map/ppermute | solution.py:419
  63.1 4.8 %collective-permute-start.13 = (bf16[32,1024]{1,0:T(8,128)(2,1)S(1)}, bf16[32,1024]{1,0:T(8,128)(2,1)S(1)}, u32[]{:S(2)}, u32[]{:S(2)}) collective-permute-start(bf16[32,1024]{1,0:T(8,128)(2,1)S(1)} %get-tuple-element.44), channel_id=1, source_target_pairs={{0,32},{8,40},{16,48},{24,56},{32,0},{40,8},{48,16},{56,24},{64,96... | collective-permute-start | bytes 196616 | tf_op jit(solution)/shard_map/ppermute | solution.py:419
